TPU v7x, 32 devices: a whole 2x2x4 slice. The times are simulated.
32 devices in a mesh: node: 4 (over y, x), table: 8 (over z, core).
Axes of the slice: x: 2, y: 2, z: 4, core: 2. Of those that a mesh axis runs over, the one named last changes fastest.
Arguments:
- emb_rows: bfloat16 [16384, 128], P(('node', 'table')), may hold values from -0.23925781 to 0.23925781
- tile_mult: int32 [256, 128, 128], P(('node', 'table')), may hold values from 0 to 3
- tile_rows: int32 [256], P(('node', 'table')), may hold values from 0 to 3
- tile_table: int32 [256], P(('node', 'table')), may hold values from 0 to 7, as said below
- tile_slot: int32 [256], P(('node', 'table')), may hold values from 0 to 51
- dense: bfloat16 [8192, 128], P(('node', 'table')), may hold values from -6 to 6
- cross_v: bfloat16 [3456, 512], P('node'), may hold values from -0.109375 to 0.109375
- cross_u: bfloat16 [512, 3456], P('node'), may hold values from -0.25 to 0.25
- cross_bias: float32 [3456], replicated, may hold values from -3 to 3
- cotangent: bfloat16 [8192, 3456], P(('node', 'table')), may hold values from -0.1796875 to 0.1796875
Outputs:
- cross_out: bfloat16 [8192, 3456], P(('node', 'table'))
- emb_grad: float32 [16384, 128], P(('node', 'table'))
Inputs may be any that keep to these rules, and one draw needn't show every extreme that they name: For each node index n and table index t, take the tiles j with j // 2 == n on the 4 devices of table index t: no tile_table value occurs more than 3 times among them, and the tiles with one value carry at most 2 distinct tile_slot values. Both bounds are reached in every such set.
All inputs are finite; a program needn't handle non-finite values.
Results may differ from a plain program's by a relative error of at most 0.0057.
Values may be sent and summed in bfloat16 or wider, within the bound.
No kernel may reach another device: no remote copies, remote signals or barrier semaphores. Data moves between devices by JAX's collectives and lax.ppermute only.
A program may use at most 128 MiB of HBM per device.

v0:
```python
import jax
import jax.numpy as jnp
from jax import lax
from jax.sharding import PartitionSpec as P

FEATURES = 26
CAP = 3
SAMPLE_BLOCKS = 2
BAG_BLOCKS = 52


def place(flat_values, slot_ids, list_entry, member_rank, entries):
    sequence = jnp.arange(slot_ids.shape[0], dtype=jnp.int32)
    targets = jnp.arange(entries, dtype=jnp.int32)[:, None]
    chosen = (list_entry[None, :] == targets) & (member_rank[None, :] == 0)
    present = jnp.any(chosen, axis=1)
    source = jnp.sum(jnp.where(chosen, sequence[None, :], 0), axis=1)
    filled = jnp.where(present[:, None], jnp.take(flat_values, source, axis=0), 0.0)
    first_slot = jnp.where(present, jnp.take(slot_ids, source), -1).astype(jnp.int32)
    return (filled, first_slot)


def owner_work(arrived, arrived_slot, dense, cross_v, cross_u, cross_bias, cotangent):
    block_size = arrived.shape[2]
    emb_width = arrived.shape[3]
    flat_arrived = arrived.reshape(-1, block_size * emb_width)
    flat_slot = arrived_slot.reshape(-1)
    selector = (flat_slot[None, :] == jnp.arange(BAG_BLOCKS, dtype=jnp.int32)[:, None]).astype(
        jnp.float32
    )
    pooled = jnp.dot(
        selector, flat_arrived, precision=lax.Precision.HIGHEST, preferred_element_type=jnp.float32
    )
    embedded = pooled.reshape(FEATURES, SAMPLE_BLOCKS, block_size, emb_width).transpose(1, 2, 0, 3)
    embedded = embedded.reshape(-1, FEATURES * emb_width).astype(jnp.bfloat16)
    first_layer = jnp.concatenate([dense, embedded], axis=1)
    hidden = jnp.dot(first_layer, cross_v, preferred_element_type=jnp.float32).astype(jnp.bfloat16)
    cross_scale = jnp.dot(hidden, cross_u, preferred_element_type=jnp.float32) + cross_bias
    layer_input = first_layer.astype(jnp.float32)
    cross_out = (layer_input * (cross_scale + 1.0)).astype(jnp.bfloat16)
    upstream = cotangent.astype(jnp.float32)
    dscale = (upstream * layer_input).astype(jnp.bfloat16)
    dhidden = lax.dot_general(
        dscale, cross_u, (((1,), (1,)), ((), ())), preferred_element_type=jnp.float32
    ).astype(jnp.bfloat16)
    dlayer = upstream * (cross_scale + 1.0) + lax.dot_general(
        dhidden, cross_v, (((1,), (1,)), ((), ())), preferred_element_type=jnp.float32
    )
    bag_grad = (
        dlayer[:, emb_width:]
        .astype(jnp.bfloat16)
        .reshape(SAMPLE_BLOCKS, block_size, FEATURES, emb_width)
    )
    bag_grad = bag_grad.transpose(2, 0, 1, 3).reshape(BAG_BLOCKS, block_size, emb_width)
    occupied = arrived_slot >= 0
    safe_slot = jnp.where(occupied, arrived_slot, 0)
    returning = jnp.where(
        occupied[..., None, None],
        jnp.take(bag_grad, safe_slot, axis=0),
        jnp.zeros((), jnp.bfloat16),
    )
    return (cross_out, returning)


def body(
    emb_rows,
    tile_mult,
    tile_rows,
    tile_table,
    tile_slot,
    dense,
    cross_v,
    cross_u,
    cross_bias,
    cotangent,
):
    tables = lax.axis_size("table")
    tile_count = tile_mult.shape[0]
    block_size = tile_mult.shape[1]
    emb_width = emb_rows.shape[1]
    row_blocks = emb_rows.reshape(-1, block_size, emb_width)
    tile_weights = tile_mult.astype(jnp.bfloat16)
    picked = jnp.take(row_blocks, tile_rows, axis=0)
    partial_rows = jnp.einsum(
        "kbr,kre->kbe", tile_weights, picked, preferred_element_type=jnp.float32
    )
    forwarded, moved_table, moved_slot = (
        lax.all_to_all(partial_rows, "node", split_axis=0, concat_axis=0, tiled=True),
        lax.all_to_all(tile_table, "node", split_axis=0, concat_axis=0, tiled=True),
        lax.all_to_all(tile_slot, "node", split_axis=0, concat_axis=0, tiled=True),
    )
    full_v, full_u = (
        lax.all_gather(cross_v, "node", axis=0, tiled=True),
        lax.all_gather(cross_u, "node", axis=0, tiled=True),
    )
    sequence = jnp.arange(tile_count, dtype=jnp.int32)
    earlier = sequence[None, :] < sequence[:, None]
    same_table = moved_table[:, None] == moved_table[None, :]
    flat_moved = forwarded.reshape(tile_count, -1)
    list_depth = CAP
    list_rank = jnp.sum(same_table & earlier, axis=1)
    list_entry = moved_table * list_depth + list_rank
    send_rows, send_slot = place(
        flat_moved, moved_slot, list_entry, jnp.zeros_like(list_entry), tables * list_depth
    )
    arrived, arrived_slot = (
        lax.all_to_all(
            send_rows.reshape(tables, list_depth, block_size, emb_width),
            "table",
            split_axis=0,
            concat_axis=0,
            tiled=True,
        ),
        lax.all_to_all(
            send_slot.reshape(tables, list_depth), "table", split_axis=0, concat_axis=0, tiled=True
        ),
    )
    cross_out, returning = owner_work(
        arrived, arrived_slot, dense, full_v, full_u, cross_bias, cotangent
    )
    came_back = lax.all_to_all(returning, "table", split_axis=0, concat_axis=0, tiled=True)
    tile_grad = jnp.take(
        came_back.reshape(tables * list_depth, block_size, emb_width), list_entry, axis=0
    )
    tile_grad = lax.all_to_all(tile_grad, "node", split_axis=0, concat_axis=0, tiled=True)
    tile_grads = jnp.einsum(
        "kbr,kbe->kre", tile_weights, tile_grad, preferred_element_type=jnp.float32
    )
    owner_rows = (
        tile_rows[None, :] == jnp.arange(row_blocks.shape[0], dtype=jnp.int32)[:, None]
    ).astype(jnp.float32)
    emb_grad = jnp.dot(
        owner_rows,
        tile_grads.reshape(tile_count, -1),
        precision=lax.Precision.HIGHEST,
        preferred_element_type=jnp.float32,
    )
    return (cross_out, emb_grad.reshape(-1, emb_width))


def solution(mesh):
    in_specs = (
        P(("node", "table"), None),
        P(("node", "table"), None, None),
        P(("node", "table")),
        P(("node", "table")),
        P(("node", "table")),
        P(("node", "table"), None),
        P("node", None),
        P("node", None),
        P(),
        P(("node", "table"), None),
    )
    out_specs = (P(("node", "table"), None), P(("node", "table"), None))
    return jax.shard_map(body, mesh=mesh, in_specs=in_specs, out_specs=out_specs, check_vma=False)
```

profile of v0, /device:TPU:0, one launch (start us, length us, event | category | flops | bytes accessed | tf_op | source)
XLA Modules:
  0.0 184.5 jit_solution(5508650706934687587)
XLA Ops:
  7.3 0.7 all-gather.3.cloned.1.call-update
  7.9 1.3 all_to_all.36
  9.3 5.2 %all-to-all-start = ((s32[4,2,1]{1,2,0:T(1,128)}), s32[4,2,1]{1,2,0:T(1,128)S(1)}, u32[]{:S(2)}, u32[]{:S(2)}) async-start(s32[4,2,1]{1,2,0:T(1,128)} %bitcast), calls=%async_computation | async-start | bytes 4096 | tf_op jit(solution)/shard_map/all_to_all | solution.py:89
  14.4 0.7 all-gather.5.cloned.1.call-update
  15.9 3.1 %all-to-all-done = s32[4,2,1]{1,2,0:T(1,128)S(1)} async-done(((s32[4,2,1]{1,2,0:T(1,128)}), s32[4,2,1]{1,2,0:T(1,128)S(1)}, u32[]{:S(2)}, u32[]{:S(2)}) %all-to-all-start) | async-done | bytes 64 | tf_op jit(solution)/shard_map/all_to_all | solution.py:89
  19.0 3.2 %all-to-all-start.1 = ((s32[4,2,1]{1,2,0:T(1,128)}), s32[4,2,1]{1,2,0:T(1,128)S(1)}, u32[]{:S(2)}, u32[]{:S(2)}) async-start(s32[4,2,1]{1,2,0:T(1,128)} %bitcast.1), calls=%async_computation.1 | async-start | bytes 4096 | tf_op jit(solution)/shard_map/all_to_all | solution.py:90
  24.5 2.2 %all-to-all-done.1 = s32[4,2,1]{1,2,0:T(1,128)S(1)} async-done(((s32[4,2,1]{1,2,0:T(1,128)}), s32[4,2,1]{1,2,0:T(1,128)S(1)}, u32[]{:S(2)}, u32[]{:S(2)}) %all-to-all-start.1) | async-done | bytes 64 | tf_op jit(solution)/shard_map/all_to_all | solution.py:90
  27.6 0.7 gather_fusion
  29.0 4.9 %all-to-all-start.2 = ((s32[8,1,3]{2,1,0:T(1,128)}), s32[8,1,3]{2,1,0:T(1,128)S(1)}, u32[]{:S(2)}, u32[]{:S(2)}) async-start(s32[8,1,3]{2,1,0:T(1,128)} %bitcast.4), calls=%async_computation.2 | async-start | bytes 8192 | tf_op jit(solution)/shard_map/all_to_all | solution.py:114
  33.9 5.5 %all-to-all-done.2 = s32[8,1,3]{2,1,0:T(1,128)S(1)} async-done(((s32[8,1,3]{2,1,0:T(1,128)}), s32[8,1,3]{2,1,0:T(1,128)S(1)}, u32[]{:S(2)}, u32[]{:S(2)}) %all-to-all-start.2) | async-done | bytes 128 | tf_op jit(solution)/shard_map/all_to_all | solution.py:114
  40.4 1.1 convolution_bitcast_fusion.1
  41.6 3.5 %all-to-all-start.3 = ((f32[8,128,128]{1,2,0:T(8,128)}), f32[8,128,128]{1,2,0:T(8,128)S(1)}, u32[]{:S(2)}, u32[]{:S(2)}) async-start(f32[8,128,128]{1,2,0:T(8,128)} %convolution_bitcast_fusion.1), calls=%async_computation.3 | async-start | bytes 1048576 | tf_op jit(solution)/shard_map/all_to_all | solution.py:88
  45.2 14.4 %all-to-all-done.3 = f32[8,128,128]{1,2,0:T(8,128)S(1)} async-done(((f32[8,128,128]{1,2,0:T(8,128)}), f32[8,128,128]{1,2,0:T(8,128)S(1)}, u32[]{:S(2)}, u32[]{:S(2)}) %all-to-all-start.3) | async-done | bytes 524320 | tf_op jit(solution)/shard_map/all_to_all | solution.py:88
  60.1 1.1 gather_fusion.2
  61.5 1.4 select_select_fusion
  62.9 3.7 %all-to-all-start.4 = ((f32[8,3,128,128]{3,2,1,0:T(8,128)}), f32[8,3,128,128]{3,2,1,0:T(8,128)S(1)}, u32[]{:S(2)}, u32[]{:S(2)}) async-start(f32[8,3,128,128]{3,2,1,0:T(8,128)} %select_select_fusion), calls=%async_computation.4 | async-start | bytes 3145728 | tf_op jit(solution)/shard_map/all_to_all | solution.py:107
  66.6 2.1 %convert_element_type.44 = f32[256,3456]{1,0:T(8,128)} convert(bf16[256,3456]{1,0:T(8,128)(2,1)S(1)} %copy-done.1) | non-fusion elementwise | flops 884736 | bytes 5308416 | tf_op jit(solution)/shard_map/convert_element_type | solution.py:41
  70.3 34.1 %all-to-all-done.4 = f32[8,3,128,128]{3,2,1,0:T(8,128)S(1)} async-done(((f32[8,3,128,128]{3,2,1,0:T(8,128)}), f32[8,3,128,128]{3,2,1,0:T(8,128)S(1)}, u32[]{:S(2)}, u32[]{:S(2)}) %all-to-all-start.4) | async-done | bytes 1572896 | tf_op jit(solution)/shard_map/all_to_all | solution.py:107
  104.3 3.4 %convolution_convert_fusion = bf16[26,2,128,128]{3,0,2,1:T(8,128)(2,1)S(1)} fusion(s32[26,2]{0,1:T(2,128)S(1)} %multiply_add_fusion, s32[24]{0:T(128)S(1)} %eq.71, f32[3,8,128,128]{3,2,1,0:T(8,128)S(1)} %bitcast.79), kind=kOutput, calls=%fused_computation.14 | convolution fusion | flops 246220000 | bytes 3277104 | tf_op jit(solution)/shard_map/dot_general | solution.py:31
  107.7 2.0 %bitcast_dynamic-update-slice_fusion = bf16[256,3456]{1,0:T(8,128)(2,1)} fusion(bf16[256,3456]{1,0:T(8,128)(2,1)} %constant_dynamic-update-slice_fusion, bf16[32,8,26,128]{3,2,1,0:T(8,128)(2,1)S(1)} %bitcast.77), kind=kLoop, calls=%fused_computation.16 | loop fusion | bytes 3407872 | tf_op jit(solution)/shard_map/concatenate | solution.py:36
  109.7 4.9 %all-gather.5.cloned.1.call-done = bf16[512,3456]{1,0:T(8,128)(2,1)} async-done(((bf16[128,3456]{1,0:T(8,128)(2,1)}), bf16[512,3456]{1,0:T(8,128)(2,1)}) %all-gather.5.cloned.1.call-update) | async-done | bytes 3538960 | tf_op jit(solution)/shard_map/all_gather | solution.py:94
  114.6 7.5 %fusion.11 = f32[256,3456]{1,0:T(8,128)} fusion(bf16[3456,512]{1,0:T(8,128)(2,1)} %all-gather.3.cloned.1.call-done, bf16[512,3456]{1,0:T(8,128)(2,1)} %all-gather.5.cloned.1.call-done, bf16[256,3456]{1,0:T(8,128)(2,1)} %bitcast_dynamic-update-slice_fusion, bf16[256,3456]{1,0:T(8,128)(2,1)S(1)} %copy-done.1), kind=kOutput, calls=%fused_computation.25 | convolution fusion | flops 1815609344 | bytes 14155776 | tf_op jit(solution)/shard_map/dot_general | solution.py:46
  122.2 8.7 %fusion.1 = (bf16[256,3456]{1,0:T(8,128)(2,1)}, f32[256,3456]{1,0:T(8,128)}) fusion(bf16[256,3456]{1,0:T(8,128)(2,1)} %bitcast_dynamic-update-slice_fusion, f32[3456]{0:T(1024)S(1)} %copy-done.11, bf16[512,3456]{1,0:T(8,128)(2,1)} %all-gather.5.cloned.1.call-done, bf16[3456,512]{1,0:T(8,128)(2,1)} %all-gather.3.cloned.1.call-done), kind=kOutput, calls=%fused_computation.9 | convolution fusion | flops 1816494080 | bytes 14169600 | tf_op jit(solution)/shard_map/dot_general | solution.py:38
  130.9 4.4 %fusion.3 = bf16[256,3328]{1,0:T(8,128)(2,1)S(1)} fusion(f32[256,3456]{1,0:T(8,128)} %fusion.11, f32[256,3456]{1,0:T(8,128)} %get-tuple-element.9, f32[256,3456]{1,0:T(8,128)} %convert_element_type.44), kind=kLoop, calls=%fused_computation.12 | loop fusion | flops 2555904 | bytes 11927552 | tf_op jit(solution)/shard_map/convert
  135.3 1.3 copy.59
  137.0 1.9 %copy.60 = bf16[26,2,128,128]{3,2,1,0:T(8,128)(2,1)S(1)} copy(bf16[26,2,128,128]{2,1,3,0:T(2,128)(2,1)S(1)} %bitcast.78) | data formatting | bytes 3407872 | tf_op jit(solution)/shard_map/transpose | solution.py:54
  139.0 0.7 gather_fusion.3
  139.7 1.1 select_select_fusion.1
  140.8 4.7 %all-to-all-start.5 = ((bf16[8,3,128,128]{3,2,1,0:T(8,128)(2,1)}), bf16[8,3,128,128]{3,2,1,0:T(8,128)(2,1)S(1)}, u32[]{:S(2)}, u32[]{:S(2)}) async-start(bf16[8,3,128,128]{3,2,1,0:T(8,128)(2,1)} %select_select_fusion.1), calls=%async_computation.5 | async-start | bytes 1572864 | tf_op jit(solution)/shard_map/all_to_all | solution.py:121
  145.6 20.9 %all-to-all-done.5 = bf16[8,3,128,128]{3,2,1,0:T(8,128)(2,1)S(1)} async-done(((bf16[8,3,128,128]{3,2,1,0:T(8,128)(2,1)}), bf16[8,3,128,128]{3,2,1,0:T(8,128)(2,1)S(1)}, u32[]{:S(2)}, u32[]{:S(2)}) %all-to-all-start.5) | async-done | bytes 786464 | tf_op jit(solution)/shard_map/all_to_all | solution.py:121
  167.4 8.3 %all_to_all.56 = bf16[8,128,128]{1,2,0:T(8,128)(2,1)S(1)} all-to-all(bf16[8,128,128]{1,2,0:T(8,128)(2,1)S(1)} %broadcast_select_fusion), channel_id=1, replica_groups=mesh['node'=4,'table'=8] {'node'}, dimensions={0} | all-to-all | bytes 524288 | tf_op jit(solution)/shard_map/all_to_all | solution.py:125
  176.8 0.9 reshape.250
  (75 shorter events, 10.6 us)
Async XLA Ops:
  7.2 32.5 %copy-start = (bf16[512,128]{1,0:T(8,128)(2,1)S(1)}, bf16[512,128]{1,0:T(8,128)(2,1)}, u32[]{:S(2)}) copy-start(bf16[512,128]{1,0:T(8,128)(2,1)} %param.10) | copy-start | bytes 393220
  7.2 8.0 %copy-start.9 = (s32[8]{0:T(128)S(1)}, s32[8]{0:T(128)}, u32[]{:S(2)}) copy-start(s32[8]{0:T(128)} %param.12) | copy-start | bytes 100
  7.2 8.0 %copy-start.6 = (s32[8]{0:T(128)S(1)}, s32[8]{0:T(128)}, u32[]{:S(2)}) copy-start(s32[8]{0:T(128)} %param.14) | copy-start | bytes 100
  7.2 33.2 %copy-start.2 = (s32[8,128,128]{2,1,0:T(8,128)S(1)}, s32[8,128,128]{2,1,0:T(8,128)}, u32[]{:S(2)}) copy-start(s32[8,128,128]{2,1,0:T(8,128)} %param.11) | copy-start | bytes 1572868
  7.2 102.5 %all-gather.3.cloned.1.call-start = ((), (), s32[]{:S(2)}) async-start(), calls=%async_computation.7 | async-start | bytes 4423680 | tf_op jit(solution)/shard_map/all_gather | solution.py:93
  9.3 9.7 %all-to-all-start = ((s32[4,2,1]{1,2,0:T(1,128)}), s32[4,2,1]{1,2,0:T(1,128)S(1)}, u32[]{:S(2)}, u32[]{:S(2)}) async-start(s32[4,2,1]{1,2,0:T(1,128)} %bitcast), calls=%async_computation | async-start | bytes 4096 | tf_op jit(solution)/shard_map/all_to_all | solution.py:89
  14.4 100.2 %all-gather.5.cloned.1.call-start = ((), (), s32[]{:S(2)}) async-start(), calls=%async_computation.8 | async-start | bytes 4423680 | tf_op jit(solution)/shard_map/all_gather | solution.py:94
  19.0 7.8 %all-to-all-start.1 = ((s32[4,2,1]{1,2,0:T(1,128)}), s32[4,2,1]{1,2,0:T(1,128)S(1)}, u32[]{:S(2)}, u32[]{:S(2)}) async-start(s32[4,2,1]{1,2,0:T(1,128)} %bitcast.1), calls=%async_computation.1 | async-start | bytes 4096 | tf_op jit(solution)/shard_map/all_to_all | solution.py:90
  23.7 0.8 copy-start.7
  29.0 10.4 %all-to-all-start.2 = ((s32[8,1,3]{2,1,0:T(1,128)}), s32[8,1,3]{2,1,0:T(1,128)S(1)}, u32[]{:S(2)}, u32[]{:S(2)}) async-start(s32[8,1,3]{2,1,0:T(1,128)} %bitcast.4), calls=%async_computation.2 | async-start | bytes 8192 | tf_op jit(solution)/shard_map/all_to_all | solution.py:114
  41.6 18.0 %all-to-all-start.3 = ((f32[8,128,128]{1,2,0:T(8,128)}), f32[8,128,128]{1,2,0:T(8,128)S(1)}, u32[]{:S(2)}, u32[]{:S(2)}) async-start(f32[8,128,128]{1,2,0:T(8,128)} %convolution_bitcast_fusion.1), calls=%async_computation.3 | async-start | bytes 1048576 | tf_op jit(solution)/shard_map/all_to_all | solution.py:88
  62.9 3.7 %copy-start.1 = (bf16[256,3456]{1,0:T(8,128)(2,1)S(1)}, bf16[256,3456]{1,0:T(8,128)(2,1)}, u32[]{:S(2)}) copy-start(bf16[256,3456]{1,0:T(8,128)(2,1)} %param.19) | copy-start | bytes 5308420
  62.9 41.5 %all-to-all-start.4 = ((f32[8,3,128,128]{3,2,1,0:T(8,128)}), f32[8,3,128,128]{3,2,1,0:T(8,128)S(1)}, u32[]{:S(2)}, u32[]{:S(2)}) async-start(f32[8,3,128,128]{3,2,1,0:T(8,128)} %select_select_fusion), calls=%async_computation.4 | async-start | bytes 3145728 | tf_op jit(solution)/shard_map/all_to_all | solution.py:107
  66.6 2.1 %copy-start.4 = (bf16[256,128]{1,0:T(8,128)(2,1)S(1)}, bf16[256,128]{1,0:T(8,128)(2,1)}, u32[]{:S(2)}) copy-start(bf16[256,128]{1,0:T(8,128)(2,1)} %param.15) | copy-start | bytes 196612
  109.7 12.5 %copy-start.11 = (f32[3456]{0:T(1024)S(1)}, f32[3456]{0:T(1024)}, u32[]{:S(2)}) copy-start(f32[3456]{0:T(1024)} %param.18) | copy-start | bytes 41476
  139.7 5.9 %copy-start.8 = (s32[8]{0:T(128)S(1)}, s32[8]{0:T(128)}, u32[]{:S(2)}) copy-start(s32[8]{0:T(128)} %copy-done.7) | copy-start | bytes 100
  139.7 27.6 %copy-start.5 = (pred[8]{0:T(512)(128)(4,1)S(1)}, pred[8]{0:T(512)(128)(4,1)}, u32[]{:S(2)}) copy-start(pred[8]{0:T(512)(128)(4,1)} %get-tuple-element.4) | copy-start | bytes 28
  140.8 34.9 %copy-start.3 = (s32[8,128,128]{2,1,0:T(8,128)S(1)}, s32[8,128,128]{2,1,0:T(8,128)}, u32[]{:S(2)}) copy-start(s32[8,128,128]{2,1,0:T(8,128)} %param.11) | copy-start | bytes 1572868
  140.8 25.7 %all-to-all-start.5 = ((bf16[8,3,128,128]{3,2,1,0:T(8,128)(2,1)}), bf16[8,3,128,128]{3,2,1,0:T(8,128)(2,1)S(1)}, u32[]{:S(2)}, u32[]{:S(2)}) async-start(bf16[8,3,128,128]{3,2,1,0:T(8,128)(2,1)} %select_select_fusion.1), calls=%async_computation.5 | async-start | bytes 1572864 | tf_op jit(solution)/shard_map/all_to_all | solution.py:121
  167.3 8.8 %copy-start.10 = (s32[8]{0:T(128)S(1)}, s32[8]{0:T(128)}, u32[]{:S(2)}) copy-start(s32[8]{0:T(128)} %param.12) | copy-start | bytes 100
Sparse Core Ops, SparseCore 0:
  9.9 55.6 all-gather.2
  67.4 47.2 all-gather.4
where the time goes:
time: 185 us
  waiting for transfers between devices  86.5 us (47%)
  starting transfers between devices  25.2 us (14%)
  matrix products  21.6 us (12%)
  local copies, waits for them, and re-layouts  15.9 us (9%)
  between operations  14.4 us (8%)
  other arithmetic  12.6 us (7%)
  blocking collectives  8.26 us (4%)
    all_to_all x1, waiting for transfers between devices, body(): lax.all_to_all(send_rows.reshape(tables, list_depth, block_size, emb_widt...  34.1 us
    all_to_all x1, waiting for transfers between devices, body(): lax.all_to_all(returning, 'table', split_axis=0, concat_axis=0, tiled=True)  20.9 us
    all_to_all x1, waiting for transfers between devices, body(): lax.all_to_all(partial_rows, 'node', split_axis=0, concat_axis=0, tiled=T...  14.4 us
    dot_general x1, matrix products, owner_work(): jnp.dot(hidden, cross_u, preferred_element_type=jnp.float32) + cross_bias  8.67 us
    all_to_all x1, blocking collectives, body(): lax.all_to_all(tile_grad, 'node', split_axis=0, concat_axis=0, tiled=True)  8.26 us
    dot_general x1, matrix products, owner_work(): lax.dot_general(dhidden, cross_v, (((1,), (1,)), ((), ())), preferred_ele...  7.54 us
    all_to_all x1, waiting for transfers between devices, body(): lax.all_to_all(send_slot.reshape(tables, list_depth), 'table', split_axis...  5.48 us
    all_to_all x1, starting transfers between devices, body(): lax.all_to_all(tile_table, 'node', split_axis=0, concat_axis=0, tiled=True)  5.16 us
  transfers between devices with their start and end apart: 8, of which 7 were waited for; matrix products, arithmetic and copies ran while one was open for 10% of the time, Pallas kernels for 0%

commit v1 on v0

v1 whole, which is shorter than its diff:
```python
import functools

import jax
import jax.numpy as jnp
from jax import lax
from jax.experimental import pallas as pl
from jax.experimental.pallas import tpu as pltpu
from jax.sharding import PartitionSpec as P

FEATURES = 26
SAMPLE_BLOCKS = 2
BAG_BLOCKS = 52
LIST = 2
META = 16
BF16 = jnp.bfloat16
F32 = jnp.float32
SMEM = pl.BlockSpec(memory_space=pltpu.SMEM)
VMEM = pl.BlockSpec(memory_space=pltpu.VMEM)


def params(mib):
    return pltpu.CompilerParams(vmem_limit_bytes=mib << 20)


def nt_dot(left, right):
    return lax.dot_general(left, right, (((1,), (1,)), ((), ())), preferred_element_type=F32)


def tn_dot(left, right):
    return lax.dot_general(left, right, (((0,), (0,)), ((), ())), preferred_element_type=F32)


def dot(left, right):
    return jnp.dot(left, right, preferred_element_type=F32)


def block(index, size):
    return pl.ds(pl.multiple_of(index * size, size), size)


def meta_rows(count):
    return -(-2 * count // 16) * 16


def id_rows(values, rows):
    row = lax.broadcasted_iota(jnp.int32, (rows, 128), 0)
    filled = jnp.full((rows, 128), -1.0, F32)
    for i, value in enumerate(values):
        filled = jnp.where(row == i, value.astype(F32), filled)
    return filled.astype(BF16)


def products_kernel(nodes, quota, size, place_ref, rows_ref, table_ref, slot_ref, emb_ref, mult_ref, *outs):
    node = place_ref[0]
    for k in range(nodes):
        ids = []
        for i in range(quota):
            tile = (node ^ k) * quota + i
            weights = mult_ref[tile].astype(F32).astype(BF16)
            part = dot(weights, emb_ref[block(rows_ref[tile], size), :])
            outs[k][i * size : (i + 1) * size, :] = part.astype(BF16)
            ids += [table_ref[tile], slot_ref[tile]]
        outs[k][quota * size :, :] = id_rows(ids, meta_rows(quota))


def relay_kernel(nodes, quota, size, tables, relative, place_ref, *refs):
    parts, outs = refs[:nodes], refs[nodes : nodes + tables]
    index_ref, total, first_slot, slots = refs[nodes + tables :]
    table = place_ref[1]
    for r in range(tables):
        first_slot[r] = -1
        for e in range(LIST):
            slots[r * LIST + e] = -1
            total[r * LIST + e] = jnp.zeros((size, 128), F32)
    for k in range(nodes):
        ids = parts[k][quota * size :, :].astype(F32).astype(jnp.int32)
        for i in range(quota):
            target, slot = ids[2 * i, 0], ids[2 * i + 1, 0]
            entry = target ^ table if relative else target
            known = first_slot[entry]
            which = jnp.where((known < 0) | (known == slot), 0, 1)
            first_slot[entry] = jnp.where(known < 0, slot, known)
            place = entry * LIST + which
            slots[place] = slot
            index_ref[k * quota + i] = place
            total[place] += parts[k][i * size : (i + 1) * size, :].astype(F32)
    for r in range(tables):
        for e in range(LIST):
            outs[r][e * size : (e + 1) * size, :] = total[r * LIST + e].astype(BF16)
        outs[r][LIST * size :, :] = id_rows([slots[r * LIST + e] for e in range(LIST)], META)


def owner_kernel(tables, size, *refs):
    parts = refs[:tables]
    dense_ref, v_ref, u_ref, bias_ref, cot_ref = refs[tables : tables + 5]
    outs = refs[tables + 5 : 2 * tables + 5]
    first_ref, hidden_ref, total, scaled, dhidden = refs[2 * tables + 5 :]
    for b in range(BAG_BLOCKS):
        total[b] = jnp.zeros((size, 128), F32)
    slots = []
    for r in range(tables):
        ids = parts[r][LIST * size :, :].astype(F32).astype(jnp.int32)
        for e in range(LIST):
            slots.append(ids[e, 0])

            @pl.when(slots[-1] >= 0)
            def _(slot=slots[-1], r=r, e=e):
                total[slot] += parts[r][e * size : (e + 1) * size, :].astype(F32)

    first_ref[:, :128] = dense_ref[...]
    for f in range(FEATURES):
        for s in range(SAMPLE_BLOCKS):
            first_ref[s * size : (s + 1) * size, (f + 1) * 128 : (f + 2) * 128] = total[f * SAMPLE_BLOCKS + s].astype(BF16)
    hidden_ref[...] = dot(first_ref[...], v_ref[...]).astype(BF16)
    for f in range(FEATURES + 1):
        columns = slice(f * 128, (f + 1) * 128)
        scaled[:, columns] = (cot_ref[:, columns].astype(F32) * first_ref[:, columns].astype(F32)).astype(BF16)
    dhidden[...] = nt_dot(scaled[...], u_ref[...]).astype(BF16)
    for r in range(tables):
        for e in range(LIST):

            @pl.when(slots[r * LIST + e] >= 0)
            def _(slot=slots[r * LIST + e], r=r, e=e):
                columns = block(slot // SAMPLE_BLOCKS + 1, 128)
                samples = block(slot % SAMPLE_BLOCKS, size)
                scale = dot(hidden_ref[samples, :], u_ref[:, columns]) + bias_ref[:, columns]
                grad = cot_ref[samples, columns].astype(F32) * (scale + 1.0)
                grad = grad + nt_dot(dhidden[samples, :], v_ref[columns, :])
                outs[r][e * size : (e + 1) * size, :] = grad.astype(BF16)


def cross_kernel(first_ref, hidden_ref, u_ref, bias_ref, out_ref):
    width = first_ref.shape[1]
    step = 256
    for start in range(0, width, step):
        columns = slice(start, min(start + step, width))
        scale = dot(hidden_ref[...], u_ref[:, columns]) + bias_ref[:, columns]
        out_ref[:, columns] = (first_ref[:, columns].astype(F32) * (scale + 1.0)).astype(BF16)


def return_kernel(nodes, quota, size, tables, index_ref, *refs):
    parts, outs, staged = refs[:tables], refs[tables : tables + nodes], refs[-1]
    for r in range(tables):
        for e in range(LIST):
            staged[r * LIST + e] = parts[r][e * size : (e + 1) * size, :]
    for k in range(nodes):
        for i in range(quota):
            outs[k][i * size : (i + 1) * size, :] = staged[index_ref[k * quota + i]]


def rows_kernel(nodes, quota, size, place_ref, rows_ref, mult_ref, *refs):
    parts, out_ref = refs[:nodes], refs[nodes]
    node = place_ref[0]
    out_ref[...] = jnp.zeros(out_ref.shape, F32)
    for k in range(nodes):
        for i in range(quota):
            tile = (node ^ k) * quota + i
            weights = mult_ref[tile].astype(F32).astype(BF16)
            rows = block(rows_ref[tile], size)
            out_ref[rows, :] += tn_dot(weights, parts[k][i * size : (i + 1) * size, :])


def xor_permute(value, axis, k):
    size = lax.axis_size(axis)
    return lax.ppermute(value, axis, [(i, i ^ k) for i in range(size)])


def exchange_tables(parts):
    tables = len(parts)
    out = [None] * tables
    out[0] = parts[0]
    order = sorted(range(2, tables), key=lambda r: (-(r // 4), r))
    for r in order:
        out[r] = xor_permute(parts[r], "table", r)
    out[1] = xor_permute(parts[1], "table", 1)
    return out


def exchange_tables_whole(parts):
    moved = lax.all_to_all(jnp.stack(parts), "table", split_axis=0, concat_axis=0, tiled=True)
    return [moved[r] for r in range(len(parts))]


def gather_weights(cross_v, cross_u):
    node = lax.axis_index("node")
    core = lax.axis_index("table") % 2

    def gathered(shard):
        rows, width = shard.shape
        half = rows // 2
        cut = half // 32 * 16
        mine = lax.dynamic_slice(shard, (core * half, 0), (half, width))
        by_x = xor_permute(mine, "node", 1)
        by_y = xor_permute(mine, "node", 2)
        far_x = xor_permute(by_y[:cut], "node", 1)
        far_y = xor_permute(by_x[cut:], "node", 2)
        whole = jnp.zeros((rows * lax.axis_size("node"), width), shard.dtype)
        whole = lax.dynamic_update_slice(whole, shard, (node * rows, 0))
        for k, begin, piece in ((1, 0, by_x), (2, 0, by_y), (3, 0, far_x), (3, cut, far_y)):
            base = (node ^ k) * rows + begin
            whole = lax.dynamic_update_slice(whole, piece, (base + core * half, 0))
            other = xor_permute(piece, "table", 1)
            whole = lax.dynamic_update_slice(whole, other, (base + (1 - core) * half, 0))
        return whole

    return gathered(cross_v), gathered(cross_u)


def body(emb_rows, tile_mult, tile_rows, tile_table, tile_slot, dense, cross_v, cross_u, cross_bias, cotangent):
    nodes, tables = lax.axis_size("node"), lax.axis_size("table")
    tiles, size = tile_mult.shape[0], tile_mult.shape[1]
    quota = tiles // nodes
    samples, cross = cotangent.shape
    rank = cross_v.shape[1]
    relative = tables <= 8
    exchange = exchange_tables if relative else exchange_tables_whole
    place = jnp.stack([lax.axis_index("node"), lax.axis_index("table")]).astype(jnp.int32)
    bias = cross_bias.reshape(1, cross)

    full_v, full_u = gather_weights(cross_v, cross_u)

    part = jax.ShapeDtypeStruct((quota * size + meta_rows(quota), 128), BF16)
    parts = pl.pallas_call(
        functools.partial(products_kernel, nodes, quota, size),
        out_shape=[part] * nodes,
        in_specs=[SMEM] * 4 + [VMEM] * 2,
        out_specs=[VMEM] * nodes,
        compiler_params=params(16),
        name="products",
    )(place, tile_rows, tile_table, tile_slot, emb_rows, tile_mult)
    parts = [parts[0]] + [xor_permute(parts[k], "node", k) for k in range(1, nodes)]

    listed = jax.ShapeDtypeStruct((LIST * size + META, 128), BF16)
    *lists, index = pl.pallas_call(
        functools.partial(relay_kernel, nodes, quota, size, tables, relative),
        out_shape=[listed] * tables + [jax.ShapeDtypeStruct((tiles,), jnp.int32)],
        in_specs=[SMEM] + [VMEM] * nodes,
        out_specs=[VMEM] * tables + [SMEM],
        scratch_shapes=[
            pltpu.VMEM((tables * LIST, size, 128), F32),
            pltpu.SMEM((tables,), jnp.int32),
            pltpu.SMEM((tables * LIST,), jnp.int32),
        ],
        compiler_params=params(32),
        name="relay",
    )(place, *parts)
    arrived = exchange(lists)

    grad = jax.ShapeDtypeStruct((LIST * size, 128), BF16)
    *grads, first, hidden = pl.pallas_call(
        functools.partial(owner_kernel, tables, size),
        out_shape=[grad] * tables
        + [jax.ShapeDtypeStruct((samples, cross), BF16), jax.ShapeDtypeStruct((samples, rank), BF16)],
        in_specs=[VMEM] * (tables + 5),
        out_specs=[VMEM] * (tables + 2),
        scratch_shapes=[
            pltpu.VMEM((BAG_BLOCKS, size, 128), F32),
            pltpu.VMEM((samples, cross), BF16),
            pltpu.VMEM((samples, rank), BF16),
        ],
        compiler_params=params(48),
        name="owner",
    )(*arrived, dense, full_v, full_u, bias, cotangent)
    returned = exchange(grads)

    cross_out = pl.pallas_call(
        cross_kernel,
        out_shape=jax.ShapeDtypeStruct((samples, cross), BF16),
        in_specs=[VMEM] * 4,
        out_specs=VMEM,
        compiler_params=params(32),
        name="cross",
    )(first, hidden, full_u, bias)

    back = jax.ShapeDtypeStruct((quota * size, 128), BF16)
    backs = pl.pallas_call(
        functools.partial(return_kernel, nodes, quota, size, tables),
        out_shape=[back] * nodes,
        in_specs=[SMEM] + [VMEM] * tables,
        out_specs=[VMEM] * nodes,
        scratch_shapes=[pltpu.VMEM((tables * LIST, size, 128), BF16)],
        compiler_params=params(32),
        name="back",
    )(index, *returned)
    backs = [backs[0]] + [xor_permute(backs[k], "node", k) for k in range(1, nodes)]

    emb_grad = pl.pallas_call(
        functools.partial(rows_kernel, nodes, quota, size),
        out_shape=jax.ShapeDtypeStruct(emb_rows.shape, F32),
        in_specs=[SMEM] * 2 + [VMEM] * (nodes + 1),
        out_specs=VMEM,
        compiler_params=params(16),
        name="rows",
    )(place, tile_rows, tile_mult, *backs)
    return cross_out, emb_grad


def solution(mesh):
    both = ("node", "table")
    in_specs = (
        P(both, None),
        P(both, None, None),
        P(both),
        P(both),
        P(both),
        P(both, None),
        P("node", None),
        P("node", None),
        P(),
        P(both, None),
    )
    out_specs = (P(both, None), P(both, None))
    return jax.shard_map(body, mesh=mesh, in_specs=in_specs, out_specs=out_specs, check_vma=False)
```

time: 185 us -> 120 us (0.65)
  waiting for transfers between devices: 86.5 us -> 45.2 us
  matrix products: 21.6 us -> 0 us
  Pallas kernels: 0 us -> 14.8 us
  between operations: 14.4 us -> 1.18 us
  other arithmetic: 12.6 us -> 0.07 us
  starting transfers between devices: 25.2 us -> 36 us
  blocking collectives: 8.26 us -> 0 us
  local copies, waits for them, and re-layouts: 15.9 us -> 21.4 us
    all_to_all x6 -> x0, waiting for transfers between devices: 80.2 us -> none  [the longest x1 34.1 us: body(): lax.all_to_all(send_rows.reshape(tables, list_depth, block_size, emb_widt...]
    ppermute x0 -> x36, waiting for transfers between devices: none -> 45.2 us  [xor_permute(): return lax.ppermute(value, axis, [(i, i ^ k) for i in range(size)])]
    ppermute x0 -> x36, starting transfers between devices: none -> 36 us  [xor_permute(): return lax.ppermute(value, axis, [(i, i ^ k) for i in range(size)])]
    all_to_all x6 -> x0, starting transfers between devices: 25.2 us -> none  [the longest x1 5.16 us: body(): lax.all_to_all(tile_table, 'node', split_axis=0, concat_axis=0, tiled=True)]
    dot_general x6 -> x0, matrix products: 21.6 us -> none  [the longest x1 8.67 us: owner_work(): jnp.dot(hidden, cross_u, preferred_element_type=jnp.float32) + cross_bias]
    pallas_call x0 -> x6, Pallas kernels: none -> 14.8 us  [the longest x1 7.24 us: body(): pl.pallas_call(functools.partial(owner_kernel, tables, size), out_shape=[...]
    all_to_all x1 -> x0, blocking collectives: 8.26 us -> none  [body(): lax.all_to_all(tile_grad, 'node', split_axis=0, concat_axis=0, tiled=True)]
    unnamed x27 -> x44, local copies, waits for them, and re-layouts: 1.29 us -> 7.83 us
  transfers between devices with their start and end apart: 8 -> 36, of which waited for: 7 -> 13; matrix products, arithmetic and copies ran while one was open for 10% -> 10% of each run, Pallas kernels for 0% -> 5%
where the time goes in v1:
time: 120 us; the launch traced here: 119 us
  waiting for transfers between devices  45.2 us (38%)
  starting transfers between devices  36 us (30%)
  local copies, waits for them, and re-layouts  21.4 us (18%)
  Pallas kernels  14.8 us (12%)
    ppermute x36, waiting for transfers between devices, xor_permute(): return lax.ppermute(value, axis, [(i, i ^ k) for i in range(size)])  45.2 us
    ppermute x36, starting transfers between devices, xor_permute(): return lax.ppermute(value, axis, [(i, i ^ k) for i in range(size)])  36 us
    unnamed x44, local copies, waits for them, and re-layouts  7.83 us
    pallas_call x1, Pallas kernels, body(): pl.pallas_call(functools.partial(owner_kernel, tables, size), out_shape=[...  7.24 us
    dynamic_update_slice x8, local copies, waits for them, and re-layouts, gathered(): whole = lax.dynamic_update_slice(whole, piece, (base + core * half, 0))  4.56 us
    dynamic_slice x2, local copies, waits for them, and re-layouts, gathered(): mine = lax.dynamic_slice(shard, (core * half, 0), (half, width))  3.63 us
  transfers between devices with their start and end apart: 36, of which 13 were waited for; matrix products, arithmetic and copies ran while one was open for 10% of the time, Pallas kernels for 5%

profile of v1, /device:TPU:0, one launch (start us, length us, event | category | flops | bytes accessed | tf_op | source)
XLA Modules:
  0.0 118.7 jit_solution(15504647567225131351)
XLA Ops:
  0.6 1.8 %constant_dynamic-slice_fusion = bf16[64,3456]{1,0:T(8,128)(2,1)} fusion(bf16[128,3456]{1,0:T(8,128)(2,1)} %param.17, s32[]{:T(128)S(6)} %select_n.79), kind=kLoop, calls=%fused_computation.8 | loop fusion | bytes 884740 | tf_op jit(solution)/shard_map/dynamic_slice | solution.py:192
  2.5 2.9 %collective-permute-start.18 = (bf16[64,3456]{1,0:T(8,128)(2,1)}, bf16[64,3456]{1,0:T(8,128)(2,1)}, u32[]{:S(2)}, u32[]{:S(2)}) collective-permute-start(bf16[64,3456]{1,0:T(8,128)(2,1)} %constant_dynamic-slice_fusion), channel_id=1, source_target_pairs={{0,8},{8,0},{16,24},{24,16},{1,9},{9,1},{17,25},{25,17},{2,10},{10... | collective-permute-start | bytes 1327112 | tf_op jit(solution)/shard_map/ppermute | solution.py:165
  5.4 1.5 %collective-permute-start.20 = (bf16[64,3456]{1,0:T(8,128)(2,1)}, bf16[64,3456]{1,0:T(8,128)(2,1)}, u32[]{:S(2)}, u32[]{:S(2)}) collective-permute-start(bf16[64,3456]{1,0:T(8,128)(2,1)} %constant_dynamic-slice_fusion), channel_id=1, source_target_pairs={{0,16},{8,24},{16,0},{24,8},{1,17},{9,25},{17,1},{25,9},{2,18},{10... | collective-permute-start | bytes 1327112 | tf_op jit(solution)/shard_map/ppermute | solution.py:165
  10.9 1.4 %products.1 = (bf16[272,128]{1,0:T(8,128)(2,1)S(1)}, bf16[272,128]{1,0:T(8,128)(2,1)S(1)}, bf16[272,128]{1,0:T(8,128)(2,1)}, bf16[272,128]{1,0:T(8,128)(2,1)S(1)}) custom-call(s32[2]{0:T(128)S(1)} %pad_add_fusion.place_ref, s32[8]{0:T(128)S(1)} %copy-done.14, s32[8]{0:T(128)S(1)} %copy-done.16, s32[8]{0:T(128)S(1)} %copy-done.17, ...), custom_call_target="tpu_custom_call" | custom-call | tf_op jit(solution)/shard_map/products/pallas_call | solution.py:223
  13.5 1.8 %constant_dynamic-slice_fusion.1 = bf16[432,512]{1,0:T(8,128)(2,1)} fusion(bf16[864,512]{1,0:T(8,128)(2,1)} %param.16, s32[]{:T(128)S(6)} %select_n.69), kind=kLoop, calls=%fused_computation.18 | loop fusion | bytes 884740 | tf_op jit(solution)/shard_map/dynamic_slice | solution.py:192
  15.3 1.5 %collective-permute-start.10 = (bf16[432,512]{1,0:T(8,128)(2,1)}, bf16[432,512]{1,0:T(8,128)(2,1)}, u32[]{:S(2)}, u32[]{:S(2)}) collective-permute-start(bf16[432,512]{1,0:T(8,128)(2,1)} %constant_dynamic-slice_fusion.1), channel_id=1, source_target_pairs={{0,8},{8,0},{16,24},{24,16},{1,9},{9,1},{17,25},{25,17},{2,10},{10... | collective-permute-start | bytes 1327112 | tf_op jit(solution)/shard_map/ppermute | solution.py:165
  18.0 2.8 %collective-permute-start.1 = (bf16[272,128]{1,0:T(8,128)(2,1)}, bf16[272,128]{1,0:T(8,128)(2,1)}, u32[]{:S(2)}, u32[]{:S(2)}) collective-permute-start(bf16[272,128]{1,0:T(8,128)(2,1)} %get-tuple-element.31), channel_id=1, source_target_pairs={{0,16},{8,24},{16,0},{24,8},{1,17},{9,25},{17,1},{25,9},{2,18},{10... | collective-permute-start | bytes 208904 | tf_op jit(solution)/shard_map/ppermute | solution.py:165
  22.1 7.2 %collective-permute-done.1.refs_2_ = bf16[272,128]{1,0:T(8,128)(2,1)} collective-permute-done((bf16[272,128]{1,0:T(8,128)(2,1)}, bf16[272,128]{1,0:T(8,128)(2,1)}, u32[]{:S(2)}, u32[]{:S(2)}) %collective-permute-start.1) | collective-permute-done | bytes 69664 | tf_op jit(solution)/shard_map/ppermute | solution.py:165
  30.1 4.7 %collective-permute-done.2.refs_3_ = bf16[272,128]{1,0:T(8,128)(2,1)S(1)} collective-permute-done((bf16[272,128]{1,0:T(8,128)(2,1)}, bf16[272,128]{1,0:T(8,128)(2,1)S(1)}, u32[]{:S(2)}, u32[]{:S(2)}) %collective-permute-start.2) | collective-permute-done | bytes 69664 | tf_op jit(solution)/shard_map/ppermute | solution.py:165
  35.4 1.6 %relay.1 = (bf16[272,128]{1,0:T(8,128)(2,1)S(1)}, bf16[272,128]{1,0:T(8,128)(2,1)S(1)}, bf16[272,128]{1,0:T(8,128)(2,1)S(1)}, bf16[272,128]{1,0:T(8,128)(2,1)S(1...) custom-call(s32[2]{0:T(128)S(1)} %copy-done.12, ...), custom_call_target="tpu_custom_call" | custom-call | tf_op jit(solution)/shard_map/relay/pallas_call | solution.py:234
  37.2 1.6 %collective-permute-start.4 = (bf16[272,128]{1,0:T(8,128)(2,1)S(1)}, bf16[272,128]{1,0:T(8,128)(2,1)S(1)}, u32[]{:S(2)}, u32[]{:S(2)}) collective-permute-start(bf16[272,128]{1,0:T(8,128)(2,1)S(1)} %get-tuple-element.35), channel_id=1, source_target_pairs={{0,2},{1,3},{2,0},{3,1},{4,6},{5,7},{6,4},{7,5},{8,10},{9,11},{10,... | collective-permute-start | bytes 208904 | tf_op jit(solution)/shard_map/ppermute | solution.py:165
  44.7 1.1 constant_dynamic-update-slice_fusion.7
  47.4 1.3 %collective-permute-done.22 = bf16[32,3456]{1,0:T(8,128)(2,1)S(1)} collective-permute-done((bf16[32,3456]{1,0:T(8,128)(2,1)S(1)}, bf16[32,3456]{1,0:T(8,128)(2,1)S(1)}, u32[]{:S(2)}, u32[]{:S(2)}) %collective-permute-start.22) | collective-permute-done | bytes 221216 | tf_op jit(solution)/shard_map/ppermute | solution.py:165
  49.3 6.3 %collective-permute-done.24 = bf16[32,3456]{1,0:T(8,128)(2,1)S(1)} collective-permute-done((bf16[32,3456]{1,0:T(8,128)(2,1)S(1)}, bf16[32,3456]{1,0:T(8,128)(2,1)S(1)}, u32[]{:S(2)}, u32[]{:S(2)}) %collective-permute-start.24) | collective-permute-done | bytes 221216 | tf_op jit(solution)/shard_map/ppermute | solution.py:165
  56.2 1.3 %collective-permute-done.25 = bf16[32,3456]{1,0:T(8,128)(2,1)S(1)} collective-permute-done((bf16[32,3456]{1,0:T(8,128)(2,1)S(1)}, bf16[32,3456]{1,0:T(8,128)(2,1)S(1)}, u32[]{:S(2)}, u32[]{:S(2)}) %collective-permute-start.25) | collective-permute-done | bytes 221216 | tf_op jit(solution)/shard_map/ppermute | solution.py:165
  58.7 1.3 %constant_dynamic-update-slice_fusion.14 = bf16[3456,512]{1,0:T(8,128)(2,1)S(1)} fusion(bf16[3456,512]{1,0:T(8,128)(2,1)S(1)} %constant_dynamic-update-slice_fusion.15, bf16[432,512]{1,0:T(8,128)(2,1)} %collective-permute-done.12, s32[]{:T(128)S(6)} %select_n.72), kind=kLoop, calls=%fused_computation.15 | loop fusion | bytes 884740 | tf_op jit(solution)/shard_map/dynamic_update_slice | solution.py:201
  60.0 5.3 %collective-permute-done.14 = bf16[208,512]{1,0:T(8,128)(2,1)S(1)} collective-permute-done((bf16[208,512]{1,0:T(8,128)(2,1)S(1)}, bf16[208,512]{1,0:T(8,128)(2,1)S(1)}, u32[]{:S(2)}, u32[]{:S(2)}) %collective-permute-start.14) | collective-permute-done | bytes 213024 | tf_op jit(solution)/shard_map/ppermute | solution.py:165
  65.9 6.3 %collective-permute-done.16 = bf16[224,512]{1,0:T(8,128)(2,1)S(1)} collective-permute-done((bf16[224,512]{1,0:T(8,128)(2,1)S(1)}, bf16[224,512]{1,0:T(8,128)(2,1)S(1)}, u32[]{:S(2)}, u32[]{:S(2)}) %collective-permute-start.16) | collective-permute-done | bytes 229408 | tf_op jit(solution)/shard_map/ppermute | solution.py:165
  72.2 2.6 %collective-permute-start.6 = (bf16[272,128]{1,0:T(8,128)(2,1)S(1)}, bf16[272,128]{1,0:T(8,128)(2,1)S(1)}, u32[]{:S(2)}, u32[]{:S(2)}) collective-permute-start(bf16[272,128]{1,0:T(8,128)(2,1)S(1)} %get-tuple-element.37), channel_id=1, source_target_pairs={{0,4},{1,5},{2,6},{3,7},{4,0},{5,1},{6,2},{7,3},{8,12},{9,13},{10,... | collective-permute-start | bytes 208904 | tf_op jit(solution)/shard_map/ppermute | solution.py:165
  75.3 3.6 %collective-permute-start.8 = (bf16[272,128]{1,0:T(8,128)(2,1)S(1)}, bf16[272,128]{1,0:T(8,128)(2,1)S(1)}, u32[]{:S(2)}, u32[]{:S(2)}) collective-permute-start(bf16[272,128]{1,0:T(8,128)(2,1)S(1)} %get-tuple-element.39), channel_id=1, source_target_pairs={{0,6},{1,7},{2,4},{3,5},{4,2},{5,3},{6,0},{7,1},{8,14},{9,15},{10,... | collective-permute-start | bytes 208904 | tf_op jit(solution)/shard_map/ppermute | solution.py:165
  79.6 3.3 %collective-permute-done.8.refs_6_ = bf16[272,128]{1,0:T(8,128)(2,1)S(1)} collective-permute-done((bf16[272,128]{1,0:T(8,128)(2,1)S(1)}, bf16[272,128]{1,0:T(8,128)(2,1)S(1)}, u32[]{:S(2)}, u32[]{:S(2)}) %collective-permute-start.8) | collective-permute-done | bytes 69664 | tf_op jit(solution)/shard_map/ppermute | solution.py:165
  82.9 2.4 %collective-permute-done.9.refs_7_ = bf16[272,128]{1,0:T(8,128)(2,1)S(1)} collective-permute-done((bf16[272,128]{1,0:T(8,128)(2,1)S(1)}, bf16[272,128]{1,0:T(8,128)(2,1)S(1)}, u32[]{:S(2)}, u32[]{:S(2)}) %collective-permute-start.9) | collective-permute-done | bytes 69664 | tf_op jit(solution)/shard_map/ppermute | solution.py:165
  85.2 7.2 %owner.1 = (bf16[256,128]{1,0:T(8,128)(2,1)S(1)}, bf16[256,128]{1,0:T(8,128)(2,1)S(1)}, bf16[256,128]{1,0:T(8,128)(2,1)S(1)}, bf16[256,128]{1,0:T(8,128)(2,1)S(1...) custom-call(bf16[272,128]{1,0:T(8,128)(2,1)S(1)} %get-tuple-element., ...), custom_call_target="tpu_custom_call" | custom-call | tf_op jit(solution)/shard_map/owner/pallas_call | solution.py:250
  92.6 3.5 %collective-permute-start.27 = (bf16[256,128]{1,0:T(8,128)(2,1)S(1)}, bf16[256,128]{1,0:T(8,128)(2,1)S(1)}, u32[]{:S(2)}, u32[]{:S(2)}) collective-permute-start(bf16[256,128]{1,0:T(8,128)(2,1)S(1)} %get-tuple-element.46), channel_id=1, source_target_pairs={{0,2},{1,3},{2,0},{3,1},{4,6},{5,7},{6,4},{7,5},{8,10},{9,11},{10,... | collective-permute-start | bytes 196616 | tf_op jit(solution)/shard_map/ppermute | solution.py:165
  96.1 2.5 %collective-permute-start.29 = (bf16[256,128]{1,0:T(8,128)(2,1)S(1)}, bf16[256,128]{1,0:T(8,128)(2,1)S(1)}, u32[]{:S(2)}, u32[]{:S(2)}) collective-permute-start(bf16[256,128]{1,0:T(8,128)(2,1)S(1)} %get-tuple-element.48), channel_id=1, source_target_pairs={{0,4},{1,5},{2,6},{3,7},{4,0},{5,1},{6,2},{7,3},{8,12},{9,13},{10,... | collective-permute-start | bytes 196616 | tf_op jit(solution)/shard_map/ppermute | solution.py:165
  99.0 2.1 %collective-permute-start.31 = (bf16[256,128]{1,0:T(8,128)(2,1)S(1)}, bf16[256,128]{1,0:T(8,128)(2,1)S(1)}, u32[]{:S(2)}, u32[]{:S(2)}) collective-permute-start(bf16[256,128]{1,0:T(8,128)(2,1)S(1)} %get-tuple-element.50), channel_id=1, source_target_pairs={{0,6},{1,7},{2,4},{3,5},{4,2},{5,3},{6,0},{7,1},{8,14},{9,15},{10,... | collective-permute-start | bytes 196616 | tf_op jit(solution)/shard_map/ppermute | solution.py:165
  101.1 1.2 %collective-permute-start.32 = (bf16[256,128]{1,0:T(8,128)(2,1)S(1)}, bf16[256,128]{1,0:T(8,128)(2,1)S(1)}, u32[]{:S(2)}, u32[]{:S(2)}) collective-permute-start(bf16[256,128]{1,0:T(8,128)(2,1)S(1)} %get-tuple-element.51), channel_id=1, source_target_pairs={{0,7},{1,6},{2,5},{3,4},{4,3},{5,2},{6,1},{7,0},{8,15},{9,14},{10,... | collective-permute-start | bytes 196616 | tf_op jit(solution)/shard_map/ppermute | solution.py:165
  102.3 6.3 %collective-permute-done.30.refs_5_ = bf16[256,128]{1,0:T(8,128)(2,1)S(1)} collective-permute-done((bf16[256,128]{1,0:T(8,128)(2,1)S(1)}, bf16[256,128]{1,0:T(8,128)(2,1)S(1)}, u32[]{:S(2)}, u32[]{:S(2)}) %collective-permute-start.30) | collective-permute-done | bytes 65568 | tf_op jit(solution)/shard_map/ppermute | solution.py:165
  110.9 1.8 %collective-permute-start.35 = (bf16[256,128]{1,0:T(8,128)(2,1)S(1)}, bf16[256,128]{1,0:T(8,128)(2,1)S(1)}, u32[]{:S(2)}, u32[]{:S(2)}) collective-permute-start(bf16[256,128]{1,0:T(8,128)(2,1)S(1)} %get-tuple-element.55), channel_id=1, source_target_pairs={{0,24},{8,16},{16,8},{24,0},{1,25},{9,17},{17,9},{25,1},{2,26},{10... | collective-permute-start | bytes 196616 | tf_op jit(solution)/shard_map/ppermute | solution.py:165
  112.7 2.0 %copy-done.1 = bf16[512,3456]{1,0:T(8,128)(2,1)S(1)} copy-done((bf16[512,3456]{1,0:T(8,128)(2,1)S(1)}, bf16[512,3456]{1,0:T(8,128)(2,1)}, u32[]{:S(2)}) %copy-start.1) | copy-done | bytes 3538968
  114.7 2.4 %cross.1 = bf16[256,3456]{1,0:T(8,128)(2,1)} custom-call(bf16[256,3456]{1,0:T(8,128)(2,1)S(1)} %get-tuple-element.41.first_ref, bf16[256,512]{1,0:T(8,128)(2,1)S(1)} %get-tuple-element.42.hidden_ref, bf16[512,3456]{1,0:T(8,128)(2,1)S(1)} %copy-done.1, f32[1,3456]{1,0:T(1,128)S(1)} %reshape.7.refs_11_.bias_ref), custom_call_target="tpu_custom_call" | custom-call | tf_op jit(solution)/shard_map/cross/pallas_call | solution.py:266
  117.2 1.5 %rows.1 = f32[512,128]{1,0:T(8,128)} custom-call(s32[2]{0:T(128)S(1)} %copy-done.13, s32[8]{0:T(128)S(1)} %copy-done.15, s32[8,128,128]{2,1,0:T(8,128)S(1)} %copy-done.3, bf16[256,128]{1,0:T(8,128)(2,1)S(1)} %get-tuple-element.52.refs_0_, bf16[256,128]{1,0:T(8,128)(2,1)S(1)} %collective-permute-done.33.refs_1_, ...), custom_call_target="tpu_custom_call" | custom-call | tf_op jit(solution)/shard_map/rows/pallas_call | solution.py:287
  (118 shorter events, 23.3 us)
Async XLA Ops:
  2.5 37.3 %collective-permute-start.18 = (bf16[64,3456]{1,0:T(8,128)(2,1)}, bf16[64,3456]{1,0:T(8,128)(2,1)}, u32[]{:S(2)}, u32[]{:S(2)}) collective-permute-start(bf16[64,3456]{1,0:T(8,128)(2,1)} %constant_dynamic-slice_fusion), channel_id=1, source_target_pairs={{0,8},{8,0},{16,24},{24,16},{1,9},{9,1},{17,25},{25,17},{2,10},{10... | collective-permute-start | bytes 1327112 | tf_op jit(solution)/shard_map/ppermute | solution.py:165
  5.4 31.7 %collective-permute-start.20 = (bf16[64,3456]{1,0:T(8,128)(2,1)}, bf16[64,3456]{1,0:T(8,128)(2,1)}, u32[]{:S(2)}, u32[]{:S(2)}) collective-permute-start(bf16[64,3456]{1,0:T(8,128)(2,1)} %constant_dynamic-slice_fusion), channel_id=1, source_target_pairs={{0,16},{8,24},{16,0},{24,8},{1,17},{9,25},{17,1},{25,9},{2,18},{10... | collective-permute-start | bytes 1327112 | tf_op jit(solution)/shard_map/ppermute | solution.py:165
  13.0 4.4 %collective-permute-start = (bf16[272,128]{1,0:T(8,128)(2,1)S(1)}, bf16[272,128]{1,0:T(8,128)(2,1)S(1)}, u32[]{:S(2)}, u32[]{:S(2)}) collective-permute-start(bf16[272,128]{1,0:T(8,128)(2,1)S(1)} %get-tuple-element.30), channel_id=1, source_target_pairs={{0,8},{8,0},{16,24},{24,16},{1,9},{9,1},{17,25},{25,17},{2,10},{10... | collective-permute-start | bytes 208904 | tf_op jit(solution)/shard_map/ppermute | solution.py:165
  15.3 27.3 %collective-permute-start.10 = (bf16[432,512]{1,0:T(8,128)(2,1)}, bf16[432,512]{1,0:T(8,128)(2,1)}, u32[]{:S(2)}, u32[]{:S(2)}) collective-permute-start(bf16[432,512]{1,0:T(8,128)(2,1)} %constant_dynamic-slice_fusion.1), channel_id=1, source_target_pairs={{0,8},{8,0},{16,24},{24,16},{1,9},{9,1},{17,25},{25,17},{2,10},{10... | collective-permute-start | bytes 1327112 | tf_op jit(solution)/shard_map/ppermute | solution.py:165
  16.8 24.2 %collective-permute-start.12 = (bf16[432,512]{1,0:T(8,128)(2,1)}, bf16[432,512]{1,0:T(8,128)(2,1)}, u32[]{:S(2)}, u32[]{:S(2)}) collective-permute-start(bf16[432,512]{1,0:T(8,128)(2,1)} %constant_dynamic-slice_fusion.1), channel_id=1, source_target_pairs={{0,16},{8,24},{16,0},{24,8},{1,17},{9,25},{17,1},{25,9},{2,18},{10... | collective-permute-start | bytes 1327112 | tf_op jit(solution)/shard_map/ppermute | solution.py:165
  18.0 11.4 %collective-permute-start.1 = (bf16[272,128]{1,0:T(8,128)(2,1)}, bf16[272,128]{1,0:T(8,128)(2,1)}, u32[]{:S(2)}, u32[]{:S(2)}) collective-permute-start(bf16[272,128]{1,0:T(8,128)(2,1)} %get-tuple-element.31), channel_id=1, source_target_pairs={{0,16},{8,24},{16,0},{24,8},{1,17},{9,25},{17,1},{25,9},{2,18},{10... | collective-permute-start | bytes 208904 | tf_op jit(solution)/shard_map/ppermute | solution.py:165
  29.4 5.4 %collective-permute-start.2 = (bf16[272,128]{1,0:T(8,128)(2,1)}, bf16[272,128]{1,0:T(8,128)(2,1)S(1)}, u32[]{:S(2)}, u32[]{:S(2)}) collective-permute-start(bf16[272,128]{1,0:T(8,128)(2,1)} %copy-done.18), channel_id=1, source_target_pairs={{0,24},{8,16},{16,8},{24,0},{1,25},{9,17},{17,9},{25,1},{2,26},{10... | collective-permute-start | bytes 208904 | tf_op jit(solution)/shard_map/ppermute | solution.py:165
  37.1 37.7 %collective-permute-start.3 = (bf16[272,128]{1,0:T(8,128)(2,1)S(1)}, bf16[272,128]{1,0:T(8,128)(2,1)S(1)}, u32[]{:S(2)}, u32[]{:S(2)}) collective-permute-start(bf16[272,128]{1,0:T(8,128)(2,1)S(1)} %get-tuple-element.34), channel_id=1, source_target_pairs={{0,1},{1,0},{2,3},{3,2},{4,5},{5,4},{6,7},{7,6},{8,9},{9,8},{10,11... | collective-permute-start | bytes 208904 | tf_op jit(solution)/shard_map/ppermute | solution.py:165
  37.2 38.2 %collective-permute-start.4 = (bf16[272,128]{1,0:T(8,128)(2,1)S(1)}, bf16[272,128]{1,0:T(8,128)(2,1)S(1)}, u32[]{:S(2)}, u32[]{:S(2)}) collective-permute-start(bf16[272,128]{1,0:T(8,128)(2,1)S(1)} %get-tuple-element.35), channel_id=1, source_target_pairs={{0,2},{1,3},{2,0},{3,1},{4,6},{5,7},{6,4},{7,5},{8,10},{9,11},{10,... | collective-permute-start | bytes 208904 | tf_op jit(solution)/shard_map/ppermute | solution.py:165
  39.8 39.2 %collective-permute-start.5 = (bf16[272,128]{1,0:T(8,128)(2,1)S(1)}, bf16[272,128]{1,0:T(8,128)(2,1)S(1)}, u32[]{:S(2)}, u32[]{:S(2)}) collective-permute-start(bf16[272,128]{1,0:T(8,128)(2,1)S(1)} %get-tuple-element.36), channel_id=1, source_target_pairs={{0,3},{1,2},{2,1},{3,0},{4,7},{5,6},{6,5},{7,4},{8,11},{9,10},{10,... | collective-permute-start | bytes 208904 | tf_op jit(solution)/shard_map/ppermute | solution.py:165
  41.0 7.8 %collective-permute-start.22 = (bf16[32,3456]{1,0:T(8,128)(2,1)S(1)}, bf16[32,3456]{1,0:T(8,128)(2,1)S(1)}, u32[]{:S(2)}, u32[]{:S(2)}) collective-permute-start(bf16[32,3456]{1,0:T(8,128)(2,1)S(1)} %slice.18), channel_id=1, source_target_pairs={{0,8},{8,0},{16,24},{24,16},{1,9},{9,1},{17,25},{25,17},{2,10},{10... | collective-permute-start | bytes 663560 | tf_op jit(solution)/shard_map/ppermute | solution.py:165
  48.8 6.9 %collective-permute-start.24 = (bf16[32,3456]{1,0:T(8,128)(2,1)S(1)}, bf16[32,3456]{1,0:T(8,128)(2,1)S(1)}, u32[]{:S(2)}, u32[]{:S(2)}) collective-permute-start(bf16[32,3456]{1,0:T(8,128)(2,1)S(1)} %slice.19), channel_id=1, source_target_pairs={{0,16},{8,24},{16,0},{24,8},{1,17},{9,25},{17,1},{25,9},{2,18},{10... | collective-permute-start | bytes 663560 | tf_op jit(solution)/shard_map/ppermute | solution.py:165
  49.3 6.4 %collective-permute-start.23 = (bf16[32,3456]{1,0:T(8,128)(2,1)S(1)}, bf16[32,3456]{1,0:T(8,128)(2,1)S(1)}, u32[]{:S(2)}, u32[]{:S(2)}) collective-permute-start(bf16[32,3456]{1,0:T(8,128)(2,1)S(1)} %collective-permute-done.22), channel_id=1, source_target_pairs={{0,1},{1,0},{2,3},{3,2},{4,5},{5,4},{6,7},{7,6},{8,9},{9,8},{10,11... | collective-permute-start | bytes 663560 | tf_op jit(solution)/shard_map/ppermute | solution.py:165
  57.5 8.3 %collective-permute-start.13 = (bf16[432,512]{1,0:T(8,128)(2,1)}, bf16[432,512]{1,0:T(8,128)(2,1)S(1)}, u32[]{:S(2)}, u32[]{:S(2)}) collective-permute-start(bf16[432,512]{1,0:T(8,128)(2,1)} %collective-permute-done.12), channel_id=1, source_target_pairs={{0,1},{1,0},{2,3},{3,2},{4,5},{5,4},{6,7},{7,6},{8,9},{9,8},{10,11... | collective-permute-start | bytes 1327112 | tf_op jit(solution)/shard_map/ppermute | solution.py:165
  58.0 7.3 %collective-permute-start.14 = (bf16[208,512]{1,0:T(8,128)(2,1)S(1)}, bf16[208,512]{1,0:T(8,128)(2,1)S(1)}, u32[]{:S(2)}, u32[]{:S(2)}) collective-permute-start(bf16[208,512]{1,0:T(8,128)(2,1)S(1)} %slice.16), channel_id=1, source_target_pairs={{0,8},{8,0},{16,24},{24,16},{1,9},{9,1},{17,25},{25,17},{2,10},{10... | collective-permute-start | bytes 638984 | tf_op jit(solution)/shard_map/ppermute | solution.py:165
  65.3 6.9 %collective-permute-start.16 = (bf16[224,512]{1,0:T(8,128)(2,1)S(1)}, bf16[224,512]{1,0:T(8,128)(2,1)S(1)}, u32[]{:S(2)}, u32[]{:S(2)}) collective-permute-start(bf16[224,512]{1,0:T(8,128)(2,1)S(1)} %slice.17), channel_id=1, source_target_pairs={{0,16},{8,24},{16,0},{24,8},{1,17},{9,25},{17,1},{25,9},{2,18},{10... | collective-permute-start | bytes 688136 | tf_op jit(solution)/shard_map/ppermute | solution.py:165
  65.8 8.9 %collective-permute-start.15 = (bf16[208,512]{1,0:T(8,128)(2,1)S(1)}, bf16[208,512]{1,0:T(8,128)(2,1)S(1)}, u32[]{:S(2)}, u32[]{:S(2)}) collective-permute-start(bf16[208,512]{1,0:T(8,128)(2,1)S(1)} %collective-permute-done.14), channel_id=1, source_target_pairs={{0,1},{1,0},{2,3},{3,2},{4,5},{5,4},{6,7},{7,6},{8,9},{9,8},{10,11... | collective-permute-start | bytes 638984 | tf_op jit(solution)/shard_map/ppermute | solution.py:165
  72.2 6.8 %collective-permute-start.6 = (bf16[272,128]{1,0:T(8,128)(2,1)S(1)}, bf16[272,128]{1,0:T(8,128)(2,1)S(1)}, u32[]{:S(2)}, u32[]{:S(2)}) collective-permute-start(bf16[272,128]{1,0:T(8,128)(2,1)S(1)} %get-tuple-element.37), channel_id=1, source_target_pairs={{0,4},{1,5},{2,6},{3,7},{4,0},{5,1},{6,2},{7,3},{8,12},{9,13},{10,... | collective-permute-start | bytes 208904 | tf_op jit(solution)/shard_map/ppermute | solution.py:165
  74.7 4.2 %collective-permute-start.17 = (bf16[224,512]{1,0:T(8,128)(2,1)S(1)}, bf16[224,512]{1,0:T(8,128)(2,1)S(1)}, u32[]{:S(2)}, u32[]{:S(2)}) collective-permute-start(bf16[224,512]{1,0:T(8,128)(2,1)S(1)} %collective-permute-done.16), channel_id=1, source_target_pairs={{0,1},{1,0},{2,3},{3,2},{4,5},{5,4},{6,7},{7,6},{8,9},{9,8},{10,11... | collective-permute-start | bytes 688136 | tf_op jit(solution)/shard_map/ppermute | solution.py:165
  74.8 4.8 %collective-permute-start.7 = (bf16[272,128]{1,0:T(8,128)(2,1)S(1)}, bf16[272,128]{1,0:T(8,128)(2,1)S(1)}, u32[]{:S(2)}, u32[]{:S(2)}) collective-permute-start(bf16[272,128]{1,0:T(8,128)(2,1)S(1)} %get-tuple-element.38), channel_id=1, source_target_pairs={{0,5},{1,4},{2,7},{3,6},{4,1},{5,0},{6,3},{7,2},{8,13},{9,12},{10,... | collective-permute-start | bytes 208904 | tf_op jit(solution)/shard_map/ppermute | solution.py:165
  75.3 7.5 %collective-permute-start.8 = (bf16[272,128]{1,0:T(8,128)(2,1)S(1)}, bf16[272,128]{1,0:T(8,128)(2,1)S(1)}, u32[]{:S(2)}, u32[]{:S(2)}) collective-permute-start(bf16[272,128]{1,0:T(8,128)(2,1)S(1)} %get-tuple-element.39), channel_id=1, source_target_pairs={{0,6},{1,7},{2,4},{3,5},{4,2},{5,3},{6,0},{7,1},{8,14},{9,15},{10,... | collective-permute-start | bytes 208904 | tf_op jit(solution)/shard_map/ppermute | solution.py:165
  78.9 6.3 %collective-permute-start.9 = (bf16[272,128]{1,0:T(8,128)(2,1)S(1)}, bf16[272,128]{1,0:T(8,128)(2,1)S(1)}, u32[]{:S(2)}, u32[]{:S(2)}) collective-permute-start(bf16[272,128]{1,0:T(8,128)(2,1)S(1)} %get-tuple-element.40), channel_id=1, source_target_pairs={{0,7},{1,6},{2,5},{3,4},{4,3},{5,2},{6,1},{7,0},{8,15},{9,14},{10,... | collective-permute-start | bytes 208904 | tf_op jit(solution)/shard_map/ppermute | solution.py:165
  92.5 6.5 %collective-permute-start.26 = (bf16[256,128]{1,0:T(8,128)(2,1)S(1)}, bf16[256,128]{1,0:T(8,128)(2,1)S(1)}, u32[]{:S(2)}, u32[]{:S(2)}) collective-permute-start(bf16[256,128]{1,0:T(8,128)(2,1)S(1)} %get-tuple-element.45), channel_id=1, source_target_pairs={{0,1},{1,0},{2,3},{3,2},{4,5},{5,4},{6,7},{7,6},{8,9},{9,8},{10,11... | collective-permute-start | bytes 196616 | tf_op jit(solution)/shard_map/ppermute | solution.py:165
  92.6 8.5 %collective-permute-start.27 = (bf16[256,128]{1,0:T(8,128)(2,1)S(1)}, bf16[256,128]{1,0:T(8,128)(2,1)S(1)}, u32[]{:S(2)}, u32[]{:S(2)}) collective-permute-start(bf16[256,128]{1,0:T(8,128)(2,1)S(1)} %get-tuple-element.46), channel_id=1, source_target_pairs={{0,2},{1,3},{2,0},{3,1},{4,6},{5,7},{6,4},{7,5},{8,10},{9,11},{10,... | collective-permute-start | bytes 196616 | tf_op jit(solution)/shard_map/ppermute | solution.py:165
  96.1 6.2 %collective-permute-start.28 = (bf16[256,128]{1,0:T(8,128)(2,1)S(1)}, bf16[256,128]{1,0:T(8,128)(2,1)S(1)}, u32[]{:S(2)}, u32[]{:S(2)}) collective-permute-start(bf16[256,128]{1,0:T(8,128)(2,1)S(1)} %get-tuple-element.47), channel_id=1, source_target_pairs={{0,3},{1,2},{2,1},{3,0},{4,7},{5,6},{6,5},{7,4},{8,11},{9,10},{10,... | collective-permute-start | bytes 196616 | tf_op jit(solution)/shard_map/ppermute | solution.py:165
  96.1 6.2 %collective-permute-start.29 = (bf16[256,128]{1,0:T(8,128)(2,1)S(1)}, bf16[256,128]{1,0:T(8,128)(2,1)S(1)}, u32[]{:S(2)}, u32[]{:S(2)}) collective-permute-start(bf16[256,128]{1,0:T(8,128)(2,1)S(1)} %get-tuple-element.48), channel_id=1, source_target_pairs={{0,4},{1,5},{2,6},{3,7},{4,0},{5,1},{6,2},{7,3},{8,12},{9,13},{10,... | collective-permute-start | bytes 196616 | tf_op jit(solution)/shard_map/ppermute | solution.py:165
  98.6 9.9 %collective-permute-start.30 = (bf16[256,128]{1,0:T(8,128)(2,1)S(1)}, bf16[256,128]{1,0:T(8,128)(2,1)S(1)}, u32[]{:S(2)}, u32[]{:S(2)}) collective-permute-start(bf16[256,128]{1,0:T(8,128)(2,1)S(1)} %get-tuple-element.49), channel_id=1, source_target_pairs={{0,5},{1,4},{2,7},{3,6},{4,1},{5,0},{6,3},{7,2},{8,13},{9,12},{10,... | collective-permute-start | bytes 196616 | tf_op jit(solution)/shard_map/ppermute | solution.py:165
  99.0 9.6 %collective-permute-start.31 = (bf16[256,128]{1,0:T(8,128)(2,1)S(1)}, bf16[256,128]{1,0:T(8,128)(2,1)S(1)}, u32[]{:S(2)}, u32[]{:S(2)}) collective-permute-start(bf16[256,128]{1,0:T(8,128)(2,1)S(1)} %get-tuple-element.50), channel_id=1, source_target_pairs={{0,6},{1,7},{2,4},{3,5},{4,2},{5,3},{6,0},{7,1},{8,14},{9,15},{10,... | collective-permute-start | bytes 196616 | tf_op jit(solution)/shard_map/ppermute | solution.py:165
  101.1 7.5 %collective-permute-start.32 = (bf16[256,128]{1,0:T(8,128)(2,1)S(1)}, bf16[256,128]{1,0:T(8,128)(2,1)S(1)}, u32[]{:S(2)}, u32[]{:S(2)}) collective-permute-start(bf16[256,128]{1,0:T(8,128)(2,1)S(1)} %get-tuple-element.51), channel_id=1, source_target_pairs={{0,7},{1,6},{2,5},{3,4},{4,3},{5,2},{6,1},{7,0},{8,15},{9,14},{10,... | collective-permute-start | bytes 196616 | tf_op jit(solution)/shard_map/ppermute | solution.py:165
  109.2 7.9 %collective-permute-start.33 = (bf16[256,128]{1,0:T(8,128)(2,1)S(1)}, bf16[256,128]{1,0:T(8,128)(2,1)S(1)}, u32[]{:S(2)}, u32[]{:S(2)}) collective-permute-start(bf16[256,128]{1,0:T(8,128)(2,1)S(1)} %get-tuple-element.53), channel_id=1, source_target_pairs={{0,8},{8,0},{16,24},{24,16},{1,9},{9,1},{17,25},{25,17},{2,10},{10... | collective-permute-start | bytes 196616 | tf_op jit(solution)/shard_map/ppermute | solution.py:165
  110.2 6.9 %collective-permute-start.34 = (bf16[256,128]{1,0:T(8,128)(2,1)S(1)}, bf16[256,128]{1,0:T(8,128)(2,1)S(1)}, u32[]{:S(2)}, u32[]{:S(2)}) collective-permute-start(bf16[256,128]{1,0:T(8,128)(2,1)S(1)} %get-tuple-element.54), channel_id=1, source_target_pairs={{0,16},{8,24},{16,0},{24,8},{1,17},{9,25},{17,1},{25,9},{2,18},{10... | collective-permute-start | bytes 196616 | tf_op jit(solution)/shard_map/ppermute | solution.py:165
  110.9 6.2 %collective-permute-start.35 = (bf16[256,128]{1,0:T(8,128)(2,1)S(1)}, bf16[256,128]{1,0:T(8,128)(2,1)S(1)}, u32[]{:S(2)}, u32[]{:S(2)}) collective-permute-start(bf16[256,128]{1,0:T(8,128)(2,1)S(1)} %get-tuple-element.55), channel_id=1, source_target_pairs={{0,24},{8,16},{16,8},{24,0},{1,25},{9,17},{17,9},{25,1},{2,26},{10... | collective-permute-start | bytes 196616 | tf_op jit(solution)/shard_map/ppermute | solution.py:165
  (26 other events, 178.8 us)

commit v2 on v1

v2 whole, which is shorter than its diff:
```python
import functools

import jax
import jax.numpy as jnp
from jax import lax
from jax.experimental import pallas as pl
from jax.experimental.pallas import tpu as pltpu
from jax.sharding import PartitionSpec as P

FEATURES = 26
SAMPLE_BLOCKS = 2
BAG_BLOCKS = 52
CORES = 2
LIST = 2
META = 16
FIRST = 5 * 10**10
BF16 = jnp.bfloat16
F32 = jnp.float32
SMEM = pl.BlockSpec(memory_space=pltpu.SMEM)
VMEM = pl.BlockSpec(memory_space=pltpu.VMEM)


def params(mib):
    return pltpu.CompilerParams(vmem_limit_bytes=mib << 20)


def nt_dot(left, right):
    return lax.dot_general(left, right, (((1,), (1,)), ((), ())), preferred_element_type=F32)


def tn_dot(left, right):
    return lax.dot_general(left, right, (((0,), (0,)), ((), ())), preferred_element_type=F32)


def dot(left, right):
    return jnp.dot(left, right, preferred_element_type=F32)


def block(index, size):
    return pl.ds(pl.multiple_of(index * size, size), size)


def meta_rows(count):
    return -(-2 * count // 16) * 16


def id_rows(values, rows):
    row = lax.broadcasted_iota(jnp.int32, (rows, 128), 0)
    filled = jnp.full((rows, 128), -1.0, F32)
    for i, value in enumerate(values):
        filled = jnp.where(row == i, value.astype(F32), filled)
    return filled.astype(BF16)


def products_kernel(nodes, quota, size, rows_hbm, table_hbm, slot_hbm, emb_hbm, mult_hbm, *refs):
    outs = refs[:nodes]
    rows_ref, table_ref, slot_ref, emb_ref, mult_ref, sems = refs[nodes:]
    pairs = ((mult_hbm, mult_ref), (emb_hbm, emb_ref), (rows_hbm, rows_ref), (table_hbm, table_ref), (slot_hbm, slot_ref))
    copies = [pltpu.make_async_copy(src, dst, sems.at[i]) for i, (src, dst) in enumerate(pairs)]
    for copy in copies:
        copy.start()
    for copy in copies:
        copy.wait()
    node = lax.axis_index("node")
    for k in range(nodes):
        ids = []
        for i in range(quota):
            tile = (node ^ k) * quota + i
            weights = mult_ref[tile].astype(F32).astype(BF16)
            part = dot(weights, emb_ref[block(rows_ref[tile], size), :])
            outs[k][i * size : (i + 1) * size, :] = part.astype(BF16)
            ids += [table_ref[tile], slot_ref[tile]]
        outs[k][quota * size :, :] = id_rows(ids, meta_rows(quota))


def relay_kernel(nodes, quota, size, tables, relative, *refs):
    chips = tables // CORES
    parts, outs = refs[:nodes], refs[nodes : nodes + chips]
    index_ref, total, first_slot, slots = refs[nodes + chips :]
    table = lax.axis_index("table")
    for r in range(tables):
        first_slot[r] = -1
        for e in range(LIST):
            slots[r * LIST + e] = -1
            total[r * LIST + e] = jnp.zeros((size, 128), F32)
    for k in range(nodes):
        ids = parts[k][quota * size :, :].astype(F32).astype(jnp.int32)
        for i in range(quota):
            target, slot = ids[2 * i, 0], ids[2 * i + 1, 0]
            entry = target ^ table if relative else target
            known = first_slot[entry]
            which = jnp.where((known < 0) | (known == slot), 0, 1)
            first_slot[entry] = jnp.where(known < 0, slot, known)
            place = entry * LIST + which
            slots[place] = slot
            index_ref[k * quota + i] = place
            total[place] += parts[k][i * size : (i + 1) * size, :].astype(F32)
    for r in range(tables):
        out, base = outs[r // CORES], r % CORES * (LIST * size + META)
        for e in range(LIST):
            out[base + e * size : base + (e + 1) * size, :] = total[r * LIST + e].astype(BF16)
        base += LIST * size
        out[base : base + META, :] = id_rows([slots[r * LIST + e] for e in range(LIST)], META)


def pool_kernel(tables, size, *refs):
    parts = refs[:tables]
    dense_ref, v_ref, cot_ref, first_ref, hidden_ref, scaled_ref, slot_ref, total = refs[tables:]
    for b in range(BAG_BLOCKS):
        total[b] = jnp.zeros((size, 128), F32)
    for r in range(tables):
        part, base = parts[r], r % CORES * (LIST * size + META)
        ids = part[base + LIST * size : base + LIST * size + META, :].astype(F32).astype(jnp.int32)
        for e in range(LIST):
            slot_ref[r * LIST + e] = ids[e, 0]

            @pl.when(ids[e, 0] >= 0)
            def _(slot=ids[e, 0], part=part, begin=base + e * size):
                total[slot] += part[begin : begin + size, :].astype(F32)

    first_ref[:, :128] = dense_ref[...]
    for f in range(FEATURES):
        for s in range(SAMPLE_BLOCKS):
            columns = slice((f + 1) * 128, (f + 2) * 128)
            first_ref[s * size : (s + 1) * size, columns] = total[f * SAMPLE_BLOCKS + s].astype(BF16)
    hidden_ref[...] = dot(first_ref[...], v_ref[...]).astype(BF16)
    for f in range(FEATURES + 1):
        columns = slice(f * 128, (f + 1) * 128)
        scaled_ref[:, columns] = (cot_ref[:, columns].astype(F32) * first_ref[:, columns].astype(F32)).astype(BF16)


def owner_kernel(tables, size, slot_ref, hidden_ref, scaled_ref, v_ref, u_ref, bias_ref, cot_ref, *refs):
    outs, dhidden = refs[: tables // CORES], refs[tables // CORES]
    dhidden[...] = nt_dot(scaled_ref[...], u_ref[...]).astype(BF16)
    for r in range(tables):
        for e in range(LIST):
            slot = slot_ref[r * LIST + e]

            @pl.when(slot >= 0)
            def _(slot=slot, out=outs[r // CORES], begin=(r % CORES * LIST + e) * size):
                columns = block(slot // SAMPLE_BLOCKS + 1, 128)
                samples = block(slot % SAMPLE_BLOCKS, size)
                scale = dot(hidden_ref[samples, :], u_ref[:, columns]) + bias_ref[:, columns]
                grad = cot_ref[samples, columns].astype(F32) * (scale + 1.0)
                grad = grad + nt_dot(dhidden[samples, :], v_ref[columns, :])
                out[begin : begin + size, :] = grad.astype(BF16)


def cross_kernel(first_ref, hidden_ref, u_ref, bias_ref, out_ref):
    width = first_ref.shape[1]
    step = 256
    for start in range(0, width, step):
        columns = slice(start, min(start + step, width))
        scale = dot(hidden_ref[...], u_ref[:, columns]) + bias_ref[:, columns]
        out_ref[:, columns] = (first_ref[:, columns].astype(F32) * (scale + 1.0)).astype(BF16)


def return_kernel(nodes, quota, size, tables, index_ref, *refs):
    parts, outs, staged = refs[:tables], refs[tables : tables + nodes], refs[-1]
    for r in range(tables):
        for e in range(LIST):
            begin = (r % CORES * LIST + e) * size
            staged[r * LIST + e] = parts[r][begin : begin + size, :]
    for k in range(nodes):
        for i in range(quota):
            outs[k][i * size : (i + 1) * size, :] = staged[index_ref[k * quota + i]]


def rows_kernel(nodes, quota, size, rows_ref, mult_ref, *refs):
    parts, out_ref = refs[:nodes], refs[nodes]
    node = lax.axis_index("node")
    out_ref[...] = jnp.zeros(out_ref.shape, F32)
    for k in range(nodes):
        for i in range(quota):
            tile = (node ^ k) * quota + i
            weights = mult_ref[tile].astype(F32).astype(BF16)
            rows = block(rows_ref[tile], size)
            out_ref[rows, :] += tn_dot(weights, parts[k][i * size : (i + 1) * size, :])


def xor_permute(value, axis, k):
    size = lax.axis_size(axis)
    return lax.ppermute(value, axis, [(i, i ^ k) for i in range(size)])


def exchange_chips(parts):
    return [parts[0]] + [xor_permute(parts[k], "table", CORES * k) for k in range(1, len(parts))]


def exchange_cores(parts):
    return [item for part in parts for item in (part, sibling(part))]


def exchange_whole(parts):
    height = parts[0].shape[0] // CORES
    stacked = jnp.stack(parts).reshape(len(parts) * CORES, height, parts[0].shape[1])
    moved = lax.all_to_all(stacked, "table", split_axis=0, concat_axis=0, tiled=True)
    moved = moved.reshape(len(parts), CORES * height, parts[0].shape[1])
    return [moved[r // CORES] for r in range(len(parts) * CORES)]


def permute(value, target):
    nodes, tables = lax.axis_size("node"), lax.axis_size("table")
    pairs = []
    for n in range(nodes):
        for t in range(tables):
            m, s = target(n, t)
            pairs.append((n * tables + t, m * tables + s))
    return lax.ppermute(value, ("node", "table"), pairs)


def near(value):
    return permute(value, lambda n, t: (n ^ (1 + t % 2), t))


def far(value):
    return permute(value, lambda n, t: (n ^ (2 - t % 2), t))


def sibling(value):
    return permute(value, lambda n, t: (n, t ^ 1))


def half_of(shard):
    half = shard.shape[0] // 2
    core = lax.axis_index("table") % 2
    return lax.dynamic_slice(shard, (core * half, 0), (half, shard.shape[1]))


def assemble(shard, first, first_other, second, second_other):
    node = lax.axis_index("node")
    core = lax.axis_index("table") % 2
    rows, width = shard.shape
    half = rows // 2
    whole = jnp.zeros((rows * lax.axis_size("node"), width), shard.dtype)
    for piece, row in (
        (shard, node * rows),
        (first, (node ^ (1 + core)) * rows),
        (first_other, (node ^ (2 - core)) * rows),
        (second, (node ^ 3) * rows + core * half),
        (second_other, (node ^ 3) * rows + (1 - core) * half),
    ):
        whole = lax.dynamic_update_slice(whole, piece, (row, 0))
    return whole


def body(emb_rows, tile_mult, tile_rows, tile_table, tile_slot, dense, cross_v, cross_u, cross_bias, cotangent):
    nodes, tables = lax.axis_size("node"), lax.axis_size("table")
    tiles, size = tile_mult.shape[0], tile_mult.shape[1]
    quota = tiles // nodes
    samples, cross = cotangent.shape
    rank = cross_v.shape[1]
    relative = tables <= 8
    bias = cross_bias.reshape(1, cross)

    part = jax.ShapeDtypeStruct((quota * size + meta_rows(quota), 128), BF16)
    hbm = pl.BlockSpec(memory_space=pltpu.HBM)
    parts = pl.pallas_call(
        functools.partial(products_kernel, nodes, quota, size),
        out_shape=[part] * nodes,
        in_specs=[hbm] * 5,
        out_specs=[VMEM] * nodes,
        scratch_shapes=[
            pltpu.SMEM((tiles,), jnp.int32),
            pltpu.SMEM((tiles,), jnp.int32),
            pltpu.SMEM((tiles,), jnp.int32),
            pltpu.VMEM(emb_rows.shape, BF16),
            pltpu.VMEM(tile_mult.shape, jnp.int32),
            pltpu.SemaphoreType.DMA((5,)),
        ],
        compiler_params=params(60),
        name="products",
    )(tile_rows, tile_table, tile_slot, emb_rows, tile_mult)
    first_v = near(cross_v)
    parts = [parts[0]] + [xor_permute(parts[k], "node", k) for k in range(1, nodes)]
    late_u, parts[1] = lax.optimization_barrier((cross_u, parts[1]))
    first_u = near(late_u)
    second_v = far(half_of(first_v))
    second_u = far(half_of(first_u))

    chips = tables // CORES
    listed = jax.ShapeDtypeStruct((CORES * (LIST * size + META), 128), BF16)
    *lists, index = pl.pallas_call(
        functools.partial(relay_kernel, nodes, quota, size, tables, relative),
        out_shape=[listed] * chips + [jax.ShapeDtypeStruct((tiles,), jnp.int32)],
        in_specs=[VMEM] * nodes,
        out_specs=[VMEM] * chips + [SMEM],
        scratch_shapes=[
            pltpu.VMEM((tables * LIST, size, 128), F32),
            pltpu.SMEM((tables,), jnp.int32),
            pltpu.SMEM((tables * LIST,), jnp.int32),
        ],
        compiler_params=params(32),
        cost_estimate=pl.CostEstimate(flops=FIRST, bytes_accessed=0, transcendentals=0),
        name="relay",
    )(*parts)
    if relative:
        first_v, second_v, *arrived = lax.optimization_barrier((first_v, second_v, *exchange_chips(lists)))
        arrived = exchange_cores(arrived)
    else:
        arrived = exchange_whole(lists)
    full_v = assemble(cross_v, first_v, sibling(first_v), second_v, sibling(second_v))

    grad = jax.ShapeDtypeStruct((CORES * LIST * size, 128), BF16)
    first, hidden, scaled, slots = pl.pallas_call(
        functools.partial(pool_kernel, tables, size),
        out_shape=[
            jax.ShapeDtypeStruct((samples, cross), BF16),
            jax.ShapeDtypeStruct((samples, rank), BF16),
            jax.ShapeDtypeStruct((samples, cross), BF16),
            jax.ShapeDtypeStruct((tables * LIST,), jnp.int32),
        ],
        in_specs=[VMEM] * (tables + 3),
        out_specs=[VMEM] * 3 + [SMEM],
        scratch_shapes=[pltpu.VMEM((BAG_BLOCKS, size, 128), F32)],
        compiler_params=params(24),
        name="pool",
    )(*arrived, dense, full_v, cotangent)

    if relative:
        second_u, hidden = lax.optimization_barrier((second_u, hidden))
    full_u = assemble(cross_u, first_u, sibling(first_u), second_u, sibling(second_u))

    grads = pl.pallas_call(
        functools.partial(owner_kernel, tables, size),
        out_shape=[grad] * chips,
        in_specs=[SMEM] + [VMEM] * 6,
        out_specs=[VMEM] * chips,
        scratch_shapes=[pltpu.VMEM((samples, rank), BF16)],
        compiler_params=params(24),
        name="owner",
    )(slots, hidden, scaled, full_v, full_u, bias, cotangent)
    cross_out = pl.pallas_call(
        cross_kernel,
        out_shape=jax.ShapeDtypeStruct((samples, cross), BF16),
        in_specs=[VMEM] * 4,
        out_specs=VMEM,
        compiler_params=params(32),
        cost_estimate=pl.CostEstimate(
            flops=2 * samples * rank * cross, bytes_accessed=4 * samples * cross + 2 * rank * cross, transcendentals=0
        ),
        name="cross",
    )(first, hidden, full_u, bias)

    if relative:
        returned = exchange_chips(grads)
        returned[-1], cross_out = lax.optimization_barrier((returned[-1], cross_out))
        returned = exchange_cores(returned)
    else:
        returned = exchange_whole(grads)

    back = jax.ShapeDtypeStruct((quota * size, 128), BF16)
    backs = pl.pallas_call(
        functools.partial(return_kernel, nodes, quota, size, tables),
        out_shape=[back] * nodes,
        in_specs=[SMEM] + [VMEM] * tables,
        out_specs=[VMEM] * nodes,
        scratch_shapes=[pltpu.VMEM((tables * LIST, size, 128), BF16)],
        compiler_params=params(32),
        name="back",
    )(index, *returned)
    backs = [backs[0]] + [xor_permute(backs[k], "node", k) for k in range(1, nodes)]

    emb_grad = pl.pallas_call(
        functools.partial(rows_kernel, nodes, quota, size),
        out_shape=jax.ShapeDtypeStruct(emb_rows.shape, F32),
        in_specs=[SMEM] + [VMEM] * (nodes + 1),
        out_specs=VMEM,
        compiler_params=params(16),
        name="rows",
    )(tile_rows, tile_mult, *backs)
    return cross_out, emb_grad


def solution(mesh):
    both = ("node", "table")
    in_specs = (
        P(both, None),
        P(both, None, None),
        P(both),
        P(both),
        P(both),
        P(both, None),
        P("node", None),
        P("node", None),
        P(),
        P(both, None),
    )
    out_specs = (P(both, None), P(both, None))
    return jax.shard_map(body, mesh=mesh, in_specs=in_specs, out_specs=out_specs, check_vma=False)
```

time: 120 us -> 76.3 us (0.64)
  local copies, waits for them, and re-layouts: 21.4 us -> 2.75 us
  starting transfers between devices: 36 us -> 24 us
  waiting for transfers between devices: 45.2 us -> 34.3 us
    ppermute x36 -> x12, waiting for transfers between devices: 45.2 us -> 12.6 us  [xor_permute(): return lax.ppermute(value, axis, [(i, i ^ k) for i in range(size)])]
    ppermute x0 -> x16, waiting for transfers between devices: none -> 21.6 us  [permute(): return lax.ppermute(value, ('node', 'table'), pairs)]
    ppermute x36 -> x12, starting transfers between devices: 36 us -> 17.1 us  [xor_permute(): return lax.ppermute(value, axis, [(i, i ^ k) for i in range(size)])]
    unnamed x44 -> x14, local copies, waits for them, and re-layouts: 7.83 us -> 0.82 us
    ppermute x0 -> x16, starting transfers between devices: none -> 6.96 us  [permute(): return lax.ppermute(value, ('node', 'table'), pairs)]
    dynamic_update_slice x18 -> x10, local copies, waits for them, and re-layouts: 4.97 us -> 0.67 us  [assemble(): whole = lax.dynamic_update_slice(whole, piece, (row, 0))]
    slice x4 -> x0, local copies, waits for them, and re-layouts: 3.8 us -> none  [the longest x2 1.9 us: gathered(): far_y = xor_permute(by_x[cut:], 'node', 2)]
    dynamic_slice x2, local copies, waits for them, and re-layouts: 3.63 us -> 0.06 us  [half_of(): return lax.dynamic_slice(shard, (core * half, 0), (half, shard.shape[1]))]
  transfers between devices with their start and end apart: 36 -> 28, of which waited for: 13 -> 16; matrix products, arithmetic and copies ran while one was open for 10% -> 2% of each run, Pallas kernels for 5% -> 8%
where the time goes in v2:
time: 76.3 us; the launch traced here: 75.9 us
  waiting for transfers between devices  34.3 us (45%)
  starting transfers between devices  24 us (31%)
  Pallas kernels  13.9 us (18%)
  local copies, waits for them, and re-layouts  2.75 us (4%)
  between operations  0.94 us (1%)
    ppermute x16, waiting for transfers between devices, permute(): return lax.ppermute(value, ('node', 'table'), pairs)  21.6 us
    ppermute x12, starting transfers between devices, xor_permute(): return lax.ppermute(value, axis, [(i, i ^ k) for i in range(size)])  17.1 us
    ppermute x12, waiting for transfers between devices, xor_permute(): return lax.ppermute(value, axis, [(i, i ^ k) for i in range(size)])  12.6 us
    ppermute x16, starting transfers between devices, permute(): return lax.ppermute(value, ('node', 'table'), pairs)  6.96 us
    pallas_call x1, Pallas kernels, body(): pl.pallas_call(functools.partial(owner_kernel, tables, size), out_shape=[...  3.78 us
    pallas_call x1, Pallas kernels, body(): pl.pallas_call(functools.partial(pool_kernel, tables, size), out_shape=[j...  2.72 us
    pallas_call x1, Pallas kernels, body(): pl.pallas_call(cross_kernel, out_shape=jax.ShapeDtypeStruct((samples, cro...  2.41 us
    pallas_call x1, Pallas kernels, body(): pl.pallas_call(functools.partial(products_kernel, nodes, quota, size), ou...  2.08 us
  transfers between devices with their start and end apart: 28, of which 16 were waited for; matrix products, arithmetic and copies ran while one was open for 2% of the time, Pallas kernels for 8%

profile of v2, /device:TPU:0, one launch (start us, length us, event | category | flops | bytes accessed | tf_op | source)
XLA Modules:
  0.0 75.9 jit_solution(14282270547136663409)
XLA Ops:
  0.6 2.1 %products.1 = (bf16[272,128]{1,0:T(8,128)(2,1)}, bf16[272,128]{1,0:T(8,128)(2,1)}, bf16[272,128]{1,0:T(8,128)(2,1)}, bf16[272,128]{1,0:T(8,128)(2,1)}) custom-call(s32[8]{0:T(128)} %rows_ref.1, s32[8]{0:T(128)} %table_hbm.1, s32[8]{0:T(128)} %slot_hbm.1, bf16[512,128]{1,0:T(8,128)(2,1)} %emb_hbm.1, s32[8,128,128]{2,1,0:T(8,128)} %mult_ref.1), custom_call_target="tpu_custom_call" | custom-call | tf_op jit(solution)/shard_map/products/pallas_call | solution.py:258
  2.7 3.0 %collective-permute-start.2 = (bf16[272,128]{1,0:T(8,128)(2,1)}, bf16[272,128]{1,0:T(8,128)(2,1)S(1)}, u32[]{:S(2)}, u32[]{:S(2)}) collective-permute-start(bf16[272,128]{1,0:T(8,128)(2,1)} %get-tuple-element.36), channel_id=1, source_target_pairs={{0,8},{8,0},{16,24},{24,16},{1,9},{9,1},{17,25},{25,17},{2,10},{10... | collective-permute-start | bytes 208904 | tf_op jit(solution)/shard_map/ppermute | solution.py:183
  5.7 1.5 %collective-permute-start.3 = (bf16[272,128]{1,0:T(8,128)(2,1)}, bf16[272,128]{1,0:T(8,128)(2,1)S(1)}, u32[]{:S(2)}, u32[]{:S(2)}) collective-permute-start(bf16[272,128]{1,0:T(8,128)(2,1)} %get-tuple-element.38), channel_id=1, source_target_pairs={{0,16},{8,24},{16,0},{24,8},{1,17},{9,25},{17,1},{25,9},{2,18},{10... | collective-permute-start | bytes 208904 | tf_op jit(solution)/shard_map/ppermute | solution.py:183
  7.3 1.9 %collective-permute-start = (bf16[864,512]{1,0:T(8,128)(2,1)}, bf16[864,512]{1,0:T(8,128)(2,1)S(1)}, u32[]{:S(2)}, u32[]{:S(2)}) collective-permute-start(bf16[864,512]{1,0:T(8,128)(2,1)} %param.16), channel_id=1, source_target_pairs={{0,8},{1,17},{2,10},{3,19},{4,12},{5,21},{6,14},{7,23},{8,0},{9,25... | collective-permute-start | bytes 2654216 | tf_op jit(solution)/shard_map/ppermute | solution.py:209
  9.2 0.7 reshape.7.bias_ref
  10.6 0.8 %copy-done.5 = bf16[864,512]{1,0:T(8,128)(2,1)S(1)} copy-done((bf16[864,512]{1,0:T(8,128)(2,1)S(1)}, bf16[864,512]{1,0:T(8,128)(2,1)}, u32[]{:S(2)}) %copy-start.5) | copy-done | bytes 884760
  11.7 1.0 %collective-permute-done.4.refs_3_ = bf16[272,128]{1,0:T(8,128)(2,1)S(1)} collective-permute-done((bf16[272,128]{1,0:T(8,128)(2,1)}, bf16[272,128]{1,0:T(8,128)(2,1)S(1)}, u32[]{:S(2)}, u32[]{:S(2)}) %collective-permute-start.4) | collective-permute-done | bytes 69664 | tf_op jit(solution)/shard_map/ppermute | solution.py:183
  12.8 0.8 relay.1
  13.5 1.6 %collective-permute-start.5 = (bf16[544,128]{1,0:T(8,128)(2,1)S(1)}, bf16[544,128]{1,0:T(8,128)(2,1)S(1)}, u32[]{:S(2)}, u32[]{:S(2)}) collective-permute-start(bf16[544,128]{1,0:T(8,128)(2,1)S(1)} %get-tuple-element.41), channel_id=1, source_target_pairs={{0,2},{1,3},{2,0},{3,1},{4,6},{5,7},{6,4},{7,5},{8,10},{9,11},{10,... | collective-permute-start | bytes 417800 | tf_op jit(solution)/shard_map/ppermute | solution.py:183
  15.2 2.6 %collective-permute-start.6 = (bf16[544,128]{1,0:T(8,128)(2,1)S(1)}, bf16[544,128]{1,0:T(8,128)(2,1)S(1)}, u32[]{:S(2)}, u32[]{:S(2)}) collective-permute-start(bf16[544,128]{1,0:T(8,128)(2,1)S(1)} %get-tuple-element.42), channel_id=1, source_target_pairs={{0,4},{1,5},{2,6},{3,7},{4,0},{5,1},{6,2},{7,3},{8,12},{9,13},{10,... | collective-permute-start | bytes 417800 | tf_op jit(solution)/shard_map/ppermute | solution.py:183
  18.0 3.2 %collective-permute-done = bf16[864,512]{1,0:T(8,128)(2,1)S(1)} collective-permute-done((bf16[864,512]{1,0:T(8,128)(2,1)}, bf16[864,512]{1,0:T(8,128)(2,1)S(1)}, u32[]{:S(2)}, u32[]{:S(2)}) %collective-permute-start) | collective-permute-done | bytes 884768 | tf_op jit(solution)/shard_map/ppermute | solution.py:209
  21.2 1.6 %collective-permute-start.1 = (bf16[432,512]{1,0:T(8,128)(2,1)S(1)}, bf16[432,512]{1,0:T(8,128)(2,1)S(1)}, u32[]{:S(2)}, u32[]{:S(2)}) collective-permute-start(bf16[432,512]{1,0:T(8,128)(2,1)S(1)} %constant_dynamic-slice_fusion.1), channel_id=1, source_target_pairs={{0,16},{1,9},{2,18},{3,11},{4,20},{5,13},{6,22},{7,15},{8,24},{9,1... | collective-permute-start | bytes 1327112 | tf_op jit(solution)/shard_map/ppermute | solution.py:209
  22.8 12.6 %collective-permute-done.14 = bf16[128,3456]{1,0:T(8,128)(2,1)S(1)} collective-permute-done((bf16[128,3456]{1,0:T(8,128)(2,1)S(1)}, bf16[128,3456]{1,0:T(8,128)(2,1)S(1)}, u32[]{:S(2)}, u32[]{:S(2)}) %collective-permute-start.14) | collective-permute-done | bytes 884768 | tf_op jit(solution)/shard_map/ppermute | solution.py:209
  35.5 1.6 %collective-permute-start.15 = (bf16[64,3456]{1,0:T(8,128)(2,1)S(1)}, bf16[64,3456]{1,0:T(8,128)(2,1)S(1)}, u32[]{:S(2)}, u32[]{:S(2)}) collective-permute-start(bf16[64,3456]{1,0:T(8,128)(2,1)S(1)} %constant_dynamic-slice_fusion), channel_id=1, source_target_pairs={{0,16},{1,9},{2,18},{3,11},{4,20},{5,13},{6,22},{7,15},{8,24},{9,1... | collective-permute-start | bytes 1327112 | tf_op jit(solution)/shard_map/ppermute | solution.py:209
  38.6 1.0 %collective-permute-done.12 = bf16[864,512]{1,0:T(8,128)(2,1)S(1)} collective-permute-done((bf16[864,512]{1,0:T(8,128)(2,1)S(1)}, bf16[864,512]{1,0:T(8,128)(2,1)S(1)}, u32[]{:S(2)}, u32[]{:S(2)}) %collective-permute-start.12) | collective-permute-done | bytes 884768 | tf_op jit(solution)/shard_map/ppermute | solution.py:209
  39.8 0.8 %collective-permute-done.13 = bf16[432,512]{1,0:T(8,128)(2,1)S(1)} collective-permute-done((bf16[432,512]{1,0:T(8,128)(2,1)S(1)}, bf16[432,512]{1,0:T(8,128)(2,1)S(1)}, u32[]{:S(2)}, u32[]{:S(2)}) %collective-permute-start.13) | collective-permute-done | bytes 442400 | tf_op jit(solution)/shard_map/ppermute | solution.py:209
  40.9 1.0 %collective-permute-done.11.refs_7_ = bf16[544,128]{1,0:T(8,128)(2,1)S(1)} collective-permute-done((bf16[544,128]{1,0:T(8,128)(2,1)S(1)}, bf16[544,128]{1,0:T(8,128)(2,1)S(1)}, u32[]{:S(2)}, u32[]{:S(2)}) %collective-permute-start.11) | collective-permute-done | bytes 139296 | tf_op jit(solution)/shard_map/ppermute | solution.py:209
  41.9 2.7 %pool.1 = (bf16[256,3456]{1,0:T(8,128)(2,1)S(1)}, bf16[256,512]{1,0:T(8,128)(2,1)S(1)}, bf16[256,3456]{1,0:T(8,128)(2,1)S(1)}, s32[16]{0:T(128)S(1)}) custom-call(bf16[544,128]{1,0:T(8,128)(2,1)S(1)} %get-tuple-element.44.refs_0_, bf16[544,128]{1,0:T(8,128)(2,1)S(1)} %collective-permute-done.8.refs_1_, bf16[544,128]{1,0:T(8,128)(2,1)S(1)} %collective-permute-done.5.refs_2_, ...), custom_call_target="tpu_custom_call" | custom-call | tf_op jit(solution)/shard_map/pool/pallas_call | solution.py:305
  44.9 1.6 %collective-permute-done.17 = bf16[64,3456]{1,0:T(8,128)(2,1)S(1)} collective-permute-done((bf16[64,3456]{1,0:T(8,128)(2,1)S(1)}, bf16[64,3456]{1,0:T(8,128)(2,1)S(1)}, u32[]{:S(2)}, u32[]{:S(2)}) %collective-permute-start.17) | collective-permute-done | bytes 442400 | tf_op jit(solution)/shard_map/ppermute | solution.py:209
  46.6 3.8 %owner.1 = (bf16[512,128]{1,0:T(8,128)(2,1)S(1)}, bf16[512,128]{1,0:T(8,128)(2,1)S(1)}, bf16[512,128]{1,0:T(8,128)(2,1)S(1)}, bf16[512,128]{1,0:T(8,128)(2,1)S(1)}) custom-call(s32[16]{0:T(128)S(1)} %get-tuple-element.50.slot_ref, bf16[256,512]{1,0:T(8,128)(2,1)S(1)} %get-tuple-element.53.hidden_ref, bf16[256,3456]{1,0:T(8,128)(2,1)S(1)} %get-tuple-element.54.scaled_ref, ...), custom_call_target="tpu_custom_call" | custom-call | tf_op jit(solution)/shard_map/owner/pallas_call | solution.py:324
  50.4 3.9 %collective-permute-start.18 = (bf16[512,128]{1,0:T(8,128)(2,1)S(1)}, bf16[512,128]{1,0:T(8,128)(2,1)S(1)}, u32[]{:S(2)}, u32[]{:S(2)}) collective-permute-start(bf16[512,128]{1,0:T(8,128)(2,1)S(1)} %get-tuple-element.56), channel_id=1, source_target_pairs={{0,6},{1,7},{2,4},{3,5},{4,2},{5,3},{6,0},{7,1},{8,14},{9,15},{10,... | collective-permute-start | bytes 393224 | tf_op jit(solution)/shard_map/ppermute | solution.py:183
  54.9 2.4 %cross.1 = bf16[256,3456]{1,0:T(8,128)(2,1)} custom-call(bf16[256,3456]{1,0:T(8,128)(2,1)S(1)} %get-tuple-element.57.first_ref, bf16[256,512]{1,0:T(8,128)(2,1)S(1)} %get-tuple-element.53.hidden_ref, bf16[512,3456]{1,0:T(8,128)(2,1)S(1)} %constant_dynamic-update-slice_fusion.u_ref, f32[1,3456]{1,0:T(1,128)S(1)} %reshape.7.bias_ref), custom_call_target="tpu_custom_call" | custom-call | flops 905969664 | bytes 7077888 | tf_op jit(solution)/shard_map/cross/pallas_call | solution.py:333
  57.3 1.3 %collective-permute-done.18.refs_6_ = bf16[512,128]{1,0:T(8,128)(2,1)S(1)} collective-permute-done((bf16[512,128]{1,0:T(8,128)(2,1)S(1)}, bf16[512,128]{1,0:T(8,128)(2,1)S(1)}, u32[]{:S(2)}, u32[]{:S(2)}) %collective-permute-start.18) | collective-permute-done | bytes 131104 | tf_op jit(solution)/shard_map/ppermute | solution.py:183
  58.6 3.9 %collective-permute-done.20.refs_2_ = bf16[512,128]{1,0:T(8,128)(2,1)S(1)} collective-permute-done((bf16[512,128]{1,0:T(8,128)(2,1)S(1)}, bf16[512,128]{1,0:T(8,128)(2,1)S(1)}, u32[]{:S(2)}, u32[]{:S(2)}) %collective-permute-start.20) | collective-permute-done | bytes 131104 | tf_op jit(solution)/shard_map/ppermute | solution.py:183
  62.5 2.5 %collective-permute-done.22.refs_4_ = bf16[512,128]{1,0:T(8,128)(2,1)S(1)} collective-permute-done((bf16[512,128]{1,0:T(8,128)(2,1)S(1)}, bf16[512,128]{1,0:T(8,128)(2,1)S(1)}, u32[]{:S(2)}, u32[]{:S(2)}) %collective-permute-start.22) | collective-permute-done | bytes 131104 | tf_op jit(solution)/shard_map/ppermute | solution.py:183
  65.0 1.3 %collective-permute-done.23.refs_5_ = bf16[512,128]{1,0:T(8,128)(2,1)S(1)} collective-permute-done((bf16[512,128]{1,0:T(8,128)(2,1)S(1)}, bf16[512,128]{1,0:T(8,128)(2,1)S(1)}, u32[]{:S(2)}, u32[]{:S(2)}) %collective-permute-start.23) | collective-permute-done | bytes 131104 | tf_op jit(solution)/shard_map/ppermute | solution.py:209
  66.9 1.6 %collective-permute-start.25 = (bf16[256,128]{1,0:T(8,128)(2,1)S(1)}, bf16[256,128]{1,0:T(8,128)(2,1)S(1)}, u32[]{:S(2)}, u32[]{:S(2)}) collective-permute-start(bf16[256,128]{1,0:T(8,128)(2,1)S(1)} %get-tuple-element.65), channel_id=1, source_target_pairs={{0,8},{8,0},{16,24},{24,16},{1,9},{9,1},{17,25},{25,17},{2,10},{10... | collective-permute-start | bytes 196616 | tf_op jit(solution)/shard_map/ppermute | solution.py:183
  69.2 1.3 %collective-permute-start.27 = (bf16[256,128]{1,0:T(8,128)(2,1)S(1)}, bf16[256,128]{1,0:T(8,128)(2,1)S(1)}, u32[]{:S(2)}, u32[]{:S(2)}) collective-permute-start(bf16[256,128]{1,0:T(8,128)(2,1)S(1)} %get-tuple-element.67), channel_id=1, source_target_pairs={{0,24},{8,16},{16,8},{24,0},{1,25},{9,17},{17,9},{25,1},{2,26},{10... | collective-permute-start | bytes 196616 | tf_op jit(solution)/shard_map/ppermute | solution.py:183
  70.5 0.8 %collective-permute-done.25.refs_1_ = bf16[256,128]{1,0:T(8,128)(2,1)S(1)} collective-permute-done((bf16[256,128]{1,0:T(8,128)(2,1)S(1)}, bf16[256,128]{1,0:T(8,128)(2,1)S(1)}, u32[]{:S(2)}, u32[]{:S(2)}) %collective-permute-start.25) | collective-permute-done | bytes 65568 | tf_op jit(solution)/shard_map/ppermute | solution.py:183
  71.3 2.3 %collective-permute-done.26.refs_2_ = bf16[256,128]{1,0:T(8,128)(2,1)S(1)} collective-permute-done((bf16[256,128]{1,0:T(8,128)(2,1)S(1)}, bf16[256,128]{1,0:T(8,128)(2,1)S(1)}, u32[]{:S(2)}, u32[]{:S(2)}) %collective-permute-start.26) | collective-permute-done | bytes 65568 | tf_op jit(solution)/shard_map/ppermute | solution.py:183
  73.5 0.8 %collective-permute-done.27.refs_3_ = bf16[256,128]{1,0:T(8,128)(2,1)S(1)} collective-permute-done((bf16[256,128]{1,0:T(8,128)(2,1)S(1)}, bf16[256,128]{1,0:T(8,128)(2,1)S(1)}, u32[]{:S(2)}, u32[]{:S(2)}) %collective-permute-start.27) | collective-permute-done | bytes 65568 | tf_op jit(solution)/shard_map/ppermute | solution.py:183
  74.4 1.5 %rows.1 = f32[512,128]{1,0:T(8,128)} custom-call(s32[8]{0:T(128)S(1)} %copy-done.3, s32[8,128,128]{2,1,0:T(8,128)S(1)} %copy-done.1, bf16[256,128]{1,0:T(8,128)(2,1)S(1)} %get-tuple-element.64.refs_0_, bf16[256,128]{1,0:T(8,128)(2,1)S(1)} %collective-permute-done.25.refs_1_, bf16[256,128]{1,0:T(8,128)(2,1)S(1)} %collective-permute-done.26.refs_2_, ...), custom_call_target="tpu_custom_call" | custom-call | tf_op jit(solution)/shard_map/rows/pallas_call | solution.py:364
  (60 shorter events, 5.4 us)
Async XLA Ops:
  0.6 9.6 %copy-start.6 = (bf16[128,3456]{1,0:T(8,128)(2,1)S(1)}, bf16[128,3456]{1,0:T(8,128)(2,1)}, u32[]{:S(2)}) copy-start(bf16[128,3456]{1,0:T(8,128)(2,1)} %param.17) | copy-start | bytes 2654212
  2.7 8.8 %collective-permute-start.2 = (bf16[272,128]{1,0:T(8,128)(2,1)}, bf16[272,128]{1,0:T(8,128)(2,1)S(1)}, u32[]{:S(2)}, u32[]{:S(2)}) collective-permute-start(bf16[272,128]{1,0:T(8,128)(2,1)} %get-tuple-element.36), channel_id=1, source_target_pairs={{0,8},{8,0},{16,24},{24,16},{1,9},{9,1},{17,25},{25,17},{2,10},{10... | collective-permute-start | bytes 208904 | tf_op jit(solution)/shard_map/ppermute | solution.py:183
  5.7 6.0 %collective-permute-start.3 = (bf16[272,128]{1,0:T(8,128)(2,1)}, bf16[272,128]{1,0:T(8,128)(2,1)S(1)}, u32[]{:S(2)}, u32[]{:S(2)}) collective-permute-start(bf16[272,128]{1,0:T(8,128)(2,1)} %get-tuple-element.38), channel_id=1, source_target_pairs={{0,16},{8,24},{16,0},{24,8},{1,17},{9,25},{17,1},{25,9},{2,18},{10... | collective-permute-start | bytes 208904 | tf_op jit(solution)/shard_map/ppermute | solution.py:183
  7.3 5.5 %collective-permute-start.4 = (bf16[272,128]{1,0:T(8,128)(2,1)}, bf16[272,128]{1,0:T(8,128)(2,1)S(1)}, u32[]{:S(2)}, u32[]{:S(2)}) collective-permute-start(bf16[272,128]{1,0:T(8,128)(2,1)} %get-tuple-element.39), channel_id=1, source_target_pairs={{0,24},{8,16},{16,8},{24,0},{1,25},{9,17},{17,9},{25,1},{2,26},{10... | collective-permute-start | bytes 208904 | tf_op jit(solution)/shard_map/ppermute | solution.py:183
  7.3 13.9 %collective-permute-start = (bf16[864,512]{1,0:T(8,128)(2,1)}, bf16[864,512]{1,0:T(8,128)(2,1)S(1)}, u32[]{:S(2)}, u32[]{:S(2)}) collective-permute-start(bf16[864,512]{1,0:T(8,128)(2,1)} %param.16), channel_id=1, source_target_pairs={{0,8},{1,17},{2,10},{3,19},{4,12},{5,21},{6,14},{7,23},{8,0},{9,25... | collective-permute-start | bytes 2654216 | tf_op jit(solution)/shard_map/ppermute | solution.py:209
  11.5 23.9 %collective-permute-start.14 = (bf16[128,3456]{1,0:T(8,128)(2,1)S(1)}, bf16[128,3456]{1,0:T(8,128)(2,1)S(1)}, u32[]{:S(2)}, u32[]{:S(2)}) collective-permute-start(bf16[128,3456]{1,0:T(8,128)(2,1)S(1)} %copy-done.6), channel_id=1, source_target_pairs={{0,8},{1,17},{2,10},{3,19},{4,12},{5,21},{6,14},{7,23},{8,0},{9,25... | collective-permute-start | bytes 2654216 | tf_op jit(solution)/shard_map/ppermute | solution.py:209
  13.5 21.9 %collective-permute-start.5 = (bf16[544,128]{1,0:T(8,128)(2,1)S(1)}, bf16[544,128]{1,0:T(8,128)(2,1)S(1)}, u32[]{:S(2)}, u32[]{:S(2)}) collective-permute-start(bf16[544,128]{1,0:T(8,128)(2,1)S(1)} %get-tuple-element.41), channel_id=1, source_target_pairs={{0,2},{1,3},{2,0},{3,1},{4,6},{5,7},{6,4},{7,5},{8,10},{9,11},{10,... | collective-permute-start | bytes 417800 | tf_op jit(solution)/shard_map/ppermute | solution.py:183
  15.2 21.9 %collective-permute-start.6 = (bf16[544,128]{1,0:T(8,128)(2,1)S(1)}, bf16[544,128]{1,0:T(8,128)(2,1)S(1)}, u32[]{:S(2)}, u32[]{:S(2)}) collective-permute-start(bf16[544,128]{1,0:T(8,128)(2,1)S(1)} %get-tuple-element.42), channel_id=1, source_target_pairs={{0,4},{1,5},{2,6},{3,7},{4,0},{5,1},{6,2},{7,3},{8,12},{9,13},{10,... | collective-permute-start | bytes 417800 | tf_op jit(solution)/shard_map/ppermute | solution.py:183
  17.8 19.3 %collective-permute-start.7 = (bf16[544,128]{1,0:T(8,128)(2,1)S(1)}, bf16[544,128]{1,0:T(8,128)(2,1)S(1)}, u32[]{:S(2)}, u32[]{:S(2)}) collective-permute-start(bf16[544,128]{1,0:T(8,128)(2,1)S(1)} %get-tuple-element.43), channel_id=1, source_target_pairs={{0,6},{1,7},{2,4},{3,5},{4,2},{5,3},{6,0},{7,1},{8,14},{9,15},{10,... | collective-permute-start | bytes 417800 | tf_op jit(solution)/shard_map/ppermute | solution.py:183
  21.2 15.8 %collective-permute-start.1 = (bf16[432,512]{1,0:T(8,128)(2,1)S(1)}, bf16[432,512]{1,0:T(8,128)(2,1)S(1)}, u32[]{:S(2)}, u32[]{:S(2)}) collective-permute-start(bf16[432,512]{1,0:T(8,128)(2,1)S(1)} %constant_dynamic-slice_fusion.1), channel_id=1, source_target_pairs={{0,16},{1,9},{2,18},{3,11},{4,20},{5,13},{6,22},{7,15},{8,24},{9,1... | collective-permute-start | bytes 1327112 | tf_op jit(solution)/shard_map/ppermute | solution.py:209
  35.4 2.6 %collective-permute-start.16 = (bf16[128,3456]{1,0:T(8,128)(2,1)S(1)}, bf16[128,3456]{1,0:T(8,128)(2,1)S(1)}, u32[]{:S(2)}, u32[]{:S(2)}) collective-permute-start(bf16[128,3456]{1,0:T(8,128)(2,1)S(1)} %collective-permute-done.14), channel_id=1, source_target_pairs={{0,1},{1,0},{2,3},{3,2},{4,5},{5,4},{6,7},{7,6},{8,9},{9,8},{10,11... | collective-permute-start | bytes 2654216 | tf_op jit(solution)/shard_map/ppermute | solution.py:209
  35.5 9.2 %collective-permute-start.15 = (bf16[64,3456]{1,0:T(8,128)(2,1)S(1)}, bf16[64,3456]{1,0:T(8,128)(2,1)S(1)}, u32[]{:S(2)}, u32[]{:S(2)}) collective-permute-start(bf16[64,3456]{1,0:T(8,128)(2,1)S(1)} %constant_dynamic-slice_fusion), channel_id=1, source_target_pairs={{0,16},{1,9},{2,18},{3,11},{4,20},{5,13},{6,22},{7,15},{8,24},{9,1... | collective-permute-start | bytes 1327112 | tf_op jit(solution)/shard_map/ppermute | solution.py:209
  37.1 2.5 %collective-permute-start.12 = (bf16[864,512]{1,0:T(8,128)(2,1)S(1)}, bf16[864,512]{1,0:T(8,128)(2,1)S(1)}, u32[]{:S(2)}, u32[]{:S(2)}) collective-permute-start(bf16[864,512]{1,0:T(8,128)(2,1)S(1)} %collective-permute-done), channel_id=1, source_target_pairs={{0,1},{1,0},{2,3},{3,2},{4,5},{5,4},{6,7},{7,6},{8,9},{9,8},{10,11... | collective-permute-start | bytes 2654216 | tf_op jit(solution)/shard_map/ppermute | solution.py:209
  37.3 4.7 %copy-start = (bf16[256,3456]{1,0:T(8,128)(2,1)S(1)}, bf16[256,3456]{1,0:T(8,128)(2,1)}, u32[]{:S(2)}) copy-start(bf16[256,3456]{1,0:T(8,128)(2,1)} %cot_ref.1) | copy-start | bytes 5308420
  37.3 3.5 %collective-permute-start.8 = (bf16[544,128]{1,0:T(8,128)(2,1)S(1)}, bf16[544,128]{1,0:T(8,128)(2,1)S(1)}, u32[]{:S(2)}, u32[]{:S(2)}) collective-permute-start(bf16[544,128]{1,0:T(8,128)(2,1)S(1)} %get-tuple-element.44.refs_0_), channel_id=1, source_target_pairs={{0,1},{1,0},{2,3},{3,2},{4,5},{5,4},{6,7},{7,6},{8,9},{9,8},{10,11... | collective-permute-start | bytes 417800 | tf_op jit(solution)/shard_map/ppermute | solution.py:209
  37.8 3.0 %collective-permute-start.9 = (bf16[544,128]{1,0:T(8,128)(2,1)S(1)}, bf16[544,128]{1,0:T(8,128)(2,1)S(1)}, u32[]{:S(2)}, u32[]{:S(2)}) collective-permute-start(bf16[544,128]{1,0:T(8,128)(2,1)S(1)} %collective-permute-done.5.refs_2_), channel_id=1, source_target_pairs={{0,1},{1,0},{2,3},{3,2},{4,5},{5,4},{6,7},{7,6},{8,9},{9,8},{10,11... | collective-permute-start | bytes 417800 | tf_op jit(solution)/shard_map/ppermute | solution.py:209
  38.0 2.6 %collective-permute-start.13 = (bf16[432,512]{1,0:T(8,128)(2,1)S(1)}, bf16[432,512]{1,0:T(8,128)(2,1)S(1)}, u32[]{:S(2)}, u32[]{:S(2)}) collective-permute-start(bf16[432,512]{1,0:T(8,128)(2,1)S(1)} %collective-permute-done.1), channel_id=1, source_target_pairs={{0,1},{1,0},{2,3},{3,2},{4,5},{5,4},{6,7},{7,6},{8,9},{9,8},{10,11... | collective-permute-start | bytes 1327112 | tf_op jit(solution)/shard_map/ppermute | solution.py:209
  39.6 1.4 %collective-permute-start.10 = (bf16[544,128]{1,0:T(8,128)(2,1)S(1)}, bf16[544,128]{1,0:T(8,128)(2,1)S(1)}, u32[]{:S(2)}, u32[]{:S(2)}) collective-permute-start(bf16[544,128]{1,0:T(8,128)(2,1)S(1)} %collective-permute-done.6.refs_4_), channel_id=1, source_target_pairs={{0,1},{1,0},{2,3},{3,2},{4,5},{5,4},{6,7},{7,6},{8,9},{9,8},{10,11... | collective-permute-start | bytes 417800 | tf_op jit(solution)/shard_map/ppermute | solution.py:209
  40.6 1.4 %collective-permute-start.11 = (bf16[544,128]{1,0:T(8,128)(2,1)S(1)}, bf16[544,128]{1,0:T(8,128)(2,1)S(1)}, u32[]{:S(2)}, u32[]{:S(2)}) collective-permute-start(bf16[544,128]{1,0:T(8,128)(2,1)S(1)} %collective-permute-done.7.refs_6_), channel_id=1, source_target_pairs={{0,1},{1,0},{2,3},{3,2},{4,5},{5,4},{6,7},{7,6},{8,9},{9,8},{10,11... | collective-permute-start | bytes 417800 | tf_op jit(solution)/shard_map/ppermute | solution.py:209
  44.7 1.9 %collective-permute-start.17 = (bf16[64,3456]{1,0:T(8,128)(2,1)S(1)}, bf16[64,3456]{1,0:T(8,128)(2,1)S(1)}, u32[]{:S(2)}, u32[]{:S(2)}) collective-permute-start(bf16[64,3456]{1,0:T(8,128)(2,1)S(1)} %collective-permute-done.15), channel_id=1, source_target_pairs={{0,1},{1,0},{2,3},{3,2},{4,5},{5,4},{6,7},{7,6},{8,9},{9,8},{10,11... | collective-permute-start | bytes 1327112 | tf_op jit(solution)/shard_map/ppermute | solution.py:209
  50.4 8.2 %collective-permute-start.18 = (bf16[512,128]{1,0:T(8,128)(2,1)S(1)}, bf16[512,128]{1,0:T(8,128)(2,1)S(1)}, u32[]{:S(2)}, u32[]{:S(2)}) collective-permute-start(bf16[512,128]{1,0:T(8,128)(2,1)S(1)} %get-tuple-element.56), channel_id=1, source_target_pairs={{0,6},{1,7},{2,4},{3,5},{4,2},{5,3},{6,0},{7,1},{8,14},{9,15},{10,... | collective-permute-start | bytes 393224 | tf_op jit(solution)/shard_map/ppermute | solution.py:183
  54.3 8.2 %collective-permute-start.20 = (bf16[512,128]{1,0:T(8,128)(2,1)S(1)}, bf16[512,128]{1,0:T(8,128)(2,1)S(1)}, u32[]{:S(2)}, u32[]{:S(2)}) collective-permute-start(bf16[512,128]{1,0:T(8,128)(2,1)S(1)} %get-tuple-element.61), channel_id=1, source_target_pairs={{0,2},{1,3},{2,0},{3,1},{4,6},{5,7},{6,4},{7,5},{8,10},{9,11},{10,... | collective-permute-start | bytes 393224 | tf_op jit(solution)/shard_map/ppermute | solution.py:183
  54.3 10.7 %collective-permute-start.22 = (bf16[512,128]{1,0:T(8,128)(2,1)S(1)}, bf16[512,128]{1,0:T(8,128)(2,1)S(1)}, u32[]{:S(2)}, u32[]{:S(2)}) collective-permute-start(bf16[512,128]{1,0:T(8,128)(2,1)S(1)} %get-tuple-element.62), channel_id=1, source_target_pairs={{0,4},{1,5},{2,6},{3,7},{4,0},{5,1},{6,2},{7,3},{8,12},{9,13},{10,... | collective-permute-start | bytes 393224 | tf_op jit(solution)/shard_map/ppermute | solution.py:183
  54.9 10.1 %collective-permute-start.19 = (bf16[512,128]{1,0:T(8,128)(2,1)S(1)}, bf16[512,128]{1,0:T(8,128)(2,1)S(1)}, u32[]{:S(2)}, u32[]{:S(2)}) collective-permute-start(bf16[512,128]{1,0:T(8,128)(2,1)S(1)} %get-tuple-element.60.refs_0_), channel_id=1, source_target_pairs={{0,1},{1,0},{2,3},{3,2},{4,5},{5,4},{6,7},{7,6},{8,9},{9,8},{10,11... | collective-permute-start | bytes 393224 | tf_op jit(solution)/shard_map/ppermute | solution.py:209
  54.9 19.4 %copy-start.1 = (s32[8,128,128]{2,1,0:T(8,128)S(1)}, s32[8,128,128]{2,1,0:T(8,128)}, u32[]{:S(2)}) copy-start(s32[8,128,128]{2,1,0:T(8,128)} %mult_ref.1) | copy-start | bytes 1572868
  54.9 19.4 %copy-start.3 = (s32[8]{0:T(128)S(1)}, s32[8]{0:T(128)}, u32[]{:S(2)}) copy-start(s32[8]{0:T(128)} %rows_ref.1) | copy-start | bytes 100
  58.6 6.4 %collective-permute-start.24 = (bf16[512,128]{1,0:T(8,128)(2,1)S(1)}, bf16[512,128]{1,0:T(8,128)(2,1)S(1)}, u32[]{:S(2)}, u32[]{:S(2)}) collective-permute-start(bf16[512,128]{1,0:T(8,128)(2,1)S(1)} %collective-permute-done.18.refs_6_), channel_id=1, source_target_pairs={{0,1},{1,0},{2,3},{3,2},{4,5},{5,4},{6,7},{7,6},{8,9},{9,8},{10,11... | collective-permute-start | bytes 393224 | tf_op jit(solution)/shard_map/ppermute | solution.py:209
  62.5 2.5 %collective-permute-start.21 = (bf16[512,128]{1,0:T(8,128)(2,1)S(1)}, bf16[512,128]{1,0:T(8,128)(2,1)S(1)}, u32[]{:S(2)}, u32[]{:S(2)}) collective-permute-start(bf16[512,128]{1,0:T(8,128)(2,1)S(1)} %collective-permute-done.20.refs_2_), channel_id=1, source_target_pairs={{0,1},{1,0},{2,3},{3,2},{4,5},{5,4},{6,7},{7,6},{8,9},{9,8},{10,11... | collective-permute-start | bytes 393224 | tf_op jit(solution)/shard_map/ppermute | solution.py:209
  65.0 1.3 %collective-permute-start.23 = (bf16[512,128]{1,0:T(8,128)(2,1)S(1)}, bf16[512,128]{1,0:T(8,128)(2,1)S(1)}, u32[]{:S(2)}, u32[]{:S(2)}) collective-permute-start(bf16[512,128]{1,0:T(8,128)(2,1)S(1)} %collective-permute-done.22.refs_4_), channel_id=1, source_target_pairs={{0,1},{1,0},{2,3},{3,2},{4,5},{5,4},{6,7},{7,6},{8,9},{9,8},{10,11... | collective-permute-start | bytes 393224 | tf_op jit(solution)/shard_map/ppermute | solution.py:209
  66.9 4.3 %collective-permute-start.25 = (bf16[256,128]{1,0:T(8,128)(2,1)S(1)}, bf16[256,128]{1,0:T(8,128)(2,1)S(1)}, u32[]{:S(2)}, u32[]{:S(2)}) collective-permute-start(bf16[256,128]{1,0:T(8,128)(2,1)S(1)} %get-tuple-element.65), channel_id=1, source_target_pairs={{0,8},{8,0},{16,24},{24,16},{1,9},{9,1},{17,25},{25,17},{2,10},{10... | collective-permute-start | bytes 196616 | tf_op jit(solution)/shard_map/ppermute | solution.py:183
  68.6 5.0 %collective-permute-start.26 = (bf16[256,128]{1,0:T(8,128)(2,1)S(1)}, bf16[256,128]{1,0:T(8,128)(2,1)S(1)}, u32[]{:S(2)}, u32[]{:S(2)}) collective-permute-start(bf16[256,128]{1,0:T(8,128)(2,1)S(1)} %get-tuple-element.66), channel_id=1, source_target_pairs={{0,16},{8,24},{16,0},{24,8},{1,17},{9,25},{17,1},{25,9},{2,18},{10... | collective-permute-start | bytes 196616 | tf_op jit(solution)/shard_map/ppermute | solution.py:183
  69.2 5.2 %collective-permute-start.27 = (bf16[256,128]{1,0:T(8,128)(2,1)S(1)}, bf16[256,128]{1,0:T(8,128)(2,1)S(1)}, u32[]{:S(2)}, u32[]{:S(2)}) collective-permute-start(bf16[256,128]{1,0:T(8,128)(2,1)S(1)} %get-tuple-element.67), channel_id=1, source_target_pairs={{0,24},{8,16},{16,8},{24,0},{1,25},{9,17},{17,9},{25,1},{2,26},{10... | collective-permute-start | bytes 196616 | tf_op jit(solution)/shard_map/ppermute | solution.py:183
  (3 other events, 8.4 us)

commit v3 on v2

--- a/solution.py
+++ b/solution.py
@@ -13,7 +13,7 @@
 CORES = 2
 LIST = 2
 META = 16
-FIRST = 5 * 10**10
+RELAY_FLOPS = 10**6
 BF16 = jnp.bfloat16
 F32 = jnp.float32
 SMEM = pl.BlockSpec(memory_space=pltpu.SMEM)
@@ -52,9 +52,13 @@
     return filled.astype(BF16)
 
 
-def products_kernel(nodes, quota, size, rows_hbm, table_hbm, slot_hbm, emb_hbm, mult_hbm, *refs):
-    outs = refs[:nodes]
-    rows_ref, table_ref, slot_ref, emb_ref, mult_ref, sems = refs[nodes:]
+def swap_bits(core):
+    return 1 + core, 2 - core
+
+
+def products_kernel(quota, size, rows_hbm, table_hbm, slot_hbm, emb_hbm, mult_hbm, *refs):
+    outs = refs[:5]
+    rows_ref, table_ref, slot_ref, emb_ref, mult_ref, sems = refs[5:]
     pairs = ((mult_hbm, mult_ref), (emb_hbm, emb_ref), (rows_hbm, rows_ref), (table_hbm, table_ref), (slot_hbm, slot_ref))
     copies = [pltpu.make_async_copy(src, dst, sems.at[i]) for i, (src, dst) in enumerate(pairs)]
     for copy in copies:
@@ -62,29 +66,41 @@
     for copy in copies:
         copy.wait()
     node = lax.axis_index("node")
-    for k in range(nodes):
+    near_bit, far_bit = swap_bits(lax.axis_index("table") % CORES)
+    own, far_out, opposite, hop_near, hop_opposite = outs
+    for out, k in ((far_out, far_bit), (hop_near, near_bit), (opposite, 3), (own, 0)):
         ids = []
         for i in range(quota):
             tile = (node ^ k) * quota + i
             weights = mult_ref[tile].astype(F32).astype(BF16)
             part = dot(weights, emb_ref[block(rows_ref[tile], size), :])
-            outs[k][i * size : (i + 1) * size, :] = part.astype(BF16)
+            out[i * size : (i + 1) * size, :] = part.astype(BF16)
             ids += [table_ref[tile], slot_ref[tile]]
-        outs[k][quota * size :, :] = id_rows(ids, meta_rows(quota))
-
-
-def relay_kernel(nodes, quota, size, tables, relative, *refs):
+        out[quota * size :, :] = id_rows(ids, meta_rows(quota))
+    hop_opposite[...] = opposite[...]
+
+
+def relay_kernel(quota, size, tables, relative, *refs):
     chips = tables // CORES
-    parts, outs = refs[:nodes], refs[nodes : nodes + chips]
-    index_ref, total, first_slot, slots = refs[nodes + chips :]
+    own, by_far, by_near, opposite, opposite_hop = refs[:5]
+    outs = refs[5 : 5 + chips]
+    index_ref, total, first_slot, slots = refs[5 + chips :]
     table = lax.axis_index("table")
     for r in range(tables):
         first_slot[r] = -1
         for e in range(LIST):
             slots[r * LIST + e] = -1
             total[r * LIST + e] = jnp.zeros((size, 128), F32)
-    for k in range(nodes):
-        ids = parts[k][quota * size :, :].astype(F32).astype(jnp.int32)
+    core = table % CORES
+    near_bit, far_bit = swap_bits(core)
+
+    def rows_of(part, rows):
+        if part is opposite:
+            return jnp.where(core == 1, opposite[rows, :].astype(F32), opposite_hop[rows, :].astype(F32))
+        return part[rows, :].astype(F32)
+
+    for part, k in ((own, 0), (by_far, far_bit), (by_near, near_bit), (opposite, 3)):
+        ids = rows_of(part, slice(quota * size, None)).astype(jnp.int32)
         for i in range(quota):
             target, slot = ids[2 * i, 0], ids[2 * i + 1, 0]
             entry = target ^ table if relative else target
@@ -94,7 +110,7 @@
             place = entry * LIST + which
             slots[place] = slot
             index_ref[k * quota + i] = place
-            total[place] += parts[k][i * size : (i + 1) * size, :].astype(F32)
+            total[place] += rows_of(part, slice(i * size, (i + 1) * size))
     for r in range(tables):
         out, base = outs[r // CORES], r % CORES * (LIST * size + META)
         for e in range(LIST):
@@ -105,18 +121,17 @@
 
 def pool_kernel(tables, size, *refs):
     parts = refs[:tables]
-    dense_ref, v_ref, cot_ref, first_ref, hidden_ref, scaled_ref, slot_ref, total = refs[tables:]
-    for b in range(BAG_BLOCKS):
+    dense_ref, cot_ref, v_ref, first_ref, scaled_ref, slot_ref, hidden_ref, total = refs[tables:]
+    for b in range(BAG_BLOCKS + 1):
         total[b] = jnp.zeros((size, 128), F32)
     for r in range(tables):
         part, base = parts[r], r % CORES * (LIST * size + META)
         ids = part[base + LIST * size : base + LIST * size + META, :].astype(F32).astype(jnp.int32)
         for e in range(LIST):
             slot_ref[r * LIST + e] = ids[e, 0]
-
-            @pl.when(ids[e, 0] >= 0)
-            def _(slot=ids[e, 0], part=part, begin=base + e * size):
-                total[slot] += part[begin : begin + size, :].astype(F32)
+            begin = base + e * size
+            place = jnp.where(ids[e, 0] < 0, BAG_BLOCKS, ids[e, 0])
+            total[place] += part[begin : begin + size, :].astype(F32)
 
     first_ref[:, :128] = dense_ref[...]
     for f in range(FEATURES):
@@ -129,21 +144,22 @@
         scaled_ref[:, columns] = (cot_ref[:, columns].astype(F32) * first_ref[:, columns].astype(F32)).astype(BF16)
 
 
-def owner_kernel(tables, size, slot_ref, hidden_ref, scaled_ref, v_ref, u_ref, bias_ref, cot_ref, *refs):
-    outs, dhidden = refs[: tables // CORES], refs[tables // CORES]
-    dhidden[...] = nt_dot(scaled_ref[...], u_ref[...]).astype(BF16)
-    for r in range(tables):
-        for e in range(LIST):
-            slot = slot_ref[r * LIST + e]
-
-            @pl.when(slot >= 0)
-            def _(slot=slot, out=outs[r // CORES], begin=(r % CORES * LIST + e) * size):
-                columns = block(slot // SAMPLE_BLOCKS + 1, 128)
-                samples = block(slot % SAMPLE_BLOCKS, size)
-                scale = dot(hidden_ref[samples, :], u_ref[:, columns]) + bias_ref[:, columns]
-                grad = cot_ref[samples, columns].astype(F32) * (scale + 1.0)
-                grad = grad + nt_dot(dhidden[samples, :], v_ref[columns, :])
-                out[begin : begin + size, :] = grad.astype(BF16)
+def blocks_kernel(group, size, slot_ref, hidden_ref, dhidden_ref, v_ref, u_ref, bias_ref, cot_ref, *outs):
+    for chip, out in zip(group, outs):
+        for entry in range(CORES * LIST):
+            slot = jnp.maximum(slot_ref[chip * CORES * LIST + entry], 0)
+            columns = block(slot // SAMPLE_BLOCKS + 1, 128)
+            samples = block(slot % SAMPLE_BLOCKS, size)
+            scale = dot(hidden_ref[samples, :], u_ref[:, columns]) + bias_ref[:, columns]
+            grad = cot_ref[samples, columns].astype(F32) * (scale + 1.0)
+            grad = grad + nt_dot(dhidden_ref[samples, :], v_ref[columns, :])
+            out[entry * size : (entry + 1) * size, :] = grad.astype(BF16)
+
+
+def owner_kernel(group, size, slot_ref, hidden_ref, scaled_ref, v_ref, u_ref, bias_ref, cot_ref, *outs):
+    dhidden_ref = outs[-1]
+    dhidden_ref[...] = nt_dot(scaled_ref[...], u_ref[...]).astype(BF16)
+    blocks_kernel(group, size, slot_ref, hidden_ref, dhidden_ref, v_ref, u_ref, bias_ref, cot_ref, *outs[:-1])
 
 
 def cross_kernel(first_ref, hidden_ref, u_ref, bias_ref, out_ref):
@@ -215,6 +231,10 @@
 
 def far(value):
     return permute(value, lambda n, t: (n ^ (2 - t % 2), t))
+
+
+def across(value):
+    return permute(value, lambda n, t: (n ^ 3 * (t % 2), t))
 
 
 def sibling(value):
@@ -256,10 +276,10 @@
     part = jax.ShapeDtypeStruct((quota * size + meta_rows(quota), 128), BF16)
     hbm = pl.BlockSpec(memory_space=pltpu.HBM)
     parts = pl.pallas_call(
-        functools.partial(products_kernel, nodes, quota, size),
-        out_shape=[part] * nodes,
+        functools.partial(products_kernel, quota, size),
+        out_shape=[part] * 5,
         in_specs=[hbm] * 5,
-        out_specs=[VMEM] * nodes,
+        out_specs=[VMEM] * 5,
         scratch_shapes=[
             pltpu.SMEM((tiles,), jnp.int32),
             pltpu.SMEM((tiles,), jnp.int32),
@@ -272,18 +292,26 @@
         name="products",
     )(tile_rows, tile_table, tile_slot, emb_rows, tile_mult)
     first_v = near(cross_v)
-    parts = [parts[0]] + [xor_permute(parts[k], "node", k) for k in range(1, nodes)]
-    late_u, parts[1] = lax.optimization_barrier((cross_u, parts[1]))
-    first_u = near(late_u)
+    first_u = near(cross_u)
+    own, far_out, opposite, hop_near, hop_opposite = parts
+    parts = [
+        own,
+        far(far_out),
+        sibling(far(sibling(hop_near))),
+        across(opposite),
+        sibling(across(sibling(hop_opposite))),
+    ]
     second_v = far(half_of(first_v))
+    first_u, first_v = lax.optimization_barrier((first_u, first_v))
+    other_v = sibling(first_v)
     second_u = far(half_of(first_u))
 
     chips = tables // CORES
     listed = jax.ShapeDtypeStruct((CORES * (LIST * size + META), 128), BF16)
     *lists, index = pl.pallas_call(
-        functools.partial(relay_kernel, nodes, quota, size, tables, relative),
+        functools.partial(relay_kernel, quota, size, tables, relative),
         out_shape=[listed] * chips + [jax.ShapeDtypeStruct((tiles,), jnp.int32)],
-        in_specs=[VMEM] * nodes,
+        in_specs=[VMEM] * 5,
         out_specs=[VMEM] * chips + [SMEM],
         scratch_shapes=[
             pltpu.VMEM((tables * LIST, size, 128), F32),
@@ -291,45 +319,58 @@
             pltpu.SMEM((tables * LIST,), jnp.int32),
         ],
         compiler_params=params(32),
-        cost_estimate=pl.CostEstimate(flops=FIRST, bytes_accessed=0, transcendentals=0),
+        cost_estimate=pl.CostEstimate(flops=RELAY_FLOPS, bytes_accessed=0, transcendentals=0),
         name="relay",
     )(*parts)
+    swap_u = first_u
     if relative:
-        first_v, second_v, *arrived = lax.optimization_barrier((first_v, second_v, *exchange_chips(lists)))
+        arrived = exchange_chips(lists)
+        second_v, swap_u, *arrived = lax.optimization_barrier((second_v, first_u, *arrived))
         arrived = exchange_cores(arrived)
     else:
         arrived = exchange_whole(lists)
-    full_v = assemble(cross_v, first_v, sibling(first_v), second_v, sibling(second_v))
+    full_v = assemble(cross_v, first_v, other_v, second_v, sibling(second_v))
 
     grad = jax.ShapeDtypeStruct((CORES * LIST * size, 128), BF16)
-    first, hidden, scaled, slots = pl.pallas_call(
+    first, scaled, slots, hidden = pl.pallas_call(
         functools.partial(pool_kernel, tables, size),
         out_shape=[
             jax.ShapeDtypeStruct((samples, cross), BF16),
-            jax.ShapeDtypeStruct((samples, rank), BF16),
             jax.ShapeDtypeStruct((samples, cross), BF16),
             jax.ShapeDtypeStruct((tables * LIST,), jnp.int32),
+            jax.ShapeDtypeStruct((samples, rank), BF16),
         ],
         in_specs=[VMEM] * (tables + 3),
-        out_specs=[VMEM] * 3 + [SMEM],
-        scratch_shapes=[pltpu.VMEM((BAG_BLOCKS, size, 128), F32)],
+        out_specs=[VMEM, VMEM, SMEM, VMEM],
+        scratch_shapes=[pltpu.VMEM((BAG_BLOCKS + 1, size, 128), F32)],
         compiler_params=params(24),
         name="pool",
-    )(*arrived, dense, full_v, cotangent)
+    )(*arrived, dense, cotangent, full_v)
 
     if relative:
-        second_u, hidden = lax.optimization_barrier((second_u, hidden))
-    full_u = assemble(cross_u, first_u, sibling(first_u), second_u, sibling(second_u))
-
-    grads = pl.pallas_call(
-        functools.partial(owner_kernel, tables, size),
-        out_shape=[grad] * chips,
+        second_u, scaled = lax.optimization_barrier((second_u, scaled))
+    full_u = assemble(cross_u, first_u, sibling(swap_u), second_u, sibling(second_u))
+
+    half = chips // 2
+    groups = (range(half, chips), range(half))
+    *far_grads, dhidden = pl.pallas_call(
+        functools.partial(owner_kernel, groups[0], size),
+        out_shape=[grad] * len(groups[0]) + [jax.ShapeDtypeStruct((samples, rank), BF16)],
         in_specs=[SMEM] + [VMEM] * 6,
-        out_specs=[VMEM] * chips,
-        scratch_shapes=[pltpu.VMEM((samples, rank), BF16)],
+        out_specs=[VMEM] * (len(groups[0]) + 1),
         compiler_params=params(24),
         name="owner",
     )(slots, hidden, scaled, full_v, full_u, bias, cotangent)
+    near_grads = pl.pallas_call(
+        functools.partial(blocks_kernel, groups[1], size),
+        out_shape=[grad] * len(groups[1]),
+        in_specs=[SMEM] + [VMEM] * 6,
+        out_specs=[VMEM] * len(groups[1]),
+        compiler_params=params(24),
+        name="blocks",
+    )(slots, hidden, dhidden, full_v, full_u, bias, cotangent)
+    grads = [*near_grads, *far_grads]
+
     cross_out = pl.pallas_call(
         cross_kernel,
         out_shape=jax.ShapeDtypeStruct((samples, cross), BF16),

time: 76.3 us -> 74.7 us (0.979)
  waiting for transfers between devices: 34.3 us -> 19.4 us
  starting transfers between devices: 24 us -> 33.7 us
  local copies, waits for them, and re-layouts: 2.75 us -> 6.33 us
    ppermute x16 -> x24, waiting for transfers between devices: 21.6 us -> 6.15 us  [permute(): return lax.ppermute(value, ('node', 'table'), pairs)]
    ppermute x16 -> x24, starting transfers between devices: 6.96 us -> 21.1 us  [permute(): return lax.ppermute(value, ('node', 'table'), pairs)]
    ppermute x12 -> x9, starting transfers between devices: 17.1 us -> 12.5 us  [xor_permute(): return lax.ppermute(value, axis, [(i, i ^ k) for i in range(size)])]
    dynamic_update_slice x10, local copies, waits for them, and re-layouts: 0.67 us -> 3.01 us  [assemble(): whole = lax.dynamic_update_slice(whole, piece, (row, 0))]
    dynamic_slice x2, local copies, waits for them, and re-layouts: 0.06 us -> 2.09 us  [half_of(): return lax.dynamic_slice(shard, (core * half, 0), (half, shard.shape[1]))]
    unnamed x14, local copies, waits for them, and re-layouts: 0.82 us -> 0.03 us
    pallas_call x3 -> x4, Pallas kernels: 6.61 us -> 7.27 us  [the longest x1 2.34 us: body(): pl.pallas_call(functools.partial(owner_kernel, groups[0], size), out_shap...]
    ppermute x12 -> x9, waiting for transfers between devices: 12.6 us -> 13.3 us  [xor_permute(): return lax.ppermute(value, axis, [(i, i ^ k) for i in range(size)])]
  transfers between devices with their start and end apart: 28 -> 33, of which waited for: 16 -> 15; matrix products, arithmetic and copies ran while one was open for 2% -> 8% of each run, Pallas kernels for 8% -> 13%
where the time goes in v3:
time: 74.7 us; the launch traced here: 74.2 us
  starting transfers between devices  33.7 us (45%)
  waiting for transfers between devices  19.4 us (26%)
  Pallas kernels  13.8 us (18%)
  local copies, waits for them, and re-layouts  6.33 us (8%)
  between operations  0.98 us (1%)
    ppermute x24, starting transfers between devices, permute(): return lax.ppermute(value, ('node', 'table'), pairs)  21.1 us
    ppermute x9, waiting for transfers between devices, xor_permute(): return lax.ppermute(value, axis, [(i, i ^ k) for i in range(size)])  13.3 us
    ppermute x9, starting transfers between devices, xor_permute(): return lax.ppermute(value, axis, [(i, i ^ k) for i in range(size)])  12.5 us
    ppermute x24, waiting for transfers between devices, permute(): return lax.ppermute(value, ('node', 'table'), pairs)  6.15 us
    dynamic_update_slice x10, local copies, waits for them, and re-layouts, assemble(): whole = lax.dynamic_update_slice(whole, piece, (row, 0))  3.01 us
    pallas_call x1, Pallas kernels, body(): pl.pallas_call(cross_kernel, out_shape=jax.ShapeDtypeStruct((samples, cro...  2.41 us
    pallas_call x1, Pallas kernels, body(): pl.pallas_call(functools.partial(owner_kernel, groups[0], size), out_shap...  2.34 us
    dynamic_slice x2, local copies, waits for them, and re-layouts, half_of(): return lax.dynamic_slice(shard, (core * half, 0), (half, shard.shape[1]))  2.09 us
  transfers between devices with their start and end apart: 33, of which 15 were waited for; matrix products, arithmetic and copies ran while one was open for 8% of the time, Pallas kernels for 13%

profile of v3, /device:TPU:0, one launch (start us, length us, event | category | flops | bytes accessed | tf_op | source)
XLA Modules:
  0.0 74.2 jit_solution(17057097480952937341)
XLA Ops:
  0.6 3.0 %collective-permute-start = (bf16[864,512]{1,0:T(8,128)(2,1)}, bf16[864,512]{1,0:T(8,128)(2,1)}, u32[]{:S(2)}, u32[]{:S(2)}) collective-permute-start(bf16[864,512]{1,0:T(8,128)(2,1)} %param.16), channel_id=1, source_target_pairs={{0,8},{1,17},{2,10},{3,19},{4,12},{5,21},{6,14},{7,23},{8,0},{9,25... | collective-permute-start | bytes 2654216 | tf_op jit(solution)/shard_map/ppermute | solution.py:225
  3.7 2.0 %products.1 = (bf16[272,128]{1,0:T(8,128)(2,1)}, bf16[272,128]{1,0:T(8,128)(2,1)}, bf16[272,128]{1,0:T(8,128)(2,1)}, bf16[272,128]{1,0:T(8,128)(2,1)}, bf16[272,128]{1,0:T(8,128)(2,1)}) custom-call(s32[8]{0:T(128)} %rows_ref.1, s32[8]{0:T(128)} %table_hbm.1, s32[8]{0:T(128)} %slot_hbm.1, bf16[512,128]{1,0:T(8,128)(2,1)} %emb_hbm.1, s32[8,128,128]{2,1,0:T(8,128)} %mult_ref.1), custom_call_target="tpu_custom_call" | custom-call | tf_op jit(solution)/shard_map/products/pallas_call | solution.py:278
  6.3 2.0 %collective-permute-start.3 = (bf16[272,128]{1,0:T(8,128)(2,1)}, bf16[272,128]{1,0:T(8,128)(2,1)}, u32[]{:S(2)}, u32[]{:S(2)}) collective-permute-start(bf16[272,128]{1,0:T(8,128)(2,1)} %get-tuple-element.39), channel_id=1, source_target_pairs={{0,16},{1,9},{2,18},{3,11},{4,20},{5,13},{6,22},{7,15},{8,24},{9,1... | collective-permute-start | bytes 208904 | tf_op jit(solution)/shard_map/ppermute | solution.py:225
  8.3 1.1 %collective-permute-start.5 = (bf16[272,128]{1,0:T(8,128)(2,1)}, bf16[272,128]{1,0:T(8,128)(2,1)}, u32[]{:S(2)}, u32[]{:S(2)}) collective-permute-start(bf16[272,128]{1,0:T(8,128)(2,1)} %collective-permute-done.4), channel_id=1, source_target_pairs={{0,16},{1,9},{2,18},{3,11},{4,20},{5,13},{6,22},{7,15},{8,24},{9,1... | collective-permute-start | bytes 208904 | tf_op jit(solution)/shard_map/ppermute | solution.py:225
  9.4 2.1 %collective-permute-start.9 = (bf16[272,128]{1,0:T(8,128)(2,1)}, bf16[272,128]{1,0:T(8,128)(2,1)}, u32[]{:S(2)}, u32[]{:S(2)}) collective-permute-start(bf16[272,128]{1,0:T(8,128)(2,1)} %collective-permute-done.8), channel_id=1, source_target_pairs={{0,0},{1,25},{2,2},{3,27},{4,4},{5,29},{6,6},{7,31},{8,8},{9,17},{... | collective-permute-start | bytes 208904 | tf_op jit(solution)/shard_map/ppermute | solution.py:225
  12.8 1.7 %collective-permute-start.7 = (bf16[272,128]{1,0:T(8,128)(2,1)}, bf16[272,128]{1,0:T(8,128)(2,1)S(1)}, u32[]{:S(2)}, u32[]{:S(2)}) collective-permute-start(bf16[272,128]{1,0:T(8,128)(2,1)} %get-tuple-element.41), channel_id=1, source_target_pairs={{0,0},{1,25},{2,2},{3,27},{4,4},{5,29},{6,6},{7,31},{8,8},{9,17},{... | collective-permute-start | bytes 208904 | tf_op jit(solution)/shard_map/ppermute | solution.py:225
  14.5 2.5 %collective-permute-start.6 = (bf16[272,128]{1,0:T(8,128)(2,1)}, bf16[272,128]{1,0:T(8,128)(2,1)S(1)}, u32[]{:S(2)}, u32[]{:S(2)}) collective-permute-start(bf16[272,128]{1,0:T(8,128)(2,1)} %collective-permute-done.5), channel_id=1, source_target_pairs={{0,1},{1,0},{2,3},{3,2},{4,5},{5,4},{6,7},{7,6},{8,9},{9,8},{10,11... | collective-permute-start | bytes 208904 | tf_op jit(solution)/shard_map/ppermute | solution.py:225
  18.4 1.6 %relay.1 = (bf16[544,128]{1,0:T(8,128)(2,1)S(1)}, bf16[544,128]{1,0:T(8,128)(2,1)S(1)}, bf16[544,128]{1,0:T(8,128)(2,1)S(1)}, bf16[544,128]{1,0:T(8,128)(2,1)S(1)}, s32[8]{0:T(128)S(1)}) custom-call(bf16[272,128]{1,0:T(8,128)(2,1)S(1)} %copy-done.2, bf16[272,128]{1,0:T(8,128)(2,1)} %collective-permute-done.3.refs_1_, ...), custom_call_target="tpu_custom_call" | custom-call | flops 1000000 | tf_op jit(solution)/shard_map/relay/pallas_call | solution.py:311
  20.0 1.6 %collective-permute-start.11 = (bf16[544,128]{1,0:T(8,128)(2,1)S(1)}, bf16[544,128]{1,0:T(8,128)(2,1)S(1)}, u32[]{:S(2)}, u32[]{:S(2)}) collective-permute-start(bf16[544,128]{1,0:T(8,128)(2,1)S(1)} %get-tuple-element.44), channel_id=1, source_target_pairs={{0,2},{1,3},{2,0},{3,1},{4,6},{5,7},{6,4},{7,5},{8,10},{9,11},{10,... | collective-permute-start | bytes 417800 | tf_op jit(solution)/shard_map/ppermute | solution.py:199
  21.7 2.6 %collective-permute-start.12 = (bf16[544,128]{1,0:T(8,128)(2,1)S(1)}, bf16[544,128]{1,0:T(8,128)(2,1)S(1)}, u32[]{:S(2)}, u32[]{:S(2)}) collective-permute-start(bf16[544,128]{1,0:T(8,128)(2,1)S(1)} %get-tuple-element.45), channel_id=1, source_target_pairs={{0,4},{1,5},{2,6},{3,7},{4,0},{5,1},{6,2},{7,3},{8,12},{9,13},{10,... | collective-permute-start | bytes 417800 | tf_op jit(solution)/shard_map/ppermute | solution.py:199
  24.5 1.0 %constant_dynamic-slice_fusion.1 = bf16[432,512]{1,0:T(8,128)(2,1)S(1)} fusion(bf16[864,512]{1,0:T(8,128)(2,1)} %collective-permute-done, s32[]{:T(128)S(6)} %select_n.50), kind=kLoop, calls=%fused_computation.11 | loop fusion | bytes 884740 | tf_op jit(solution)/shard_map/dynamic_slice | solution.py:247
  25.5 1.6 %collective-permute-start.1 = (bf16[432,512]{1,0:T(8,128)(2,1)S(1)}, bf16[432,512]{1,0:T(8,128)(2,1)S(1)}, u32[]{:S(2)}, u32[]{:S(2)}) collective-permute-start(bf16[432,512]{1,0:T(8,128)(2,1)S(1)} %constant_dynamic-slice_fusion.1), channel_id=1, source_target_pairs={{0,16},{1,9},{2,18},{3,11},{4,20},{5,13},{6,22},{7,15},{8,24},{9,1... | collective-permute-start | bytes 1327112 | tf_op jit(solution)/shard_map/ppermute | solution.py:225
  28.4 1.0 %constant_dynamic-slice_fusion = bf16[64,3456]{1,0:T(8,128)(2,1)S(1)} fusion(bf16[128,3456]{1,0:T(8,128)(2,1)} %collective-permute-done.2, s32[]{:T(128)S(6)} %select_n.56), kind=kLoop, calls=%fused_computation.5 | loop fusion | bytes 884740 | tf_op jit(solution)/shard_map/dynamic_slice | solution.py:247
  29.5 1.2 %collective-permute-start.20 = (bf16[64,3456]{1,0:T(8,128)(2,1)S(1)}, bf16[64,3456]{1,0:T(8,128)(2,1)S(1)}, u32[]{:S(2)}, u32[]{:S(2)}) collective-permute-start(bf16[64,3456]{1,0:T(8,128)(2,1)S(1)} %constant_dynamic-slice_fusion), channel_id=1, source_target_pairs={{0,16},{1,9},{2,18},{3,11},{4,20},{5,13},{6,22},{7,15},{8,24},{9,1... | collective-permute-start | bytes 1327112 | tf_op jit(solution)/shard_map/ppermute | solution.py:225
  30.6 2.5 %collective-permute-done.13.refs_6_ = bf16[544,128]{1,0:T(8,128)(2,1)S(1)} collective-permute-done((bf16[544,128]{1,0:T(8,128)(2,1)S(1)}, bf16[544,128]{1,0:T(8,128)(2,1)S(1)}, u32[]{:S(2)}, u32[]{:S(2)}) %collective-permute-start.13) | collective-permute-done | bytes 139296 | tf_op jit(solution)/shard_map/ppermute | solution.py:199
  33.9 2.3 %collective-permute-start.19 = (bf16[432,512]{1,0:T(8,128)(2,1)S(1)}, bf16[432,512]{1,0:T(8,128)(2,1)S(1)}, u32[]{:S(2)}, u32[]{:S(2)}) collective-permute-start(bf16[432,512]{1,0:T(8,128)(2,1)S(1)} %collective-permute-done.1), channel_id=1, source_target_pairs={{0,1},{1,0},{2,3},{3,2},{4,5},{5,4},{6,7},{7,6},{8,9},{9,8},{10,11... | collective-permute-start | bytes 1327112 | tf_op jit(solution)/shard_map/ppermute | solution.py:225
  36.2 1.3 %constant_dynamic-update-slice_fusion.3 = bf16[512,3456]{1,0:T(8,128)(2,1)S(1)} fusion(bf16[512,3456]{1,0:T(8,128)(2,1)S(1)} %constant_dynamic-update-slice_fusion.4, bf16[128,3456]{1,0:T(8,128)(2,1)} %collective-permute-done.2, s32[]{:T(128)S(6)} %select_n.58), kind=kLoop, calls=%fused_computation.3 | loop fusion | bytes 1769476 | tf_op jit(solution)/shard_map/dynamic_update_slice | solution.py:263
  38.0 1.2 %constant_dynamic-update-slice_fusion.8 = bf16[3456,512]{1,0:T(8,128)(2,1)S(1)} fusion(bf16[3456,512]{1,0:T(8,128)(2,1)S(1)} %constant_dynamic-update-slice_fusion.9, bf16[864,512]{1,0:T(8,128)(2,1)} %collective-permute-done, s32[]{:T(128)S(6)} %select_n.52), kind=kLoop, calls=%fused_computation.9 | loop fusion | bytes 1769476 | tf_op jit(solution)/shard_map/dynamic_update_slice | solution.py:263
  41.4 2.0 %pool.1 = (bf16[256,3456]{1,0:T(8,128)(2,1)S(1)}, bf16[256,3456]{1,0:T(8,128)(2,1)S(1)}, s32[16]{0:T(128)S(1)}, bf16[256,512]{1,0:T(8,128)(2,1)S(1)}) custom-call(bf16[544,128]{1,0:T(8,128)(2,1)S(1)} %get-tuple-element.47.refs_0_, bf16[544,128]{1,0:T(8,128)(2,1)S(1)} %collective-permute-done.14.refs_1_, ...), custom_call_target="tpu_custom_call" | custom-call | tf_op jit(solution)/shard_map/pool/pallas_call | solution.py:335
  43.8 1.4 %collective-permute-done.22 = bf16[64,3456]{1,0:T(8,128)(2,1)S(1)} collective-permute-done((bf16[64,3456]{1,0:T(8,128)(2,1)S(1)}, bf16[64,3456]{1,0:T(8,128)(2,1)S(1)}, u32[]{:S(2)}, u32[]{:S(2)}) %collective-permute-start.22) | collective-permute-done | bytes 442400 | tf_op jit(solution)/shard_map/ppermute | solution.py:225
  45.3 2.3 %owner.1 = (bf16[512,128]{1,0:T(8,128)(2,1)S(1)}, bf16[512,128]{1,0:T(8,128)(2,1)S(1)}, bf16[256,512]{1,0:T(8,128)(2,1)S(1)}) custom-call(s32[16]{0:T(128)S(1)} %get-tuple-element.53.slot_ref, bf16[256,512]{1,0:T(8,128)(2,1)S(1)} %get-tuple-element.54.hidden_ref, bf16[256,3456]{1,0:T(8,128)(2,1)S(1)} %get-tuple-element.56.scaled_ref, ...), custom_call_target="tpu_custom_call" | custom-call | tf_op jit(solution)/shard_map/owner/pallas_call | solution.py:356
  47.6 2.5 %collective-permute-start.23 = (bf16[512,128]{1,0:T(8,128)(2,1)S(1)}, bf16[512,128]{1,0:T(8,128)(2,1)S(1)}, u32[]{:S(2)}, u32[]{:S(2)}) collective-permute-start(bf16[512,128]{1,0:T(8,128)(2,1)S(1)} %get-tuple-element.59), channel_id=1, source_target_pairs={{0,6},{1,7},{2,4},{3,5},{4,2},{5,3},{6,0},{7,1},{8,14},{9,15},{10,... | collective-permute-start | bytes 393224 | tf_op jit(solution)/shard_map/ppermute | solution.py:199
  50.2 1.3 %blocks.1 = (bf16[512,128]{1,0:T(8,128)(2,1)S(1)}, bf16[512,128]{1,0:T(8,128)(2,1)S(1)}) custom-call(s32[16]{0:T(128)S(1)} %get-tuple-element.53.slot_ref, bf16[256,512]{1,0:T(8,128)(2,1)S(1)} %get-tuple-element.54.hidden_ref, bf16[256,512]{1,0:T(8,128)(2,1)S(1)} %get-tuple-element.63.dhidden_ref, ...), custom_call_target="tpu_custom_call" | custom-call | tf_op jit(solution)/shard_map/blocks/pallas_call | solution.py:364
  51.4 1.9 %collective-permute-start.25 = (bf16[512,128]{1,0:T(8,128)(2,1)S(1)}, bf16[512,128]{1,0:T(8,128)(2,1)S(1)}, u32[]{:S(2)}, u32[]{:S(2)}) collective-permute-start(bf16[512,128]{1,0:T(8,128)(2,1)S(1)} %get-tuple-element.65), channel_id=1, source_target_pairs={{0,2},{1,3},{2,0},{3,1},{4,6},{5,7},{6,4},{7,5},{8,10},{9,11},{10,... | collective-permute-start | bytes 393224 | tf_op jit(solution)/shard_map/ppermute | solution.py:199
  53.4 2.4 %cross.1 = bf16[256,3456]{1,0:T(8,128)(2,1)} custom-call(bf16[256,3456]{1,0:T(8,128)(2,1)S(1)} %get-tuple-element.60.first_ref, bf16[256,512]{1,0:T(8,128)(2,1)S(1)} %get-tuple-element.54.hidden_ref, bf16[512,3456]{1,0:T(8,128)(2,1)S(1)} %constant_dynamic-update-slice_fusion.u_ref, f32[1,3456]{1,0:T(1,128)S(1)} %reshape.7.bias_ref), custom_call_target="tpu_custom_call" | custom-call | flops 905969664 | bytes 7077888 | tf_op jit(solution)/shard_map/cross/pallas_call | solution.py:374
  56.4 1.7 %collective-permute-done.25.refs_2_ = bf16[512,128]{1,0:T(8,128)(2,1)S(1)} collective-permute-done((bf16[512,128]{1,0:T(8,128)(2,1)S(1)}, bf16[512,128]{1,0:T(8,128)(2,1)S(1)}, u32[]{:S(2)}, u32[]{:S(2)}) %collective-permute-start.25) | collective-permute-done | bytes 131104 | tf_op jit(solution)/shard_map/ppermute | solution.py:199
  58.0 5.5 %collective-permute-done.27.refs_4_ = bf16[512,128]{1,0:T(8,128)(2,1)S(1)} collective-permute-done((bf16[512,128]{1,0:T(8,128)(2,1)S(1)}, bf16[512,128]{1,0:T(8,128)(2,1)S(1)}, u32[]{:S(2)}, u32[]{:S(2)}) %collective-permute-start.27) | collective-permute-done | bytes 131104 | tf_op jit(solution)/shard_map/ppermute | solution.py:199
  63.6 1.3 %collective-permute-done.28.refs_5_ = bf16[512,128]{1,0:T(8,128)(2,1)S(1)} collective-permute-done((bf16[512,128]{1,0:T(8,128)(2,1)S(1)}, bf16[512,128]{1,0:T(8,128)(2,1)S(1)}, u32[]{:S(2)}, u32[]{:S(2)}) %collective-permute-start.28) | collective-permute-done | bytes 131104 | tf_op jit(solution)/shard_map/ppermute | solution.py:225
  66.2 1.3 %collective-permute-start.31 = (bf16[256,128]{1,0:T(8,128)(2,1)S(1)}, bf16[256,128]{1,0:T(8,128)(2,1)S(1)}, u32[]{:S(2)}, u32[]{:S(2)}) collective-permute-start(bf16[256,128]{1,0:T(8,128)(2,1)S(1)} %get-tuple-element.70), channel_id=1, source_target_pairs={{0,16},{8,24},{16,0},{24,8},{1,17},{9,25},{17,1},{25,9},{2,18},{10... | collective-permute-start | bytes 196616 | tf_op jit(solution)/shard_map/ppermute | solution.py:199
  67.5 1.5 %collective-permute-start.32 = (bf16[256,128]{1,0:T(8,128)(2,1)S(1)}, bf16[256,128]{1,0:T(8,128)(2,1)S(1)}, u32[]{:S(2)}, u32[]{:S(2)}) collective-permute-start(bf16[256,128]{1,0:T(8,128)(2,1)S(1)} %get-tuple-element.71), channel_id=1, source_target_pairs={{0,24},{8,16},{16,8},{24,0},{1,25},{9,17},{17,9},{25,1},{2,26},{10... | collective-permute-start | bytes 196616 | tf_op jit(solution)/shard_map/ppermute | solution.py:199
  70.5 2.2 %collective-permute-done.32.refs_3_ = bf16[256,128]{1,0:T(8,128)(2,1)S(1)} collective-permute-done((bf16[256,128]{1,0:T(8,128)(2,1)S(1)}, bf16[256,128]{1,0:T(8,128)(2,1)S(1)}, u32[]{:S(2)}, u32[]{:S(2)}) %collective-permute-start.32) | collective-permute-done | bytes 65568 | tf_op jit(solution)/shard_map/ppermute | solution.py:199
  72.7 1.5 %rows.1 = f32[512,128]{1,0:T(8,128)} custom-call(s32[8]{0:T(128)S(1)} %copy-done.4, s32[8,128,128]{2,1,0:T(8,128)S(1)} %copy-done.1, bf16[256,128]{1,0:T(8,128)(2,1)S(1)} %get-tuple-element.68.refs_0_, bf16[256,128]{1,0:T(8,128)(2,1)S(1)} %collective-permute-done.30.refs_1_, bf16[256,128]{1,0:T(8,128)(2,1)S(1)} %collective-permute-done.31.refs_2_, ...), custom_call_target="tpu_custom_call" | custom-call | tf_op jit(solution)/shard_map/rows/pallas_call | solution.py:405
  (71 shorter events, 12.1 us)
Async XLA Ops:
  0.6 23.9 %collective-permute-start = (bf16[864,512]{1,0:T(8,128)(2,1)}, bf16[864,512]{1,0:T(8,128)(2,1)}, u32[]{:S(2)}, u32[]{:S(2)}) collective-permute-start(bf16[864,512]{1,0:T(8,128)(2,1)} %param.16), channel_id=1, source_target_pairs={{0,8},{1,17},{2,10},{3,19},{4,12},{5,21},{6,14},{7,23},{8,0},{9,25... | collective-permute-start | bytes 2654216 | tf_op jit(solution)/shard_map/ppermute | solution.py:225
  3.6 23.8 %collective-permute-start.2 = (bf16[128,3456]{1,0:T(8,128)(2,1)}, bf16[128,3456]{1,0:T(8,128)(2,1)}, u32[]{:S(2)}, u32[]{:S(2)}) collective-permute-start(bf16[128,3456]{1,0:T(8,128)(2,1)} %param.17), channel_id=1, source_target_pairs={{0,8},{1,17},{2,10},{3,19},{4,12},{5,21},{6,14},{7,23},{8,0},{9,25... | collective-permute-start | bytes 2654216 | tf_op jit(solution)/shard_map/ppermute | solution.py:225
  5.8 2.6 %collective-permute-start.4 = (bf16[272,128]{1,0:T(8,128)(2,1)}, bf16[272,128]{1,0:T(8,128)(2,1)}, u32[]{:S(2)}, u32[]{:S(2)}) collective-permute-start(bf16[272,128]{1,0:T(8,128)(2,1)} %get-tuple-element.40), channel_id=1, source_target_pairs={{0,1},{1,0},{2,3},{3,2},{4,5},{5,4},{6,7},{7,6},{8,9},{9,8},{10,11... | collective-permute-start | bytes 208904 | tf_op jit(solution)/shard_map/ppermute | solution.py:225
  5.8 3.6 %collective-permute-start.8 = (bf16[272,128]{1,0:T(8,128)(2,1)}, bf16[272,128]{1,0:T(8,128)(2,1)}, u32[]{:S(2)}, u32[]{:S(2)}) collective-permute-start(bf16[272,128]{1,0:T(8,128)(2,1)} %get-tuple-element.42), channel_id=1, source_target_pairs={{0,1},{1,0},{2,3},{3,2},{4,5},{5,4},{6,7},{7,6},{8,9},{9,8},{10,11... | collective-permute-start | bytes 208904 | tf_op jit(solution)/shard_map/ppermute | solution.py:225
  6.3 6.4 %collective-permute-start.3 = (bf16[272,128]{1,0:T(8,128)(2,1)}, bf16[272,128]{1,0:T(8,128)(2,1)}, u32[]{:S(2)}, u32[]{:S(2)}) collective-permute-start(bf16[272,128]{1,0:T(8,128)(2,1)} %get-tuple-element.39), channel_id=1, source_target_pairs={{0,16},{1,9},{2,18},{3,11},{4,20},{5,13},{6,22},{7,15},{8,24},{9,1... | collective-permute-start | bytes 208904 | tf_op jit(solution)/shard_map/ppermute | solution.py:225
  8.3 6.1 %collective-permute-start.5 = (bf16[272,128]{1,0:T(8,128)(2,1)}, bf16[272,128]{1,0:T(8,128)(2,1)}, u32[]{:S(2)}, u32[]{:S(2)}) collective-permute-start(bf16[272,128]{1,0:T(8,128)(2,1)} %collective-permute-done.4), channel_id=1, source_target_pairs={{0,16},{1,9},{2,18},{3,11},{4,20},{5,13},{6,22},{7,15},{8,24},{9,1... | collective-permute-start | bytes 208904 | tf_op jit(solution)/shard_map/ppermute | solution.py:225
  9.4 7.5 %collective-permute-start.9 = (bf16[272,128]{1,0:T(8,128)(2,1)}, bf16[272,128]{1,0:T(8,128)(2,1)}, u32[]{:S(2)}, u32[]{:S(2)}) collective-permute-start(bf16[272,128]{1,0:T(8,128)(2,1)} %collective-permute-done.8), channel_id=1, source_target_pairs={{0,0},{1,25},{2,2},{3,27},{4,4},{5,29},{6,6},{7,31},{8,8},{9,17},{... | collective-permute-start | bytes 208904 | tf_op jit(solution)/shard_map/ppermute | solution.py:225
  12.8 4.6 %collective-permute-start.7 = (bf16[272,128]{1,0:T(8,128)(2,1)}, bf16[272,128]{1,0:T(8,128)(2,1)S(1)}, u32[]{:S(2)}, u32[]{:S(2)}) collective-permute-start(bf16[272,128]{1,0:T(8,128)(2,1)} %get-tuple-element.41), channel_id=1, source_target_pairs={{0,0},{1,25},{2,2},{3,27},{4,4},{5,29},{6,6},{7,31},{8,8},{9,17},{... | collective-permute-start | bytes 208904 | tf_op jit(solution)/shard_map/ppermute | solution.py:225
  14.5 3.6 %collective-permute-start.6 = (bf16[272,128]{1,0:T(8,128)(2,1)}, bf16[272,128]{1,0:T(8,128)(2,1)S(1)}, u32[]{:S(2)}, u32[]{:S(2)}) collective-permute-start(bf16[272,128]{1,0:T(8,128)(2,1)} %collective-permute-done.5), channel_id=1, source_target_pairs={{0,1},{1,0},{2,3},{3,2},{4,5},{5,4},{6,7},{7,6},{8,9},{9,8},{10,11... | collective-permute-start | bytes 208904 | tf_op jit(solution)/shard_map/ppermute | solution.py:225
  16.9 1.5 %collective-permute-start.10 = (bf16[272,128]{1,0:T(8,128)(2,1)}, bf16[272,128]{1,0:T(8,128)(2,1)S(1)}, u32[]{:S(2)}, u32[]{:S(2)}) collective-permute-start(bf16[272,128]{1,0:T(8,128)(2,1)} %collective-permute-done.9), channel_id=1, source_target_pairs={{0,1},{1,0},{2,3},{3,2},{4,5},{5,4},{6,7},{7,6},{8,9},{9,8},{10,11... | collective-permute-start | bytes 208904 | tf_op jit(solution)/shard_map/ppermute | solution.py:225
  20.0 9.4 %collective-permute-start.11 = (bf16[544,128]{1,0:T(8,128)(2,1)S(1)}, bf16[544,128]{1,0:T(8,128)(2,1)S(1)}, u32[]{:S(2)}, u32[]{:S(2)}) collective-permute-start(bf16[544,128]{1,0:T(8,128)(2,1)S(1)} %get-tuple-element.44), channel_id=1, source_target_pairs={{0,2},{1,3},{2,0},{3,1},{4,6},{5,7},{6,4},{7,5},{8,10},{9,11},{10,... | collective-permute-start | bytes 417800 | tf_op jit(solution)/shard_map/ppermute | solution.py:199
  21.7 8.9 %collective-permute-start.12 = (bf16[544,128]{1,0:T(8,128)(2,1)S(1)}, bf16[544,128]{1,0:T(8,128)(2,1)S(1)}, u32[]{:S(2)}, u32[]{:S(2)}) collective-permute-start(bf16[544,128]{1,0:T(8,128)(2,1)S(1)} %get-tuple-element.45), channel_id=1, source_target_pairs={{0,4},{1,5},{2,6},{3,7},{4,0},{5,1},{6,2},{7,3},{8,12},{9,13},{10,... | collective-permute-start | bytes 417800 | tf_op jit(solution)/shard_map/ppermute | solution.py:199
  24.3 8.8 %collective-permute-start.13 = (bf16[544,128]{1,0:T(8,128)(2,1)S(1)}, bf16[544,128]{1,0:T(8,128)(2,1)S(1)}, u32[]{:S(2)}, u32[]{:S(2)}) collective-permute-start(bf16[544,128]{1,0:T(8,128)(2,1)S(1)} %get-tuple-element.46), channel_id=1, source_target_pairs={{0,6},{1,7},{2,4},{3,5},{4,2},{5,3},{6,0},{7,1},{8,14},{9,15},{10,... | collective-permute-start | bytes 417800 | tf_op jit(solution)/shard_map/ppermute | solution.py:199
  25.5 8.4 %collective-permute-start.1 = (bf16[432,512]{1,0:T(8,128)(2,1)S(1)}, bf16[432,512]{1,0:T(8,128)(2,1)S(1)}, u32[]{:S(2)}, u32[]{:S(2)}) collective-permute-start(bf16[432,512]{1,0:T(8,128)(2,1)S(1)} %constant_dynamic-slice_fusion.1), channel_id=1, source_target_pairs={{0,16},{1,9},{2,18},{3,11},{4,20},{5,13},{6,22},{7,15},{8,24},{9,1... | collective-permute-start | bytes 1327112 | tf_op jit(solution)/shard_map/ppermute | solution.py:225
  27.4 11.8 %collective-permute-start.18 = (bf16[864,512]{1,0:T(8,128)(2,1)}, bf16[864,512]{1,0:T(8,128)(2,1)S(1)}, u32[]{:S(2)}, u32[]{:S(2)}) collective-permute-start(bf16[864,512]{1,0:T(8,128)(2,1)} %collective-permute-done), channel_id=1, source_target_pairs={{0,1},{1,0},{2,3},{3,2},{4,5},{5,4},{6,7},{7,6},{8,9},{9,8},{10,11... | collective-permute-start | bytes 2654216 | tf_op jit(solution)/shard_map/ppermute | solution.py:225
  29.5 13.9 %collective-permute-start.20 = (bf16[64,3456]{1,0:T(8,128)(2,1)S(1)}, bf16[64,3456]{1,0:T(8,128)(2,1)S(1)}, u32[]{:S(2)}, u32[]{:S(2)}) collective-permute-start(bf16[64,3456]{1,0:T(8,128)(2,1)S(1)} %constant_dynamic-slice_fusion), channel_id=1, source_target_pairs={{0,16},{1,9},{2,18},{3,11},{4,20},{5,13},{6,22},{7,15},{8,24},{9,1... | collective-permute-start | bytes 1327112 | tf_op jit(solution)/shard_map/ppermute | solution.py:225
  33.9 6.1 %collective-permute-start.19 = (bf16[432,512]{1,0:T(8,128)(2,1)S(1)}, bf16[432,512]{1,0:T(8,128)(2,1)S(1)}, u32[]{:S(2)}, u32[]{:S(2)}) collective-permute-start(bf16[432,512]{1,0:T(8,128)(2,1)S(1)} %collective-permute-done.1), channel_id=1, source_target_pairs={{0,1},{1,0},{2,3},{3,2},{4,5},{5,4},{6,7},{7,6},{8,9},{9,8},{10,11... | collective-permute-start | bytes 1327112 | tf_op jit(solution)/shard_map/ppermute | solution.py:225
  36.2 7.5 %collective-permute-start.21 = (bf16[128,3456]{1,0:T(8,128)(2,1)}, bf16[128,3456]{1,0:T(8,128)(2,1)S(1)}, u32[]{:S(2)}, u32[]{:S(2)}) collective-permute-start(bf16[128,3456]{1,0:T(8,128)(2,1)} %collective-permute-done.2), channel_id=1, source_target_pairs={{0,1},{1,0},{2,3},{3,2},{4,5},{5,4},{6,7},{7,6},{8,9},{9,8},{10,11... | collective-permute-start | bytes 2654216 | tf_op jit(solution)/shard_map/ppermute | solution.py:225
  37.5 2.0 %collective-permute-start.14 = (bf16[544,128]{1,0:T(8,128)(2,1)S(1)}, bf16[544,128]{1,0:T(8,128)(2,1)S(1)}, u32[]{:S(2)}, u32[]{:S(2)}) collective-permute-start(bf16[544,128]{1,0:T(8,128)(2,1)S(1)} %get-tuple-element.47.refs_0_), channel_id=1, source_target_pairs={{0,1},{1,0},{2,3},{3,2},{4,5},{5,4},{6,7},{7,6},{8,9},{9,8},{10,11... | collective-permute-start | bytes 417800 | tf_op jit(solution)/shard_map/ppermute | solution.py:225
  39.3 1.4 %collective-permute-start.15 = (bf16[544,128]{1,0:T(8,128)(2,1)S(1)}, bf16[544,128]{1,0:T(8,128)(2,1)S(1)}, u32[]{:S(2)}, u32[]{:S(2)}) collective-permute-start(bf16[544,128]{1,0:T(8,128)(2,1)S(1)} %collective-permute-done.11.refs_2_), channel_id=1, source_target_pairs={{0,1},{1,0},{2,3},{3,2},{4,5},{5,4},{6,7},{7,6},{8,9},{9,8},{10,11... | collective-permute-start | bytes 417800 | tf_op jit(solution)/shard_map/ppermute | solution.py:225
  39.5 1.5 %collective-permute-start.16 = (bf16[544,128]{1,0:T(8,128)(2,1)S(1)}, bf16[544,128]{1,0:T(8,128)(2,1)S(1)}, u32[]{:S(2)}, u32[]{:S(2)}) collective-permute-start(bf16[544,128]{1,0:T(8,128)(2,1)S(1)} %collective-permute-done.12.refs_4_), channel_id=1, source_target_pairs={{0,1},{1,0},{2,3},{3,2},{4,5},{5,4},{6,7},{7,6},{8,9},{9,8},{10,11... | collective-permute-start | bytes 417800 | tf_op jit(solution)/shard_map/ppermute | solution.py:225
  40.0 1.4 %collective-permute-start.17 = (bf16[544,128]{1,0:T(8,128)(2,1)S(1)}, bf16[544,128]{1,0:T(8,128)(2,1)S(1)}, u32[]{:S(2)}, u32[]{:S(2)}) collective-permute-start(bf16[544,128]{1,0:T(8,128)(2,1)S(1)} %collective-permute-done.13.refs_6_), channel_id=1, source_target_pairs={{0,1},{1,0},{2,3},{3,2},{4,5},{5,4},{6,7},{7,6},{8,9},{9,8},{10,11... | collective-permute-start | bytes 417800 | tf_op jit(solution)/shard_map/ppermute | solution.py:225
  43.4 1.9 %collective-permute-start.22 = (bf16[64,3456]{1,0:T(8,128)(2,1)S(1)}, bf16[64,3456]{1,0:T(8,128)(2,1)S(1)}, u32[]{:S(2)}, u32[]{:S(2)}) collective-permute-start(bf16[64,3456]{1,0:T(8,128)(2,1)S(1)} %collective-permute-done.20), channel_id=1, source_target_pairs={{0,1},{1,0},{2,3},{3,2},{4,5},{5,4},{6,7},{7,6},{8,9},{9,8},{10,11... | collective-permute-start | bytes 1327112 | tf_op jit(solution)/shard_map/ppermute | solution.py:225
  47.6 8.2 %collective-permute-start.23 = (bf16[512,128]{1,0:T(8,128)(2,1)S(1)}, bf16[512,128]{1,0:T(8,128)(2,1)S(1)}, u32[]{:S(2)}, u32[]{:S(2)}) collective-permute-start(bf16[512,128]{1,0:T(8,128)(2,1)S(1)} %get-tuple-element.59), channel_id=1, source_target_pairs={{0,6},{1,7},{2,4},{3,5},{4,2},{5,3},{6,0},{7,1},{8,14},{9,15},{10,... | collective-permute-start | bytes 393224 | tf_op jit(solution)/shard_map/ppermute | solution.py:199
  51.4 6.6 %collective-permute-start.25 = (bf16[512,128]{1,0:T(8,128)(2,1)S(1)}, bf16[512,128]{1,0:T(8,128)(2,1)S(1)}, u32[]{:S(2)}, u32[]{:S(2)}) collective-permute-start(bf16[512,128]{1,0:T(8,128)(2,1)S(1)} %get-tuple-element.65), channel_id=1, source_target_pairs={{0,2},{1,3},{2,0},{3,1},{4,6},{5,7},{6,4},{7,5},{8,10},{9,11},{10,... | collective-permute-start | bytes 393224 | tf_op jit(solution)/shard_map/ppermute | solution.py:199
  53.3 10.2 %collective-permute-start.27 = (bf16[512,128]{1,0:T(8,128)(2,1)S(1)}, bf16[512,128]{1,0:T(8,128)(2,1)S(1)}, u32[]{:S(2)}, u32[]{:S(2)}) collective-permute-start(bf16[512,128]{1,0:T(8,128)(2,1)S(1)} %get-tuple-element.66), channel_id=1, source_target_pairs={{0,4},{1,5},{2,6},{3,7},{4,0},{5,1},{6,2},{7,3},{8,12},{9,13},{10,... | collective-permute-start | bytes 393224 | tf_op jit(solution)/shard_map/ppermute | solution.py:199
  53.4 10.2 %collective-permute-start.24 = (bf16[512,128]{1,0:T(8,128)(2,1)S(1)}, bf16[512,128]{1,0:T(8,128)(2,1)S(1)}, u32[]{:S(2)}, u32[]{:S(2)}) collective-permute-start(bf16[512,128]{1,0:T(8,128)(2,1)S(1)} %get-tuple-element.64.refs_0_), channel_id=1, source_target_pairs={{0,1},{1,0},{2,3},{3,2},{4,5},{5,4},{6,7},{7,6},{8,9},{9,8},{10,11... | collective-permute-start | bytes 393224 | tf_op jit(solution)/shard_map/ppermute | solution.py:225
  55.8 7.7 %collective-permute-start.29 = (bf16[512,128]{1,0:T(8,128)(2,1)S(1)}, bf16[512,128]{1,0:T(8,128)(2,1)S(1)}, u32[]{:S(2)}, u32[]{:S(2)}) collective-permute-start(bf16[512,128]{1,0:T(8,128)(2,1)S(1)} %collective-permute-done.23.refs_6_), channel_id=1, source_target_pairs={{0,1},{1,0},{2,3},{3,2},{4,5},{5,4},{6,7},{7,6},{8,9},{9,8},{10,11... | collective-permute-start | bytes 393224 | tf_op jit(solution)/shard_map/ppermute | solution.py:225
  58.0 5.6 %collective-permute-start.26 = (bf16[512,128]{1,0:T(8,128)(2,1)S(1)}, bf16[512,128]{1,0:T(8,128)(2,1)S(1)}, u32[]{:S(2)}, u32[]{:S(2)}) collective-permute-start(bf16[512,128]{1,0:T(8,128)(2,1)S(1)} %collective-permute-done.25.refs_2_), channel_id=1, source_target_pairs={{0,1},{1,0},{2,3},{3,2},{4,5},{5,4},{6,7},{7,6},{8,9},{9,8},{10,11... | collective-permute-start | bytes 393224 | tf_op jit(solution)/shard_map/ppermute | solution.py:225
  65.5 4.3 %collective-permute-start.30 = (bf16[256,128]{1,0:T(8,128)(2,1)S(1)}, bf16[256,128]{1,0:T(8,128)(2,1)S(1)}, u32[]{:S(2)}, u32[]{:S(2)}) collective-permute-start(bf16[256,128]{1,0:T(8,128)(2,1)S(1)} %get-tuple-element.69), channel_id=1, source_target_pairs={{0,8},{8,0},{16,24},{24,16},{1,9},{9,1},{17,25},{25,17},{2,10},{10... | collective-permute-start | bytes 196616 | tf_op jit(solution)/shard_map/ppermute | solution.py:199
  66.2 4.3 %collective-permute-start.31 = (bf16[256,128]{1,0:T(8,128)(2,1)S(1)}, bf16[256,128]{1,0:T(8,128)(2,1)S(1)}, u32[]{:S(2)}, u32[]{:S(2)}) collective-permute-start(bf16[256,128]{1,0:T(8,128)(2,1)S(1)} %get-tuple-element.70), channel_id=1, source_target_pairs={{0,16},{8,24},{16,0},{24,8},{1,17},{9,25},{17,1},{25,9},{2,18},{10... | collective-permute-start | bytes 196616 | tf_op jit(solution)/shard_map/ppermute | solution.py:199
  67.5 5.2 %collective-permute-start.32 = (bf16[256,128]{1,0:T(8,128)(2,1)S(1)}, bf16[256,128]{1,0:T(8,128)(2,1)S(1)}, u32[]{:S(2)}, u32[]{:S(2)}) collective-permute-start(bf16[256,128]{1,0:T(8,128)(2,1)S(1)} %get-tuple-element.71), channel_id=1, source_target_pairs={{0,24},{8,16},{16,8},{24,0},{1,25},{9,17},{17,9},{25,1},{2,26},{10... | collective-permute-start | bytes 196616 | tf_op jit(solution)/shard_map/ppermute | solution.py:199
  (8 other events, 68.3 us)

commit v4 on v3

--- a/solution.py
+++ b/solution.py
@@ -200,7 +200,10 @@
 
 
 def exchange_chips(parts):
-    return [parts[0]] + [xor_permute(parts[k], "table", CORES * k) for k in range(1, len(parts))]
+    arrived = list(parts)
+    for k in range(1, len(parts)):
+        arrived[k] = xor_permute(parts[k], "table", CORES * k)
+    return arrived
 
 
 def exchange_cores(parts):
@@ -271,7 +274,6 @@
     samples, cross = cotangent.shape
     rank = cross_v.shape[1]
     relative = tables <= 8
-    bias = cross_bias.reshape(1, cross)
 
     part = jax.ShapeDtypeStruct((quota * size + meta_rows(quota), 128), BF16)
     hbm = pl.BlockSpec(memory_space=pltpu.HBM)
@@ -301,11 +303,6 @@
         across(opposite),
         sibling(across(sibling(hop_opposite))),
     ]
-    second_v = far(half_of(first_v))
-    first_u, first_v = lax.optimization_barrier((first_u, first_v))
-    other_v = sibling(first_v)
-    second_u = far(half_of(first_u))
-
     chips = tables // CORES
     listed = jax.ShapeDtypeStruct((CORES * (LIST * size + META), 128), BF16)
     *lists, index = pl.pallas_call(
@@ -322,6 +319,15 @@
         cost_estimate=pl.CostEstimate(flops=RELAY_FLOPS, bytes_accessed=0, transcendentals=0),
         name="relay",
     )(*parts)
+    half_v = half_of(first_v)
+    if relative:
+        half_v, lists[1] = lax.optimization_barrier((half_v, lists[1]))
+    second_v = far(half_v)
+    first_u, first_v = lax.optimization_barrier((first_u, first_v))
+    other_v = sibling(first_v)
+    second_u = far(half_of(first_u))
+    late_v, late_u, late_bias, lists[0] = lax.optimization_barrier((cross_v, cross_u, cross_bias, lists[0]))
+    bias = late_bias.reshape(1, cross)
     swap_u = first_u
     if relative:
         arrived = exchange_chips(lists)
@@ -329,7 +335,7 @@
         arrived = exchange_cores(arrived)
     else:
         arrived = exchange_whole(lists)
-    full_v = assemble(cross_v, first_v, other_v, second_v, sibling(second_v))
+    full_v = assemble(late_v, first_v, other_v, second_v, sibling(second_v))
 
     grad = jax.ShapeDtypeStruct((CORES * LIST * size, 128), BF16)
     first, scaled, slots, hidden = pl.pallas_call(
@@ -349,7 +355,7 @@
 
     if relative:
         second_u, scaled = lax.optimization_barrier((second_u, scaled))
-    full_u = assemble(cross_u, first_u, sibling(swap_u), second_u, sibling(second_u))
+    full_u = assemble(late_u, first_u, sibling(swap_u), second_u, sibling(second_u))
 
     half = chips // 2
     groups = (range(half, chips), range(half))
@@ -400,7 +406,9 @@
         compiler_params=params(32),
         name="back",
     )(index, *returned)
-    backs = [backs[0]] + [xor_permute(backs[k], "node", k) for k in range(1, nodes)]
+    backs = list(backs)
+    for k in range(1, nodes):
+        backs[k] = xor_permute(backs[k], "node", k)
 
     emb_grad = pl.pallas_call(
         functools.partial(rows_kernel, nodes, quota, size),

time: 74.7 us -> 72.5 us (0.971)
  waiting for transfers between devices: 19.4 us -> 28.5 us
  starting transfers between devices: 33.7 us -> 26.3 us
  local copies, waits for them, and re-layouts: 6.33 us -> 3.68 us
  Pallas kernels: 13.8 us -> 12.8 us
    ppermute x24, starting transfers between devices: 21.1 us -> 13.9 us  [permute(): return lax.ppermute(value, ('node', 'table'), pairs)]
    ppermute x24, waiting for transfers between devices: 6.15 us -> 10.9 us  [permute(): return lax.ppermute(value, ('node', 'table'), pairs)]
    ppermute x9, waiting for transfers between devices: 13.3 us -> 17.6 us  [xor_permute(): return lax.ppermute(value, axis, [(i, i ^ k) for i in range(size)])]
    dynamic_update_slice x10, local copies, waits for them, and re-layouts: 3.01 us -> 0.67 us  [assemble(): whole = lax.dynamic_update_slice(whole, piece, (row, 0))]
    dynamic_slice x2, local copies, waits for them, and re-layouts: 2.09 us -> 0.07 us  [half_of(): return lax.dynamic_slice(shard, (core * half, 0), (half, shard.shape[1]))]
    unnamed x14, local copies, waits for them, and re-layouts: 0.03 us -> 1.74 us
    pallas_call x1, Pallas kernels: 1.64 us -> 0.73 us  [body(): pl.pallas_call(functools.partial(relay_kernel, quota, size, tables, relat...]
  transfers between devices with their start and end apart: 33 -> 33, of which waited for: 15 -> 17; matrix products, arithmetic and copies ran while one was open for 8% -> 3% of each run, Pallas kernels for 13% -> 12%
where the time goes in v4:
time: 72.5 us; the launch traced here: 72.2 us
  waiting for transfers between devices  28.5 us (39%)
  starting transfers between devices  26.3 us (36%)
  Pallas kernels  12.8 us (18%)
  local copies, waits for them, and re-layouts  3.68 us (5%)
  between operations  0.87 us (1%)
    ppermute x9, waiting for transfers between devices, xor_permute(): return lax.ppermute(value, axis, [(i, i ^ k) for i in range(size)])  17.6 us
    ppermute x24, starting transfers between devices, permute(): return lax.ppermute(value, ('node', 'table'), pairs)  13.9 us
    ppermute x9, starting transfers between devices, xor_permute(): return lax.ppermute(value, axis, [(i, i ^ k) for i in range(size)])  12.4 us
    ppermute x24, waiting for transfers between devices, permute(): return lax.ppermute(value, ('node', 'table'), pairs)  10.9 us
    pallas_call x1, Pallas kernels, body(): pl.pallas_call(cross_kernel, out_shape=jax.ShapeDtypeStruct((samples, cro...  2.37 us
    pallas_call x1, Pallas kernels, body(): pl.pallas_call(functools.partial(owner_kernel, groups[0], size), out_shap...  2.35 us
    pallas_call x1, Pallas kernels, body(): pl.pallas_call(functools.partial(products_kernel, quota, size), out_shape...  2.04 us
    pallas_call x1, Pallas kernels, body(): pl.pallas_call(functools.partial(pool_kernel, tables, size), out_shape=[j...  1.95 us
  transfers between devices with their start and end apart: 33, of which 17 were waited for; matrix products, arithmetic and copies ran while one was open for 3% of the time, Pallas kernels for 12%

profile of v4, /device:TPU:0, one launch (start us, length us, event | category | flops | bytes accessed | tf_op | source)
XLA Modules:
  0.0 72.2 jit_solution(11846481631352329355)
XLA Ops:
  0.6 3.0 %collective-permute-start = (bf16[864,512]{1,0:T(8,128)(2,1)}, bf16[864,512]{1,0:T(8,128)(2,1)S(1)}, u32[]{:S(2)}, u32[]{:S(2)}) collective-permute-start(bf16[864,512]{1,0:T(8,128)(2,1)} %param.16), channel_id=1, source_target_pairs={{0,8},{1,17},{2,10},{3,19},{4,12},{5,21},{6,14},{7,23},{8,0},{9,25... | collective-permute-start | bytes 2654216 | tf_op jit(solution)/shard_map/ppermute | solution.py:228
  3.6 2.0 %products.1 = (bf16[272,128]{1,0:T(8,128)(2,1)}, bf16[272,128]{1,0:T(8,128)(2,1)}, bf16[272,128]{1,0:T(8,128)(2,1)}, bf16[272,128]{1,0:T(8,128)(2,1)}, bf16[272,128]{1,0:T(8,128)(2,1)}) custom-call(s32[8]{0:T(128)} %rows_ref.1, s32[8]{0:T(128)} %table_hbm.1, s32[8]{0:T(128)} %slot_hbm.1, bf16[512,128]{1,0:T(8,128)(2,1)} %emb_hbm.1, s32[8,128,128]{2,1,0:T(8,128)} %mult_ref.1), custom_call_target="tpu_custom_call" | custom-call | tf_op jit(solution)/shard_map/products/pallas_call | solution.py:280
  6.9 1.4 %collective-permute-start.1 = (bf16[272,128]{1,0:T(8,128)(2,1)}, bf16[272,128]{1,0:T(8,128)(2,1)S(1)}, u32[]{:S(2)}, u32[]{:S(2)}) collective-permute-start(bf16[272,128]{1,0:T(8,128)(2,1)} %get-tuple-element.44), channel_id=1, source_target_pairs={{0,16},{1,9},{2,18},{3,11},{4,20},{5,13},{6,22},{7,15},{8,24},{9,1... | collective-permute-start | bytes 208904 | tf_op jit(solution)/shard_map/ppermute | solution.py:228
  9.6 2.6 %collective-permute-done.1.refs_1_ = bf16[272,128]{1,0:T(8,128)(2,1)S(1)} collective-permute-done((bf16[272,128]{1,0:T(8,128)(2,1)}, bf16[272,128]{1,0:T(8,128)(2,1)S(1)}, u32[]{:S(2)}, u32[]{:S(2)}) %collective-permute-start.1) | collective-permute-done | bytes 69664 | tf_op jit(solution)/shard_map/ppermute | solution.py:228
  12.2 1.5 %collective-permute-start.5 = (bf16[272,128]{1,0:T(8,128)(2,1)}, bf16[272,128]{1,0:T(8,128)(2,1)S(1)}, u32[]{:S(2)}, u32[]{:S(2)}) collective-permute-start(bf16[272,128]{1,0:T(8,128)(2,1)} %get-tuple-element.46), channel_id=1, source_target_pairs={{0,0},{1,25},{2,2},{3,27},{4,4},{5,29},{6,6},{7,31},{8,8},{9,17},{... | collective-permute-start | bytes 208904 | tf_op jit(solution)/shard_map/ppermute | solution.py:228
  13.8 1.6 %collective-permute-start.4 = (bf16[272,128]{1,0:T(8,128)(2,1)S(1)}, bf16[272,128]{1,0:T(8,128)(2,1)S(1)}, u32[]{:S(2)}, u32[]{:S(2)}) collective-permute-start(bf16[272,128]{1,0:T(8,128)(2,1)S(1)} %collective-permute-done.3), channel_id=1, source_target_pairs={{0,1},{1,0},{2,3},{3,2},{4,5},{5,4},{6,7},{7,6},{8,9},{9,8},{10,11... | collective-permute-start | bytes 208904 | tf_op jit(solution)/shard_map/ppermute | solution.py:228
  16.7 0.9 %copy-done.2 = bf16[272,128]{1,0:T(8,128)(2,1)S(1)} copy-done((bf16[272,128]{1,0:T(8,128)(2,1)S(1)}, bf16[272,128]{1,0:T(8,128)(2,1)}, u32[]{:S(2)}) %copy-start.2) | copy-done | bytes 69656
  17.6 0.7 %relay.1 = (bf16[544,128]{1,0:T(8,128)(2,1)S(1)}, bf16[544,128]{1,0:T(8,128)(2,1)S(1)}, bf16[544,128]{1,0:T(8,128)(2,1)S(1)}, bf16[544,128]{1,0:T(8,128)(2,1)S(1)}, s32[8]{0:T(128)S(1)}) custom-call(bf16[272,128]{1,0:T(8,128)(2,1)S(1)} %copy-done.2, bf16[272,128]{1,0:T(8,128)(2,1)S(1)} %collective-permute-done.1.refs_1_, ...), custom_call_target="tpu_custom_call" | custom-call | flops 1000000 | tf_op jit(solution)/shard_map/relay/pallas_call | solution.py:308
  18.3 0.7 %reshape.7.bias_ref = f32[1,3456]{1,0:T(1,128)S(1)} reshape(f32[3456]{0:T(1024)} %param.18) | data formatting | bytes 27648 | tf_op jit(solution)/shard_map/reshape | solution.py:330
  19.1 2.7 %collective-permute-start.12 = (bf16[544,128]{1,0:T(8,128)(2,1)S(1)}, bf16[544,128]{1,0:T(8,128)(2,1)S(1)}, u32[]{:S(2)}, u32[]{:S(2)}) collective-permute-start(bf16[544,128]{1,0:T(8,128)(2,1)S(1)} %get-tuple-element.54), channel_id=1, source_target_pairs={{0,4},{1,5},{2,6},{3,7},{4,0},{5,1},{6,2},{7,3},{8,12},{9,13},{10,... | collective-permute-start | bytes 417800 | tf_op jit(solution)/shard_map/ppermute | solution.py:199
  21.7 1.3 %collective-permute-start.13 = (bf16[544,128]{1,0:T(8,128)(2,1)S(1)}, bf16[544,128]{1,0:T(8,128)(2,1)S(1)}, u32[]{:S(2)}, u32[]{:S(2)}) collective-permute-start(bf16[544,128]{1,0:T(8,128)(2,1)S(1)} %get-tuple-element.55), channel_id=1, source_target_pairs={{0,6},{1,7},{2,4},{3,5},{4,2},{5,3},{6,0},{7,1},{8,14},{9,15},{10,... | collective-permute-start | bytes 417800 | tf_op jit(solution)/shard_map/ppermute | solution.py:199
  23.7 0.8 %copy-done.6 = bf16[128,3456]{1,0:T(8,128)(2,1)S(1)} copy-done((bf16[128,3456]{1,0:T(8,128)(2,1)S(1)}, bf16[128,3456]{1,0:T(8,128)(2,1)}, u32[]{:S(2)}) %copy-start.6) | copy-done | bytes 884760
  25.4 1.9 %collective-permute-done.10 = bf16[128,3456]{1,0:T(8,128)(2,1)S(1)} collective-permute-done((bf16[128,3456]{1,0:T(8,128)(2,1)}, bf16[128,3456]{1,0:T(8,128)(2,1)S(1)}, u32[]{:S(2)}, u32[]{:S(2)}) %collective-permute-start.10) | collective-permute-done | bytes 884768 | tf_op jit(solution)/shard_map/ppermute | solution.py:228
  27.4 4.1 %collective-permute-done.12.refs_4_ = bf16[544,128]{1,0:T(8,128)(2,1)S(1)} collective-permute-done((bf16[544,128]{1,0:T(8,128)(2,1)S(1)}, bf16[544,128]{1,0:T(8,128)(2,1)S(1)}, u32[]{:S(2)}, u32[]{:S(2)}) %collective-permute-start.12) | collective-permute-done | bytes 139296 | tf_op jit(solution)/shard_map/ppermute | solution.py:199
  32.0 3.5 %collective-permute-done.11.refs_2_ = bf16[544,128]{1,0:T(8,128)(2,1)S(1)} collective-permute-done((bf16[544,128]{1,0:T(8,128)(2,1)S(1)}, bf16[544,128]{1,0:T(8,128)(2,1)S(1)}, u32[]{:S(2)}, u32[]{:S(2)}) %collective-permute-start.11) | collective-permute-done | bytes 139296 | tf_op jit(solution)/shard_map/ppermute | solution.py:199
  36.9 1.8 %collective-permute-done.14.refs_1_ = bf16[544,128]{1,0:T(8,128)(2,1)S(1)} collective-permute-done((bf16[544,128]{1,0:T(8,128)(2,1)S(1)}, bf16[544,128]{1,0:T(8,128)(2,1)S(1)}, u32[]{:S(2)}, u32[]{:S(2)}) %collective-permute-start.14) | collective-permute-done | bytes 139296 | tf_op jit(solution)/shard_map/ppermute | solution.py:228
  39.3 0.8 %collective-permute-done.16.refs_5_ = bf16[544,128]{1,0:T(8,128)(2,1)S(1)} collective-permute-done((bf16[544,128]{1,0:T(8,128)(2,1)S(1)}, bf16[544,128]{1,0:T(8,128)(2,1)S(1)}, u32[]{:S(2)}, u32[]{:S(2)}) %collective-permute-start.16) | collective-permute-done | bytes 139296 | tf_op jit(solution)/shard_map/ppermute | solution.py:228
  40.3 2.0 %pool.1 = (bf16[256,3456]{1,0:T(8,128)(2,1)S(1)}, bf16[256,3456]{1,0:T(8,128)(2,1)S(1)}, s32[16]{0:T(128)S(1)}, bf16[256,512]{1,0:T(8,128)(2,1)S(1)}) custom-call(bf16[544,128]{1,0:T(8,128)(2,1)S(1)} %get-tuple-element.56.refs_0_, bf16[544,128]{1,0:T(8,128)(2,1)S(1)} %collective-permute-done.14.refs_1_, ...), custom_call_target="tpu_custom_call" | custom-call | tf_op jit(solution)/shard_map/pool/pallas_call | solution.py:341
  42.8 1.3 %collective-permute-done.22 = bf16[64,3456]{1,0:T(8,128)(2,1)S(1)} collective-permute-done((bf16[64,3456]{1,0:T(8,128)(2,1)S(1)}, bf16[64,3456]{1,0:T(8,128)(2,1)S(1)}, u32[]{:S(2)}, u32[]{:S(2)}) %collective-permute-start.22) | collective-permute-done | bytes 442400 | tf_op jit(solution)/shard_map/ppermute | solution.py:228
  44.1 2.4 %owner.1 = (bf16[512,128]{1,0:T(8,128)(2,1)S(1)}, bf16[512,128]{1,0:T(8,128)(2,1)S(1)}, bf16[256,512]{1,0:T(8,128)(2,1)S(1)}) custom-call(s32[16]{0:T(128)S(1)} %get-tuple-element.63.slot_ref, bf16[256,512]{1,0:T(8,128)(2,1)S(1)} %get-tuple-element.64.hidden_ref, bf16[256,3456]{1,0:T(8,128)(2,1)S(1)} %get-tuple-element.66.scaled_ref, ...), custom_call_target="tpu_custom_call" | custom-call | tf_op jit(solution)/shard_map/owner/pallas_call | solution.py:362
  46.5 2.9 %collective-permute-start.23 = (bf16[512,128]{1,0:T(8,128)(2,1)S(1)}, bf16[512,128]{1,0:T(8,128)(2,1)S(1)}, u32[]{:S(2)}, u32[]{:S(2)}) collective-permute-start(bf16[512,128]{1,0:T(8,128)(2,1)S(1)} %get-tuple-element.71), channel_id=1, source_target_pairs={{0,6},{1,7},{2,4},{3,5},{4,2},{5,3},{6,0},{7,1},{8,14},{9,15},{10,... | collective-permute-start | bytes 393224 | tf_op jit(solution)/shard_map/ppermute | solution.py:199
  49.4 1.3 %blocks.1 = (bf16[512,128]{1,0:T(8,128)(2,1)S(1)}, bf16[512,128]{1,0:T(8,128)(2,1)S(1)}) custom-call(s32[16]{0:T(128)S(1)} %get-tuple-element.63.slot_ref, bf16[256,512]{1,0:T(8,128)(2,1)S(1)} %get-tuple-element.64.hidden_ref, bf16[256,512]{1,0:T(8,128)(2,1)S(1)} %get-tuple-element.75.dhidden_ref, ...), custom_call_target="tpu_custom_call" | custom-call | tf_op jit(solution)/shard_map/blocks/pallas_call | solution.py:370
  51.1 1.2 %collective-permute-start.27 = (bf16[512,128]{1,0:T(8,128)(2,1)S(1)}, bf16[512,128]{1,0:T(8,128)(2,1)S(1)}, u32[]{:S(2)}, u32[]{:S(2)}) collective-permute-start(bf16[512,128]{1,0:T(8,128)(2,1)S(1)} %get-tuple-element.78), channel_id=1, source_target_pairs={{0,4},{1,5},{2,6},{3,7},{4,0},{5,1},{6,2},{7,3},{8,12},{9,13},{10,... | collective-permute-start | bytes 393224 | tf_op jit(solution)/shard_map/ppermute | solution.py:199
  52.3 2.4 %cross.1 = bf16[256,3456]{1,0:T(8,128)(2,1)} custom-call(bf16[256,3456]{1,0:T(8,128)(2,1)S(1)} %get-tuple-element.72.first_ref, bf16[256,512]{1,0:T(8,128)(2,1)S(1)} %get-tuple-element.64.hidden_ref, bf16[512,3456]{1,0:T(8,128)(2,1)S(1)} %constant_dynamic-update-slice_fusion.u_ref, f32[1,3456]{1,0:T(1,128)S(1)} %reshape.7.bias_ref), custom_call_target="tpu_custom_call" | custom-call | flops 905969664 | bytes 7077888 | tf_op jit(solution)/shard_map/cross/pallas_call | solution.py:380
  55.2 2.9 %collective-permute-done.25.refs_2_ = bf16[512,128]{1,0:T(8,128)(2,1)S(1)} collective-permute-done((bf16[512,128]{1,0:T(8,128)(2,1)S(1)}, bf16[512,128]{1,0:T(8,128)(2,1)S(1)}, u32[]{:S(2)}, u32[]{:S(2)}) %collective-permute-start.25) | collective-permute-done | bytes 131104 | tf_op jit(solution)/shard_map/ppermute | solution.py:199
  58.1 3.5 %collective-permute-done.27.refs_4_ = bf16[512,128]{1,0:T(8,128)(2,1)S(1)} collective-permute-done((bf16[512,128]{1,0:T(8,128)(2,1)S(1)}, bf16[512,128]{1,0:T(8,128)(2,1)S(1)}, u32[]{:S(2)}, u32[]{:S(2)}) %collective-permute-start.27) | collective-permute-done | bytes 131104 | tf_op jit(solution)/shard_map/ppermute | solution.py:199
  61.6 1.3 %collective-permute-done.28.refs_5_ = bf16[512,128]{1,0:T(8,128)(2,1)S(1)} collective-permute-done((bf16[512,128]{1,0:T(8,128)(2,1)S(1)}, bf16[512,128]{1,0:T(8,128)(2,1)S(1)}, u32[]{:S(2)}, u32[]{:S(2)}) %collective-permute-start.28) | collective-permute-done | bytes 131104 | tf_op jit(solution)/shard_map/ppermute | solution.py:228
  64.1 1.4 %collective-permute-start.31 = (bf16[256,128]{1,0:T(8,128)(2,1)S(1)}, bf16[256,128]{1,0:T(8,128)(2,1)S(1)}, u32[]{:S(2)}, u32[]{:S(2)}) collective-permute-start(bf16[256,128]{1,0:T(8,128)(2,1)S(1)} %get-tuple-element.82), channel_id=1, source_target_pairs={{0,16},{8,24},{16,0},{24,8},{1,17},{9,25},{17,1},{25,9},{2,18},{10... | collective-permute-start | bytes 196616 | tf_op jit(solution)/shard_map/ppermute | solution.py:199
  65.5 1.6 %collective-permute-start.32 = (bf16[256,128]{1,0:T(8,128)(2,1)S(1)}, bf16[256,128]{1,0:T(8,128)(2,1)S(1)}, u32[]{:S(2)}, u32[]{:S(2)}) collective-permute-start(bf16[256,128]{1,0:T(8,128)(2,1)S(1)} %get-tuple-element.83), channel_id=1, source_target_pairs={{0,24},{8,16},{16,8},{24,0},{1,25},{9,17},{17,9},{25,1},{2,26},{10... | collective-permute-start | bytes 196616 | tf_op jit(solution)/shard_map/ppermute | solution.py:199
  67.1 0.9 %collective-permute-done.30.refs_1_ = bf16[256,128]{1,0:T(8,128)(2,1)S(1)} collective-permute-done((bf16[256,128]{1,0:T(8,128)(2,1)S(1)}, bf16[256,128]{1,0:T(8,128)(2,1)S(1)}, u32[]{:S(2)}, u32[]{:S(2)}) %collective-permute-start.30) | collective-permute-done | bytes 65568 | tf_op jit(solution)/shard_map/ppermute | solution.py:199
  68.4 2.2 %collective-permute-done.32.refs_3_ = bf16[256,128]{1,0:T(8,128)(2,1)S(1)} collective-permute-done((bf16[256,128]{1,0:T(8,128)(2,1)S(1)}, bf16[256,128]{1,0:T(8,128)(2,1)S(1)}, u32[]{:S(2)}, u32[]{:S(2)}) %collective-permute-start.32) | collective-permute-done | bytes 65568 | tf_op jit(solution)/shard_map/ppermute | solution.py:199
  70.6 1.5 %rows.1 = f32[512,128]{1,0:T(8,128)} custom-call(s32[8]{0:T(128)S(1)} %copy-done.4, s32[8,128,128]{2,1,0:T(8,128)S(1)} %copy-done.1, bf16[256,128]{1,0:T(8,128)(2,1)S(1)} %get-tuple-element.80.refs_0_, bf16[256,128]{1,0:T(8,128)(2,1)S(1)} %collective-permute-done.30.refs_1_, bf16[256,128]{1,0:T(8,128)(2,1)S(1)} %collective-permute-done.31.refs_2_, ...), custom_call_target="tpu_custom_call" | custom-call | tf_op jit(solution)/shard_map/rows/pallas_call | solution.py:413
  (71 shorter events, 11.2 us)
Async XLA Ops:
  0.6 24.0 %collective-permute-start = (bf16[864,512]{1,0:T(8,128)(2,1)}, bf16[864,512]{1,0:T(8,128)(2,1)S(1)}, u32[]{:S(2)}, u32[]{:S(2)}) collective-permute-start(bf16[864,512]{1,0:T(8,128)(2,1)} %param.16), channel_id=1, source_target_pairs={{0,8},{1,17},{2,10},{3,19},{4,12},{5,21},{6,14},{7,23},{8,0},{9,25... | collective-permute-start | bytes 2654216 | tf_op jit(solution)/shard_map/ppermute | solution.py:228
  5.7 2.6 %collective-permute-start.2 = (bf16[272,128]{1,0:T(8,128)(2,1)}, bf16[272,128]{1,0:T(8,128)(2,1)S(1)}, u32[]{:S(2)}, u32[]{:S(2)}) collective-permute-start(bf16[272,128]{1,0:T(8,128)(2,1)} %get-tuple-element.45), channel_id=1, source_target_pairs={{0,1},{1,0},{2,3},{3,2},{4,5},{5,4},{6,7},{7,6},{8,9},{9,8},{10,11... | collective-permute-start | bytes 208904 | tf_op jit(solution)/shard_map/ppermute | solution.py:228
  5.8 3.2 %collective-permute-start.6 = (bf16[272,128]{1,0:T(8,128)(2,1)}, bf16[272,128]{1,0:T(8,128)(2,1)S(1)}, u32[]{:S(2)}, u32[]{:S(2)}) collective-permute-start(bf16[272,128]{1,0:T(8,128)(2,1)} %get-tuple-element.47), channel_id=1, source_target_pairs={{0,1},{1,0},{2,3},{3,2},{4,5},{5,4},{6,7},{7,6},{8,9},{9,8},{10,11... | collective-permute-start | bytes 208904 | tf_op jit(solution)/shard_map/ppermute | solution.py:228
  6.3 21.1 %collective-permute-start.10 = (bf16[128,3456]{1,0:T(8,128)(2,1)}, bf16[128,3456]{1,0:T(8,128)(2,1)S(1)}, u32[]{:S(2)}, u32[]{:S(2)}) collective-permute-start(bf16[128,3456]{1,0:T(8,128)(2,1)} %param.17), channel_id=1, source_target_pairs={{0,8},{1,17},{2,10},{3,19},{4,12},{5,21},{6,14},{7,23},{8,0},{9,25... | collective-permute-start | bytes 2654216 | tf_op jit(solution)/shard_map/ppermute | solution.py:228
  6.9 5.3 %collective-permute-start.1 = (bf16[272,128]{1,0:T(8,128)(2,1)}, bf16[272,128]{1,0:T(8,128)(2,1)S(1)}, u32[]{:S(2)}, u32[]{:S(2)}) collective-permute-start(bf16[272,128]{1,0:T(8,128)(2,1)} %get-tuple-element.44), channel_id=1, source_target_pairs={{0,16},{1,9},{2,18},{3,11},{4,20},{5,13},{6,22},{7,15},{8,24},{9,1... | collective-permute-start | bytes 208904 | tf_op jit(solution)/shard_map/ppermute | solution.py:228
  8.3 5.4 %collective-permute-start.3 = (bf16[272,128]{1,0:T(8,128)(2,1)S(1)}, bf16[272,128]{1,0:T(8,128)(2,1)S(1)}, u32[]{:S(2)}, u32[]{:S(2)}) collective-permute-start(bf16[272,128]{1,0:T(8,128)(2,1)S(1)} %collective-permute-done.2), channel_id=1, source_target_pairs={{0,16},{1,9},{2,18},{3,11},{4,20},{5,13},{6,22},{7,15},{8,24},{9,1... | collective-permute-start | bytes 208904 | tf_op jit(solution)/shard_map/ppermute | solution.py:228
  8.9 6.4 %collective-permute-start.7 = (bf16[272,128]{1,0:T(8,128)(2,1)S(1)}, bf16[272,128]{1,0:T(8,128)(2,1)S(1)}, u32[]{:S(2)}, u32[]{:S(2)}) collective-permute-start(bf16[272,128]{1,0:T(8,128)(2,1)S(1)} %collective-permute-done.6), channel_id=1, source_target_pairs={{0,0},{1,25},{2,2},{3,27},{4,4},{5,29},{6,6},{7,31},{8,8},{9,17},{... | collective-permute-start | bytes 208904 | tf_op jit(solution)/shard_map/ppermute | solution.py:228
  12.2 3.6 %collective-permute-start.5 = (bf16[272,128]{1,0:T(8,128)(2,1)}, bf16[272,128]{1,0:T(8,128)(2,1)S(1)}, u32[]{:S(2)}, u32[]{:S(2)}) collective-permute-start(bf16[272,128]{1,0:T(8,128)(2,1)} %get-tuple-element.46), channel_id=1, source_target_pairs={{0,0},{1,25},{2,2},{3,27},{4,4},{5,29},{6,6},{7,31},{8,8},{9,17},{... | collective-permute-start | bytes 208904 | tf_op jit(solution)/shard_map/ppermute | solution.py:228
  13.8 2.5 %collective-permute-start.4 = (bf16[272,128]{1,0:T(8,128)(2,1)S(1)}, bf16[272,128]{1,0:T(8,128)(2,1)S(1)}, u32[]{:S(2)}, u32[]{:S(2)}) collective-permute-start(bf16[272,128]{1,0:T(8,128)(2,1)S(1)} %collective-permute-done.3), channel_id=1, source_target_pairs={{0,1},{1,0},{2,3},{3,2},{4,5},{5,4},{6,7},{7,6},{8,9},{9,8},{10,11... | collective-permute-start | bytes 208904 | tf_op jit(solution)/shard_map/ppermute | solution.py:228
  15.3 1.4 %collective-permute-start.8 = (bf16[272,128]{1,0:T(8,128)(2,1)S(1)}, bf16[272,128]{1,0:T(8,128)(2,1)S(1)}, u32[]{:S(2)}, u32[]{:S(2)}) collective-permute-start(bf16[272,128]{1,0:T(8,128)(2,1)S(1)} %collective-permute-done.7), channel_id=1, source_target_pairs={{0,1},{1,0},{2,3},{3,2},{4,5},{5,4},{6,7},{7,6},{8,9},{9,8},{10,11... | collective-permute-start | bytes 208904 | tf_op jit(solution)/shard_map/ppermute | solution.py:228
  19.1 12.4 %collective-permute-start.12 = (bf16[544,128]{1,0:T(8,128)(2,1)S(1)}, bf16[544,128]{1,0:T(8,128)(2,1)S(1)}, u32[]{:S(2)}, u32[]{:S(2)}) collective-permute-start(bf16[544,128]{1,0:T(8,128)(2,1)S(1)} %get-tuple-element.54), channel_id=1, source_target_pairs={{0,4},{1,5},{2,6},{3,7},{4,0},{5,1},{6,2},{7,3},{8,12},{9,13},{10,... | collective-permute-start | bytes 417800 | tf_op jit(solution)/shard_map/ppermute | solution.py:199
  21.7 10.3 %collective-permute-start.13 = (bf16[544,128]{1,0:T(8,128)(2,1)S(1)}, bf16[544,128]{1,0:T(8,128)(2,1)S(1)}, u32[]{:S(2)}, u32[]{:S(2)}) collective-permute-start(bf16[544,128]{1,0:T(8,128)(2,1)S(1)} %get-tuple-element.55), channel_id=1, source_target_pairs={{0,6},{1,7},{2,4},{3,5},{4,2},{5,3},{6,0},{7,1},{8,14},{9,15},{10,... | collective-permute-start | bytes 417800 | tf_op jit(solution)/shard_map/ppermute | solution.py:199
  24.7 10.8 %collective-permute-start.11 = (bf16[544,128]{1,0:T(8,128)(2,1)S(1)}, bf16[544,128]{1,0:T(8,128)(2,1)S(1)}, u32[]{:S(2)}, u32[]{:S(2)}) collective-permute-start(bf16[544,128]{1,0:T(8,128)(2,1)S(1)} %get-tuple-element.53), channel_id=1, source_target_pairs={{0,2},{1,3},{2,0},{3,1},{4,6},{5,7},{6,4},{7,5},{8,10},{9,11},{10,... | collective-permute-start | bytes 417800 | tf_op jit(solution)/shard_map/ppermute | solution.py:199
  24.9 10.5 %collective-permute-start.9 = (bf16[432,512]{1,0:T(8,128)(2,1)S(1)}, bf16[432,512]{1,0:T(8,128)(2,1)S(1)}, u32[]{:S(2)}, u32[]{:S(2)}) collective-permute-start(bf16[432,512]{1,0:T(8,128)(2,1)S(1)} %constant_dynamic-slice_fusion.1), channel_id=1, source_target_pairs={{0,16},{1,9},{2,18},{3,11},{4,20},{5,13},{6,22},{7,15},{8,24},{9,1... | collective-permute-start | bytes 1327112 | tf_op jit(solution)/shard_map/ppermute | solution.py:228
  27.3 9.1 %collective-permute-start.18 = (bf16[864,512]{1,0:T(8,128)(2,1)S(1)}, bf16[864,512]{1,0:T(8,128)(2,1)S(1)}, u32[]{:S(2)}, u32[]{:S(2)}) collective-permute-start(bf16[864,512]{1,0:T(8,128)(2,1)S(1)} %collective-permute-done), channel_id=1, source_target_pairs={{0,1},{1,0},{2,3},{3,2},{4,5},{5,4},{6,7},{7,6},{8,9},{9,8},{10,11... | collective-permute-start | bytes 2654216 | tf_op jit(solution)/shard_map/ppermute | solution.py:228
  31.5 10.8 %collective-permute-start.20 = (bf16[64,3456]{1,0:T(8,128)(2,1)S(1)}, bf16[64,3456]{1,0:T(8,128)(2,1)S(1)}, u32[]{:S(2)}, u32[]{:S(2)}) collective-permute-start(bf16[64,3456]{1,0:T(8,128)(2,1)S(1)} %constant_dynamic-slice_fusion), channel_id=1, source_target_pairs={{0,16},{1,9},{2,18},{3,11},{4,20},{5,13},{6,22},{7,15},{8,24},{9,1... | collective-permute-start | bytes 1327112 | tf_op jit(solution)/shard_map/ppermute | solution.py:228
  35.5 3.5 %collective-permute-start.19 = (bf16[432,512]{1,0:T(8,128)(2,1)S(1)}, bf16[432,512]{1,0:T(8,128)(2,1)S(1)}, u32[]{:S(2)}, u32[]{:S(2)}) collective-permute-start(bf16[432,512]{1,0:T(8,128)(2,1)S(1)} %collective-permute-done.9), channel_id=1, source_target_pairs={{0,1},{1,0},{2,3},{3,2},{4,5},{5,4},{6,7},{7,6},{8,9},{9,8},{10,11... | collective-permute-start | bytes 1327112 | tf_op jit(solution)/shard_map/ppermute | solution.py:228
  35.7 7.0 %collective-permute-start.21 = (bf16[128,3456]{1,0:T(8,128)(2,1)S(1)}, bf16[128,3456]{1,0:T(8,128)(2,1)S(1)}, u32[]{:S(2)}, u32[]{:S(2)}) collective-permute-start(bf16[128,3456]{1,0:T(8,128)(2,1)S(1)} %collective-permute-done.10), channel_id=1, source_target_pairs={{0,1},{1,0},{2,3},{3,2},{4,5},{5,4},{6,7},{7,6},{8,9},{9,8},{10,11... | collective-permute-start | bytes 2654216 | tf_op jit(solution)/shard_map/ppermute | solution.py:228
  36.1 2.6 %collective-permute-start.14 = (bf16[544,128]{1,0:T(8,128)(2,1)S(1)}, bf16[544,128]{1,0:T(8,128)(2,1)S(1)}, u32[]{:S(2)}, u32[]{:S(2)}) collective-permute-start(bf16[544,128]{1,0:T(8,128)(2,1)S(1)} %get-tuple-element.56.refs_0_), channel_id=1, source_target_pairs={{0,1},{1,0},{2,3},{3,2},{4,5},{5,4},{6,7},{7,6},{8,9},{9,8},{10,11... | collective-permute-start | bytes 417800 | tf_op jit(solution)/shard_map/ppermute | solution.py:228
  36.4 2.9 %collective-permute-start.15 = (bf16[544,128]{1,0:T(8,128)(2,1)S(1)}, bf16[544,128]{1,0:T(8,128)(2,1)S(1)}, u32[]{:S(2)}, u32[]{:S(2)}) collective-permute-start(bf16[544,128]{1,0:T(8,128)(2,1)S(1)} %collective-permute-done.11.refs_2_), channel_id=1, source_target_pairs={{0,1},{1,0},{2,3},{3,2},{4,5},{5,4},{6,7},{7,6},{8,9},{9,8},{10,11... | collective-permute-start | bytes 417800 | tf_op jit(solution)/shard_map/ppermute | solution.py:228
  38.7 1.4 %collective-permute-start.16 = (bf16[544,128]{1,0:T(8,128)(2,1)S(1)}, bf16[544,128]{1,0:T(8,128)(2,1)S(1)}, u32[]{:S(2)}, u32[]{:S(2)}) collective-permute-start(bf16[544,128]{1,0:T(8,128)(2,1)S(1)} %collective-permute-done.12.refs_4_), channel_id=1, source_target_pairs={{0,1},{1,0},{2,3},{3,2},{4,5},{5,4},{6,7},{7,6},{8,9},{9,8},{10,11... | collective-permute-start | bytes 417800 | tf_op jit(solution)/shard_map/ppermute | solution.py:228
  38.9 1.4 %collective-permute-start.17 = (bf16[544,128]{1,0:T(8,128)(2,1)S(1)}, bf16[544,128]{1,0:T(8,128)(2,1)S(1)}, u32[]{:S(2)}, u32[]{:S(2)}) collective-permute-start(bf16[544,128]{1,0:T(8,128)(2,1)S(1)} %collective-permute-done.13.refs_6_), channel_id=1, source_target_pairs={{0,1},{1,0},{2,3},{3,2},{4,5},{5,4},{6,7},{7,6},{8,9},{9,8},{10,11... | collective-permute-start | bytes 417800 | tf_op jit(solution)/shard_map/ppermute | solution.py:228
  42.3 1.9 %collective-permute-start.22 = (bf16[64,3456]{1,0:T(8,128)(2,1)S(1)}, bf16[64,3456]{1,0:T(8,128)(2,1)S(1)}, u32[]{:S(2)}, u32[]{:S(2)}) collective-permute-start(bf16[64,3456]{1,0:T(8,128)(2,1)S(1)} %collective-permute-done.20), channel_id=1, source_target_pairs={{0,1},{1,0},{2,3},{3,2},{4,5},{5,4},{6,7},{7,6},{8,9},{9,8},{10,11... | collective-permute-start | bytes 1327112 | tf_op jit(solution)/shard_map/ppermute | solution.py:228
  46.5 8.2 %collective-permute-start.23 = (bf16[512,128]{1,0:T(8,128)(2,1)S(1)}, bf16[512,128]{1,0:T(8,128)(2,1)S(1)}, u32[]{:S(2)}, u32[]{:S(2)}) collective-permute-start(bf16[512,128]{1,0:T(8,128)(2,1)S(1)} %get-tuple-element.71), channel_id=1, source_target_pairs={{0,6},{1,7},{2,4},{3,5},{4,2},{5,3},{6,0},{7,1},{8,14},{9,15},{10,... | collective-permute-start | bytes 393224 | tf_op jit(solution)/shard_map/ppermute | solution.py:199
  50.6 7.4 %collective-permute-start.25 = (bf16[512,128]{1,0:T(8,128)(2,1)S(1)}, bf16[512,128]{1,0:T(8,128)(2,1)S(1)}, u32[]{:S(2)}, u32[]{:S(2)}) collective-permute-start(bf16[512,128]{1,0:T(8,128)(2,1)S(1)} %get-tuple-element.77), channel_id=1, source_target_pairs={{0,2},{1,3},{2,0},{3,1},{4,6},{5,7},{6,4},{7,5},{8,10},{9,11},{10,... | collective-permute-start | bytes 393224 | tf_op jit(solution)/shard_map/ppermute | solution.py:199
  51.1 10.5 %collective-permute-start.27 = (bf16[512,128]{1,0:T(8,128)(2,1)S(1)}, bf16[512,128]{1,0:T(8,128)(2,1)S(1)}, u32[]{:S(2)}, u32[]{:S(2)}) collective-permute-start(bf16[512,128]{1,0:T(8,128)(2,1)S(1)} %get-tuple-element.78), channel_id=1, source_target_pairs={{0,4},{1,5},{2,6},{3,7},{4,0},{5,1},{6,2},{7,3},{8,12},{9,13},{10,... | collective-permute-start | bytes 393224 | tf_op jit(solution)/shard_map/ppermute | solution.py:199
  52.3 9.3 %collective-permute-start.24 = (bf16[512,128]{1,0:T(8,128)(2,1)S(1)}, bf16[512,128]{1,0:T(8,128)(2,1)S(1)}, u32[]{:S(2)}, u32[]{:S(2)}) collective-permute-start(bf16[512,128]{1,0:T(8,128)(2,1)S(1)} %get-tuple-element.76.refs_0_), channel_id=1, source_target_pairs={{0,1},{1,0},{2,3},{3,2},{4,5},{5,4},{6,7},{7,6},{8,9},{9,8},{10,11... | collective-permute-start | bytes 393224 | tf_op jit(solution)/shard_map/ppermute | solution.py:228
  54.7 6.9 %collective-permute-start.29 = (bf16[512,128]{1,0:T(8,128)(2,1)S(1)}, bf16[512,128]{1,0:T(8,128)(2,1)S(1)}, u32[]{:S(2)}, u32[]{:S(2)}) collective-permute-start(bf16[512,128]{1,0:T(8,128)(2,1)S(1)} %collective-permute-done.23.refs_6_), channel_id=1, source_target_pairs={{0,1},{1,0},{2,3},{3,2},{4,5},{5,4},{6,7},{7,6},{8,9},{9,8},{10,11... | collective-permute-start | bytes 393224 | tf_op jit(solution)/shard_map/ppermute | solution.py:228
  58.0 3.6 %collective-permute-start.26 = (bf16[512,128]{1,0:T(8,128)(2,1)S(1)}, bf16[512,128]{1,0:T(8,128)(2,1)S(1)}, u32[]{:S(2)}, u32[]{:S(2)}) collective-permute-start(bf16[512,128]{1,0:T(8,128)(2,1)S(1)} %collective-permute-done.25.refs_2_), channel_id=1, source_target_pairs={{0,1},{1,0},{2,3},{3,2},{4,5},{5,4},{6,7},{7,6},{8,9},{9,8},{10,11... | collective-permute-start | bytes 393224 | tf_op jit(solution)/shard_map/ppermute | solution.py:228
  63.5 4.5 %collective-permute-start.30 = (bf16[256,128]{1,0:T(8,128)(2,1)S(1)}, bf16[256,128]{1,0:T(8,128)(2,1)S(1)}, u32[]{:S(2)}, u32[]{:S(2)}) collective-permute-start(bf16[256,128]{1,0:T(8,128)(2,1)S(1)} %get-tuple-element.81), channel_id=1, source_target_pairs={{0,8},{8,0},{16,24},{24,16},{1,9},{9,1},{17,25},{25,17},{2,10},{10... | collective-permute-start | bytes 196616 | tf_op jit(solution)/shard_map/ppermute | solution.py:199
  64.1 4.3 %collective-permute-start.31 = (bf16[256,128]{1,0:T(8,128)(2,1)S(1)}, bf16[256,128]{1,0:T(8,128)(2,1)S(1)}, u32[]{:S(2)}, u32[]{:S(2)}) collective-permute-start(bf16[256,128]{1,0:T(8,128)(2,1)S(1)} %get-tuple-element.82), channel_id=1, source_target_pairs={{0,16},{8,24},{16,0},{24,8},{1,17},{9,25},{17,1},{25,9},{2,18},{10... | collective-permute-start | bytes 196616 | tf_op jit(solution)/shard_map/ppermute | solution.py:199
  65.5 5.2 %collective-permute-start.32 = (bf16[256,128]{1,0:T(8,128)(2,1)S(1)}, bf16[256,128]{1,0:T(8,128)(2,1)S(1)}, u32[]{:S(2)}, u32[]{:S(2)}) collective-permute-start(bf16[256,128]{1,0:T(8,128)(2,1)S(1)} %get-tuple-element.83), channel_id=1, source_target_pairs={{0,24},{8,16},{16,8},{24,0},{1,25},{9,17},{17,9},{25,1},{2,26},{10... | collective-permute-start | bytes 196616 | tf_op jit(solution)/shard_map/ppermute | solution.py:199
  (8 other events, 71.6 us)

commit v5 on v4

--- a/solution.py
+++ b/solution.py
@@ -323,10 +323,11 @@
     if relative:
         half_v, lists[1] = lax.optimization_barrier((half_v, lists[1]))
     second_v = far(half_v)
-    first_u, first_v = lax.optimization_barrier((first_u, first_v))
+    first_u, first_v, late_v, late_u, late_bias = lax.optimization_barrier(
+        (first_u, first_v, cross_v, cross_u, cross_bias)
+    )
     other_v = sibling(first_v)
     second_u = far(half_of(first_u))
-    late_v, late_u, late_bias, lists[0] = lax.optimization_barrier((cross_v, cross_u, cross_bias, lists[0]))
     bias = late_bias.reshape(1, cross)
     swap_u = first_u
     if relative:

time: 72.5 us -> 71.7 us (0.989)
  starting transfers between devices: 26.3 us -> 30.3 us
  waiting for transfers between devices: 28.5 us -> 25.3 us
  local copies, waits for them, and re-layouts: 3.68 us -> 2.15 us
    ppermute x24, starting transfers between devices: 13.9 us -> 17.8 us  [permute(): return lax.ppermute(value, ('node', 'table'), pairs)]
    ppermute x9, waiting for transfers between devices: 17.6 us -> 13.9 us  [xor_permute(): return lax.ppermute(value, axis, [(i, i ^ k) for i in range(size)])]
    unnamed x14 -> x16, local copies, waits for them, and re-layouts: 1.74 us -> 0.92 us
  transfers between devices with their start and end apart: 33 -> 33, of which waited for: 17 -> 17; matrix products, arithmetic and copies ran while one was open for 3% -> 2% of each run, Pallas kernels for 12% -> 12%
where the time goes in v5:
time: 71.7 us; the launch traced here: 71.5 us
  starting transfers between devices  30.3 us (42%)
  waiting for transfers between devices  25.3 us (35%)
  Pallas kernels  12.9 us (18%)
  local copies, waits for them, and re-layouts  2.15 us (3%)
  between operations  0.9 us (1%)
    ppermute x24, starting transfers between devices, permute(): return lax.ppermute(value, ('node', 'table'), pairs)  17.8 us
    ppermute x9, waiting for transfers between devices, xor_permute(): return lax.ppermute(value, axis, [(i, i ^ k) for i in range(size)])  13.9 us
    ppermute x9, starting transfers between devices, xor_permute(): return lax.ppermute(value, axis, [(i, i ^ k) for i in range(size)])  12.5 us
    ppermute x24, waiting for transfers between devices, permute(): return lax.ppermute(value, ('node', 'table'), pairs)  11.4 us
    pallas_call x1, Pallas kernels, body(): pl.pallas_call(cross_kernel, out_shape=jax.ShapeDtypeStruct((samples, cro...  2.41 us
    pallas_call x1, Pallas kernels, body(): pl.pallas_call(functools.partial(owner_kernel, groups[0], size), out_shap...  2.35 us
    pallas_call x1, Pallas kernels, body(): pl.pallas_call(functools.partial(products_kernel, quota, size), out_shape...  2.04 us
    pallas_call x1, Pallas kernels, body(): pl.pallas_call(functools.partial(pool_kernel, tables, size), out_shape=[j...  1.98 us
  transfers between devices with their start and end apart: 33, of which 17 were waited for; matrix products, arithmetic and copies ran while one was open for 2% of the time, Pallas kernels for 12%

profile of v5, /device:TPU:0, one launch (start us, length us, event | category | flops | bytes accessed | tf_op | source)
XLA Modules:
  0.0 71.5 jit_solution(12893746034487465354)
XLA Ops:
  0.6 3.0 %collective-permute-start = (bf16[864,512]{1,0:T(8,128)(2,1)}, bf16[864,512]{1,0:T(8,128)(2,1)S(1)}, u32[]{:S(2)}, u32[]{:S(2)}) collective-permute-start(bf16[864,512]{1,0:T(8,128)(2,1)} %param.16), channel_id=1, source_target_pairs={{0,8},{1,17},{2,10},{3,19},{4,12},{5,21},{6,14},{7,23},{8,0},{9,25... | collective-permute-start | bytes 2654216 | tf_op jit(solution)/shard_map/ppermute | solution.py:228
  3.7 2.0 %products.1 = (bf16[272,128]{1,0:T(8,128)(2,1)}, bf16[272,128]{1,0:T(8,128)(2,1)}, bf16[272,128]{1,0:T(8,128)(2,1)}, bf16[272,128]{1,0:T(8,128)(2,1)}, bf16[272,128]{1,0:T(8,128)(2,1)}) custom-call(s32[8]{0:T(128)} %rows_ref.1, s32[8]{0:T(128)} %table_hbm.1, s32[8]{0:T(128)} %slot_hbm.1, bf16[512,128]{1,0:T(8,128)(2,1)} %emb_hbm.1, s32[8,128,128]{2,1,0:T(8,128)} %mult_ref.1), custom_call_target="tpu_custom_call" | custom-call | tf_op jit(solution)/shard_map/products/pallas_call | solution.py:280
  6.3 2.0 %collective-permute-start.1 = (bf16[272,128]{1,0:T(8,128)(2,1)}, bf16[272,128]{1,0:T(8,128)(2,1)S(1)}, u32[]{:S(2)}, u32[]{:S(2)}) collective-permute-start(bf16[272,128]{1,0:T(8,128)(2,1)} %get-tuple-element.43), channel_id=1, source_target_pairs={{0,16},{1,9},{2,18},{3,11},{4,20},{5,13},{6,22},{7,15},{8,24},{9,1... | collective-permute-start | bytes 208904 | tf_op jit(solution)/shard_map/ppermute | solution.py:228
  8.3 1.0 %collective-permute-start.3 = (bf16[272,128]{1,0:T(8,128)(2,1)S(1)}, bf16[272,128]{1,0:T(8,128)(2,1)S(1)}, u32[]{:S(2)}, u32[]{:S(2)}) collective-permute-start(bf16[272,128]{1,0:T(8,128)(2,1)S(1)} %collective-permute-done.2), channel_id=1, source_target_pairs={{0,16},{1,9},{2,18},{3,11},{4,20},{5,13},{6,22},{7,15},{8,24},{9,1... | collective-permute-start | bytes 208904 | tf_op jit(solution)/shard_map/ppermute | solution.py:228
  9.9 1.7 %collective-permute-done.1.refs_1_ = bf16[272,128]{1,0:T(8,128)(2,1)S(1)} collective-permute-done((bf16[272,128]{1,0:T(8,128)(2,1)}, bf16[272,128]{1,0:T(8,128)(2,1)S(1)}, u32[]{:S(2)}, u32[]{:S(2)}) %collective-permute-start.1) | collective-permute-done | bytes 69664 | tf_op jit(solution)/shard_map/ppermute | solution.py:228
  11.7 1.5 %collective-permute-start.5 = (bf16[272,128]{1,0:T(8,128)(2,1)}, bf16[272,128]{1,0:T(8,128)(2,1)S(1)}, u32[]{:S(2)}, u32[]{:S(2)}) collective-permute-start(bf16[272,128]{1,0:T(8,128)(2,1)} %get-tuple-element.45), channel_id=1, source_target_pairs={{0,0},{1,25},{2,2},{3,27},{4,4},{5,29},{6,6},{7,31},{8,8},{9,17},{... | collective-permute-start | bytes 208904 | tf_op jit(solution)/shard_map/ppermute | solution.py:228
  13.4 2.1 %collective-permute-start.4 = (bf16[272,128]{1,0:T(8,128)(2,1)S(1)}, bf16[272,128]{1,0:T(8,128)(2,1)S(1)}, u32[]{:S(2)}, u32[]{:S(2)}) collective-permute-start(bf16[272,128]{1,0:T(8,128)(2,1)S(1)} %collective-permute-done.3), channel_id=1, source_target_pairs={{0,1},{1,0},{2,3},{3,2},{4,5},{5,4},{6,7},{7,6},{8,9},{9,8},{10,11... | collective-permute-start | bytes 208904 | tf_op jit(solution)/shard_map/ppermute | solution.py:228
  16.8 0.9 %copy-done.2 = bf16[272,128]{1,0:T(8,128)(2,1)S(1)} copy-done((bf16[272,128]{1,0:T(8,128)(2,1)S(1)}, bf16[272,128]{1,0:T(8,128)(2,1)}, u32[]{:S(2)}) %copy-start.2) | copy-done | bytes 69656
  18.4 2.7 %collective-permute-start.12 = (bf16[544,128]{1,0:T(8,128)(2,1)S(1)}, bf16[544,128]{1,0:T(8,128)(2,1)S(1)}, u32[]{:S(2)}, u32[]{:S(2)}) collective-permute-start(bf16[544,128]{1,0:T(8,128)(2,1)S(1)} %get-tuple-element.52), channel_id=1, source_target_pairs={{0,4},{1,5},{2,6},{3,7},{4,0},{5,1},{6,2},{7,3},{8,12},{9,13},{10,... | collective-permute-start | bytes 417800 | tf_op jit(solution)/shard_map/ppermute | solution.py:199
  21.1 1.3 %collective-permute-start.13 = (bf16[544,128]{1,0:T(8,128)(2,1)S(1)}, bf16[544,128]{1,0:T(8,128)(2,1)S(1)}, u32[]{:S(2)}, u32[]{:S(2)}) collective-permute-start(bf16[544,128]{1,0:T(8,128)(2,1)S(1)} %get-tuple-element.53), channel_id=1, source_target_pairs={{0,6},{1,7},{2,4},{3,5},{4,2},{5,3},{6,0},{7,1},{8,14},{9,15},{10,... | collective-permute-start | bytes 417800 | tf_op jit(solution)/shard_map/ppermute | solution.py:199
  22.7 1.5 %collective-permute-start.9 = (bf16[432,512]{1,0:T(8,128)(2,1)S(1)}, bf16[432,512]{1,0:T(8,128)(2,1)S(1)}, u32[]{:S(2)}, u32[]{:S(2)}) collective-permute-start(bf16[432,512]{1,0:T(8,128)(2,1)S(1)} %constant_dynamic-slice_fusion.1), channel_id=1, source_target_pairs={{0,16},{1,9},{2,18},{3,11},{4,20},{5,13},{6,22},{7,15},{8,24},{9,1... | collective-permute-start | bytes 1327112 | tf_op jit(solution)/shard_map/ppermute | solution.py:228
  24.3 3.3 %collective-permute-done.10 = bf16[128,3456]{1,0:T(8,128)(2,1)S(1)} collective-permute-done((bf16[128,3456]{1,0:T(8,128)(2,1)}, bf16[128,3456]{1,0:T(8,128)(2,1)S(1)}, u32[]{:S(2)}, u32[]{:S(2)}) %collective-permute-start.10) | collective-permute-done | bytes 884768 | tf_op jit(solution)/shard_map/ppermute | solution.py:228
  28.0 2.7 %collective-permute-done.12.refs_4_ = bf16[544,128]{1,0:T(8,128)(2,1)S(1)} collective-permute-done((bf16[544,128]{1,0:T(8,128)(2,1)S(1)}, bf16[544,128]{1,0:T(8,128)(2,1)S(1)}, u32[]{:S(2)}, u32[]{:S(2)}) %collective-permute-start.12) | collective-permute-done | bytes 139296 | tf_op jit(solution)/shard_map/ppermute | solution.py:199
  30.6 2.3 %collective-permute-start.20 = (bf16[64,3456]{1,0:T(8,128)(2,1)S(1)}, bf16[64,3456]{1,0:T(8,128)(2,1)S(1)}, u32[]{:S(2)}, u32[]{:S(2)}) collective-permute-start(bf16[64,3456]{1,0:T(8,128)(2,1)S(1)} %constant_dynamic-slice_fusion), channel_id=1, source_target_pairs={{0,16},{1,9},{2,18},{3,11},{4,20},{5,13},{6,22},{7,15},{8,24},{9,1... | collective-permute-start | bytes 1327112 | tf_op jit(solution)/shard_map/ppermute | solution.py:228
  35.2 1.4 %collective-permute-done.14.refs_1_ = bf16[544,128]{1,0:T(8,128)(2,1)S(1)} collective-permute-done((bf16[544,128]{1,0:T(8,128)(2,1)S(1)}, bf16[544,128]{1,0:T(8,128)(2,1)S(1)}, u32[]{:S(2)}, u32[]{:S(2)}) %collective-permute-start.14) | collective-permute-done | bytes 139296 | tf_op jit(solution)/shard_map/ppermute | solution.py:228
  38.3 2.0 %pool.1 = (bf16[256,3456]{1,0:T(8,128)(2,1)S(1)}, bf16[256,3456]{1,0:T(8,128)(2,1)S(1)}, s32[16]{0:T(128)S(1)}, bf16[256,512]{1,0:T(8,128)(2,1)S(1)}) custom-call(bf16[544,128]{1,0:T(8,128)(2,1)S(1)} %get-tuple-element.54.refs_0_, bf16[544,128]{1,0:T(8,128)(2,1)S(1)} %collective-permute-done.14.refs_1_, ...), custom_call_target="tpu_custom_call" | custom-call | tf_op jit(solution)/shard_map/pool/pallas_call | solution.py:342
  40.7 1.4 %collective-permute-done.22 = bf16[64,3456]{1,0:T(8,128)(2,1)S(1)} collective-permute-done((bf16[64,3456]{1,0:T(8,128)(2,1)S(1)}, bf16[64,3456]{1,0:T(8,128)(2,1)S(1)}, u32[]{:S(2)}, u32[]{:S(2)}) %collective-permute-start.22) | collective-permute-done | bytes 442400 | tf_op jit(solution)/shard_map/ppermute | solution.py:228
  42.2 2.4 %owner.1 = (bf16[512,128]{1,0:T(8,128)(2,1)S(1)}, bf16[512,128]{1,0:T(8,128)(2,1)S(1)}, bf16[256,512]{1,0:T(8,128)(2,1)S(1)}) custom-call(s32[16]{0:T(128)S(1)} %get-tuple-element.61.slot_ref, bf16[256,512]{1,0:T(8,128)(2,1)S(1)} %get-tuple-element.62.hidden_ref, bf16[256,3456]{1,0:T(8,128)(2,1)S(1)} %get-tuple-element.64.scaled_ref, ...), custom_call_target="tpu_custom_call" | custom-call | tf_op jit(solution)/shard_map/owner/pallas_call | solution.py:363
  44.6 3.6 %collective-permute-start.23 = (bf16[512,128]{1,0:T(8,128)(2,1)S(1)}, bf16[512,128]{1,0:T(8,128)(2,1)S(1)}, u32[]{:S(2)}, u32[]{:S(2)}) collective-permute-start(bf16[512,128]{1,0:T(8,128)(2,1)S(1)} %get-tuple-element.69), channel_id=1, source_target_pairs={{0,6},{1,7},{2,4},{3,5},{4,2},{5,3},{6,0},{7,1},{8,14},{9,15},{10,... | collective-permute-start | bytes 393224 | tf_op jit(solution)/shard_map/ppermute | solution.py:199
  48.2 1.3 %blocks.1 = (bf16[512,128]{1,0:T(8,128)(2,1)S(1)}, bf16[512,128]{1,0:T(8,128)(2,1)S(1)}) custom-call(s32[16]{0:T(128)S(1)} %get-tuple-element.61.slot_ref, bf16[256,512]{1,0:T(8,128)(2,1)S(1)} %get-tuple-element.62.hidden_ref, bf16[256,512]{1,0:T(8,128)(2,1)S(1)} %get-tuple-element.73.dhidden_ref, ...), custom_call_target="tpu_custom_call" | custom-call | tf_op jit(solution)/shard_map/blocks/pallas_call | solution.py:371
  49.4 1.0 %collective-permute-start.25 = (bf16[512,128]{1,0:T(8,128)(2,1)S(1)}, bf16[512,128]{1,0:T(8,128)(2,1)S(1)}, u32[]{:S(2)}, u32[]{:S(2)}) collective-permute-start(bf16[512,128]{1,0:T(8,128)(2,1)S(1)} %get-tuple-element.75), channel_id=1, source_target_pairs={{0,2},{1,3},{2,0},{3,1},{4,6},{5,7},{6,4},{7,5},{8,10},{9,11},{10,... | collective-permute-start | bytes 393224 | tf_op jit(solution)/shard_map/ppermute | solution.py:199
  50.5 2.4 %cross.1 = bf16[256,3456]{1,0:T(8,128)(2,1)} custom-call(bf16[256,3456]{1,0:T(8,128)(2,1)S(1)} %get-tuple-element.70.first_ref, bf16[256,512]{1,0:T(8,128)(2,1)S(1)} %get-tuple-element.62.hidden_ref, bf16[512,3456]{1,0:T(8,128)(2,1)S(1)} %constant_dynamic-update-slice_fusion.u_ref, f32[1,3456]{1,0:T(1,128)S(1)} %reshape.7.bias_ref), custom_call_target="tpu_custom_call" | custom-call | flops 905969664 | bytes 7077888 | tf_op jit(solution)/shard_map/cross/pallas_call | solution.py:381
  53.4 1.6 %collective-permute-done.25.refs_2_ = bf16[512,128]{1,0:T(8,128)(2,1)S(1)} collective-permute-done((bf16[512,128]{1,0:T(8,128)(2,1)S(1)}, bf16[512,128]{1,0:T(8,128)(2,1)S(1)}, u32[]{:S(2)}, u32[]{:S(2)}) %collective-permute-start.25) | collective-permute-done | bytes 131104 | tf_op jit(solution)/shard_map/ppermute | solution.py:199
  55.0 5.5 %collective-permute-done.27.refs_4_ = bf16[512,128]{1,0:T(8,128)(2,1)S(1)} collective-permute-done((bf16[512,128]{1,0:T(8,128)(2,1)S(1)}, bf16[512,128]{1,0:T(8,128)(2,1)S(1)}, u32[]{:S(2)}, u32[]{:S(2)}) %collective-permute-start.27) | collective-permute-done | bytes 131104 | tf_op jit(solution)/shard_map/ppermute | solution.py:199
  60.7 1.3 %collective-permute-done.28.refs_5_ = bf16[512,128]{1,0:T(8,128)(2,1)S(1)} collective-permute-done((bf16[512,128]{1,0:T(8,128)(2,1)S(1)}, bf16[512,128]{1,0:T(8,128)(2,1)S(1)}, u32[]{:S(2)}, u32[]{:S(2)}) %collective-permute-start.28) | collective-permute-done | bytes 131104 | tf_op jit(solution)/shard_map/ppermute | solution.py:228
  62.5 1.0 %collective-permute-start.30 = (bf16[256,128]{1,0:T(8,128)(2,1)S(1)}, bf16[256,128]{1,0:T(8,128)(2,1)S(1)}, u32[]{:S(2)}, u32[]{:S(2)}) collective-permute-start(bf16[256,128]{1,0:T(8,128)(2,1)S(1)} %get-tuple-element.79), channel_id=1, source_target_pairs={{0,8},{8,0},{16,24},{24,16},{1,9},{9,1},{17,25},{25,17},{2,10},{10... | collective-permute-start | bytes 196616 | tf_op jit(solution)/shard_map/ppermute | solution.py:199
  63.5 1.3 %collective-permute-start.31 = (bf16[256,128]{1,0:T(8,128)(2,1)S(1)}, bf16[256,128]{1,0:T(8,128)(2,1)S(1)}, u32[]{:S(2)}, u32[]{:S(2)}) collective-permute-start(bf16[256,128]{1,0:T(8,128)(2,1)S(1)} %get-tuple-element.80), channel_id=1, source_target_pairs={{0,16},{8,24},{16,0},{24,8},{1,17},{9,25},{17,1},{25,9},{2,18},{10... | collective-permute-start | bytes 196616 | tf_op jit(solution)/shard_map/ppermute | solution.py:199
  64.8 1.3 %collective-permute-start.32 = (bf16[256,128]{1,0:T(8,128)(2,1)S(1)}, bf16[256,128]{1,0:T(8,128)(2,1)S(1)}, u32[]{:S(2)}, u32[]{:S(2)}) collective-permute-start(bf16[256,128]{1,0:T(8,128)(2,1)S(1)} %get-tuple-element.81), channel_id=1, source_target_pairs={{0,24},{8,16},{16,8},{24,0},{1,25},{9,17},{17,9},{25,1},{2,26},{10... | collective-permute-start | bytes 196616 | tf_op jit(solution)/shard_map/ppermute | solution.py:199
  66.1 0.8 %collective-permute-done.30.refs_1_ = bf16[256,128]{1,0:T(8,128)(2,1)S(1)} collective-permute-done((bf16[256,128]{1,0:T(8,128)(2,1)S(1)}, bf16[256,128]{1,0:T(8,128)(2,1)S(1)}, u32[]{:S(2)}, u32[]{:S(2)}) %collective-permute-start.30) | collective-permute-done | bytes 65568 | tf_op jit(solution)/shard_map/ppermute | solution.py:199
  66.8 0.9 %collective-permute-done.31.refs_2_ = bf16[256,128]{1,0:T(8,128)(2,1)S(1)} collective-permute-done((bf16[256,128]{1,0:T(8,128)(2,1)S(1)}, bf16[256,128]{1,0:T(8,128)(2,1)S(1)}, u32[]{:S(2)}, u32[]{:S(2)}) %collective-permute-start.31) | collective-permute-done | bytes 65568 | tf_op jit(solution)/shard_map/ppermute | solution.py:199
  67.8 2.2 %collective-permute-done.32.refs_3_ = bf16[256,128]{1,0:T(8,128)(2,1)S(1)} collective-permute-done((bf16[256,128]{1,0:T(8,128)(2,1)S(1)}, bf16[256,128]{1,0:T(8,128)(2,1)S(1)}, u32[]{:S(2)}, u32[]{:S(2)}) %collective-permute-start.32) | collective-permute-done | bytes 65568 | tf_op jit(solution)/shard_map/ppermute | solution.py:199
  69.9 1.5 %rows.1 = f32[512,128]{1,0:T(8,128)} custom-call(s32[8]{0:T(128)S(1)} %copy-done.4, s32[8,128,128]{2,1,0:T(8,128)S(1)} %copy-done.1, bf16[256,128]{1,0:T(8,128)(2,1)S(1)} %get-tuple-element.78.refs_0_, bf16[256,128]{1,0:T(8,128)(2,1)S(1)} %collective-permute-done.30.refs_1_, bf16[256,128]{1,0:T(8,128)(2,1)S(1)} %collective-permute-done.31.refs_2_, ...), custom_call_target="tpu_custom_call" | custom-call | tf_op jit(solution)/shard_map/rows/pallas_call | solution.py:414
  (73 shorter events, 9.8 us)
Async XLA Ops:
  0.6 21.8 %collective-permute-start = (bf16[864,512]{1,0:T(8,128)(2,1)}, bf16[864,512]{1,0:T(8,128)(2,1)S(1)}, u32[]{:S(2)}, u32[]{:S(2)}) collective-permute-start(bf16[864,512]{1,0:T(8,128)(2,1)} %param.16), channel_id=1, source_target_pairs={{0,8},{1,17},{2,10},{3,19},{4,12},{5,21},{6,14},{7,23},{8,0},{9,25... | collective-permute-start | bytes 2654216 | tf_op jit(solution)/shard_map/ppermute | solution.py:228
  3.6 23.9 %collective-permute-start.10 = (bf16[128,3456]{1,0:T(8,128)(2,1)}, bf16[128,3456]{1,0:T(8,128)(2,1)S(1)}, u32[]{:S(2)}, u32[]{:S(2)}) collective-permute-start(bf16[128,3456]{1,0:T(8,128)(2,1)} %param.17), channel_id=1, source_target_pairs={{0,8},{1,17},{2,10},{3,19},{4,12},{5,21},{6,14},{7,23},{8,0},{9,25... | collective-permute-start | bytes 2654216 | tf_op jit(solution)/shard_map/ppermute | solution.py:228
  5.8 2.6 %collective-permute-start.2 = (bf16[272,128]{1,0:T(8,128)(2,1)}, bf16[272,128]{1,0:T(8,128)(2,1)S(1)}, u32[]{:S(2)}, u32[]{:S(2)}) collective-permute-start(bf16[272,128]{1,0:T(8,128)(2,1)} %get-tuple-element.44), channel_id=1, source_target_pairs={{0,1},{1,0},{2,3},{3,2},{4,5},{5,4},{6,7},{7,6},{8,9},{9,8},{10,11... | collective-permute-start | bytes 208904 | tf_op jit(solution)/shard_map/ppermute | solution.py:228
  5.8 3.4 %collective-permute-start.6 = (bf16[272,128]{1,0:T(8,128)(2,1)}, bf16[272,128]{1,0:T(8,128)(2,1)S(1)}, u32[]{:S(2)}, u32[]{:S(2)}) collective-permute-start(bf16[272,128]{1,0:T(8,128)(2,1)} %get-tuple-element.46), channel_id=1, source_target_pairs={{0,1},{1,0},{2,3},{3,2},{4,5},{5,4},{6,7},{7,6},{8,9},{9,8},{10,11... | collective-permute-start | bytes 208904 | tf_op jit(solution)/shard_map/ppermute | solution.py:228
  6.3 5.3 %collective-permute-start.1 = (bf16[272,128]{1,0:T(8,128)(2,1)}, bf16[272,128]{1,0:T(8,128)(2,1)S(1)}, u32[]{:S(2)}, u32[]{:S(2)}) collective-permute-start(bf16[272,128]{1,0:T(8,128)(2,1)} %get-tuple-element.43), channel_id=1, source_target_pairs={{0,16},{1,9},{2,18},{3,11},{4,20},{5,13},{6,22},{7,15},{8,24},{9,1... | collective-permute-start | bytes 208904 | tf_op jit(solution)/shard_map/ppermute | solution.py:228
  8.3 5.1 %collective-permute-start.3 = (bf16[272,128]{1,0:T(8,128)(2,1)S(1)}, bf16[272,128]{1,0:T(8,128)(2,1)S(1)}, u32[]{:S(2)}, u32[]{:S(2)}) collective-permute-start(bf16[272,128]{1,0:T(8,128)(2,1)S(1)} %collective-permute-done.2), channel_id=1, source_target_pairs={{0,16},{1,9},{2,18},{3,11},{4,20},{5,13},{6,22},{7,15},{8,24},{9,1... | collective-permute-start | bytes 208904 | tf_op jit(solution)/shard_map/ppermute | solution.py:228
  9.3 6.2 %collective-permute-start.7 = (bf16[272,128]{1,0:T(8,128)(2,1)S(1)}, bf16[272,128]{1,0:T(8,128)(2,1)S(1)}, u32[]{:S(2)}, u32[]{:S(2)}) collective-permute-start(bf16[272,128]{1,0:T(8,128)(2,1)S(1)} %collective-permute-done.6), channel_id=1, source_target_pairs={{0,0},{1,25},{2,2},{3,27},{4,4},{5,29},{6,6},{7,31},{8,8},{9,17},{... | collective-permute-start | bytes 208904 | tf_op jit(solution)/shard_map/ppermute | solution.py:228
  11.7 4.2 %collective-permute-start.5 = (bf16[272,128]{1,0:T(8,128)(2,1)}, bf16[272,128]{1,0:T(8,128)(2,1)S(1)}, u32[]{:S(2)}, u32[]{:S(2)}) collective-permute-start(bf16[272,128]{1,0:T(8,128)(2,1)} %get-tuple-element.45), channel_id=1, source_target_pairs={{0,0},{1,25},{2,2},{3,27},{4,4},{5,29},{6,6},{7,31},{8,8},{9,17},{... | collective-permute-start | bytes 208904 | tf_op jit(solution)/shard_map/ppermute | solution.py:228
  13.4 3.0 %collective-permute-start.4 = (bf16[272,128]{1,0:T(8,128)(2,1)S(1)}, bf16[272,128]{1,0:T(8,128)(2,1)S(1)}, u32[]{:S(2)}, u32[]{:S(2)}) collective-permute-start(bf16[272,128]{1,0:T(8,128)(2,1)S(1)} %collective-permute-done.3), channel_id=1, source_target_pairs={{0,1},{1,0},{2,3},{3,2},{4,5},{5,4},{6,7},{7,6},{8,9},{9,8},{10,11... | collective-permute-start | bytes 208904 | tf_op jit(solution)/shard_map/ppermute | solution.py:228
  18.4 12.2 %collective-permute-start.12 = (bf16[544,128]{1,0:T(8,128)(2,1)S(1)}, bf16[544,128]{1,0:T(8,128)(2,1)S(1)}, u32[]{:S(2)}, u32[]{:S(2)}) collective-permute-start(bf16[544,128]{1,0:T(8,128)(2,1)S(1)} %get-tuple-element.52), channel_id=1, source_target_pairs={{0,4},{1,5},{2,6},{3,7},{4,0},{5,1},{6,2},{7,3},{8,12},{9,13},{10,... | collective-permute-start | bytes 417800 | tf_op jit(solution)/shard_map/ppermute | solution.py:199
  21.1 11.9 %collective-permute-start.13 = (bf16[544,128]{1,0:T(8,128)(2,1)S(1)}, bf16[544,128]{1,0:T(8,128)(2,1)S(1)}, u32[]{:S(2)}, u32[]{:S(2)}) collective-permute-start(bf16[544,128]{1,0:T(8,128)(2,1)S(1)} %get-tuple-element.53), channel_id=1, source_target_pairs={{0,6},{1,7},{2,4},{3,5},{4,2},{5,3},{6,0},{7,1},{8,14},{9,15},{10,... | collective-permute-start | bytes 417800 | tf_op jit(solution)/shard_map/ppermute | solution.py:199
  22.4 10.7 %collective-permute-start.11 = (bf16[544,128]{1,0:T(8,128)(2,1)S(1)}, bf16[544,128]{1,0:T(8,128)(2,1)S(1)}, u32[]{:S(2)}, u32[]{:S(2)}) collective-permute-start(bf16[544,128]{1,0:T(8,128)(2,1)S(1)} %get-tuple-element.51), channel_id=1, source_target_pairs={{0,2},{1,3},{2,0},{3,1},{4,6},{5,7},{6,4},{7,5},{8,10},{9,11},{10,... | collective-permute-start | bytes 417800 | tf_op jit(solution)/shard_map/ppermute | solution.py:199
  22.7 10.4 %collective-permute-start.9 = (bf16[432,512]{1,0:T(8,128)(2,1)S(1)}, bf16[432,512]{1,0:T(8,128)(2,1)S(1)}, u32[]{:S(2)}, u32[]{:S(2)}) collective-permute-start(bf16[432,512]{1,0:T(8,128)(2,1)S(1)} %constant_dynamic-slice_fusion.1), channel_id=1, source_target_pairs={{0,16},{1,9},{2,18},{3,11},{4,20},{5,13},{6,22},{7,15},{8,24},{9,1... | collective-permute-start | bytes 1327112 | tf_op jit(solution)/shard_map/ppermute | solution.py:228
  27.5 7.3 %collective-permute-start.18 = (bf16[864,512]{1,0:T(8,128)(2,1)S(1)}, bf16[864,512]{1,0:T(8,128)(2,1)S(1)}, u32[]{:S(2)}, u32[]{:S(2)}) collective-permute-start(bf16[864,512]{1,0:T(8,128)(2,1)S(1)} %collective-permute-done), channel_id=1, source_target_pairs={{0,1},{1,0},{2,3},{3,2},{4,5},{5,4},{6,7},{7,6},{8,9},{9,8},{10,11... | collective-permute-start | bytes 2654216 | tf_op jit(solution)/shard_map/ppermute | solution.py:228
  30.6 9.7 %collective-permute-start.20 = (bf16[64,3456]{1,0:T(8,128)(2,1)S(1)}, bf16[64,3456]{1,0:T(8,128)(2,1)S(1)}, u32[]{:S(2)}, u32[]{:S(2)}) collective-permute-start(bf16[64,3456]{1,0:T(8,128)(2,1)S(1)} %constant_dynamic-slice_fusion), channel_id=1, source_target_pairs={{0,16},{1,9},{2,18},{3,11},{4,20},{5,13},{6,22},{7,15},{8,24},{9,1... | collective-permute-start | bytes 1327112 | tf_op jit(solution)/shard_map/ppermute | solution.py:228
  33.1 3.8 %collective-permute-start.19 = (bf16[432,512]{1,0:T(8,128)(2,1)S(1)}, bf16[432,512]{1,0:T(8,128)(2,1)S(1)}, u32[]{:S(2)}, u32[]{:S(2)}) collective-permute-start(bf16[432,512]{1,0:T(8,128)(2,1)S(1)} %collective-permute-done.9), channel_id=1, source_target_pairs={{0,1},{1,0},{2,3},{3,2},{4,5},{5,4},{6,7},{7,6},{8,9},{9,8},{10,11... | collective-permute-start | bytes 1327112 | tf_op jit(solution)/shard_map/ppermute | solution.py:228
  33.7 6.9 %collective-permute-start.21 = (bf16[128,3456]{1,0:T(8,128)(2,1)S(1)}, bf16[128,3456]{1,0:T(8,128)(2,1)S(1)}, u32[]{:S(2)}, u32[]{:S(2)}) collective-permute-start(bf16[128,3456]{1,0:T(8,128)(2,1)S(1)} %collective-permute-done.10), channel_id=1, source_target_pairs={{0,1},{1,0},{2,3},{3,2},{4,5},{5,4},{6,7},{7,6},{8,9},{9,8},{10,11... | collective-permute-start | bytes 2654216 | tf_op jit(solution)/shard_map/ppermute | solution.py:228
  34.2 2.4 %collective-permute-start.14 = (bf16[544,128]{1,0:T(8,128)(2,1)S(1)}, bf16[544,128]{1,0:T(8,128)(2,1)S(1)}, u32[]{:S(2)}, u32[]{:S(2)}) collective-permute-start(bf16[544,128]{1,0:T(8,128)(2,1)S(1)} %get-tuple-element.54.refs_0_), channel_id=1, source_target_pairs={{0,1},{1,0},{2,3},{3,2},{4,5},{5,4},{6,7},{7,6},{8,9},{9,8},{10,11... | collective-permute-start | bytes 417800 | tf_op jit(solution)/shard_map/ppermute | solution.py:228
  34.8 2.3 %collective-permute-start.15 = (bf16[544,128]{1,0:T(8,128)(2,1)S(1)}, bf16[544,128]{1,0:T(8,128)(2,1)S(1)}, u32[]{:S(2)}, u32[]{:S(2)}) collective-permute-start(bf16[544,128]{1,0:T(8,128)(2,1)S(1)} %collective-permute-done.11.refs_2_), channel_id=1, source_target_pairs={{0,1},{1,0},{2,3},{3,2},{4,5},{5,4},{6,7},{7,6},{8,9},{9,8},{10,11... | collective-permute-start | bytes 417800 | tf_op jit(solution)/shard_map/ppermute | solution.py:228
  36.6 1.4 %collective-permute-start.16 = (bf16[544,128]{1,0:T(8,128)(2,1)S(1)}, bf16[544,128]{1,0:T(8,128)(2,1)S(1)}, u32[]{:S(2)}, u32[]{:S(2)}) collective-permute-start(bf16[544,128]{1,0:T(8,128)(2,1)S(1)} %collective-permute-done.12.refs_4_), channel_id=1, source_target_pairs={{0,1},{1,0},{2,3},{3,2},{4,5},{5,4},{6,7},{7,6},{8,9},{9,8},{10,11... | collective-permute-start | bytes 417800 | tf_op jit(solution)/shard_map/ppermute | solution.py:228
  36.9 1.4 %collective-permute-start.17 = (bf16[544,128]{1,0:T(8,128)(2,1)S(1)}, bf16[544,128]{1,0:T(8,128)(2,1)S(1)}, u32[]{:S(2)}, u32[]{:S(2)}) collective-permute-start(bf16[544,128]{1,0:T(8,128)(2,1)S(1)} %collective-permute-done.13.refs_6_), channel_id=1, source_target_pairs={{0,1},{1,0},{2,3},{3,2},{4,5},{5,4},{6,7},{7,6},{8,9},{9,8},{10,11... | collective-permute-start | bytes 417800 | tf_op jit(solution)/shard_map/ppermute | solution.py:228
  40.3 1.9 %collective-permute-start.22 = (bf16[64,3456]{1,0:T(8,128)(2,1)S(1)}, bf16[64,3456]{1,0:T(8,128)(2,1)S(1)}, u32[]{:S(2)}, u32[]{:S(2)}) collective-permute-start(bf16[64,3456]{1,0:T(8,128)(2,1)S(1)} %collective-permute-done.20), channel_id=1, source_target_pairs={{0,1},{1,0},{2,3},{3,2},{4,5},{5,4},{6,7},{7,6},{8,9},{9,8},{10,11... | collective-permute-start | bytes 1327112 | tf_op jit(solution)/shard_map/ppermute | solution.py:228
  44.6 8.4 %collective-permute-start.23 = (bf16[512,128]{1,0:T(8,128)(2,1)S(1)}, bf16[512,128]{1,0:T(8,128)(2,1)S(1)}, u32[]{:S(2)}, u32[]{:S(2)}) collective-permute-start(bf16[512,128]{1,0:T(8,128)(2,1)S(1)} %get-tuple-element.69), channel_id=1, source_target_pairs={{0,6},{1,7},{2,4},{3,5},{4,2},{5,3},{6,0},{7,1},{8,14},{9,15},{10,... | collective-permute-start | bytes 393224 | tf_op jit(solution)/shard_map/ppermute | solution.py:199
  49.4 5.6 %collective-permute-start.25 = (bf16[512,128]{1,0:T(8,128)(2,1)S(1)}, bf16[512,128]{1,0:T(8,128)(2,1)S(1)}, u32[]{:S(2)}, u32[]{:S(2)}) collective-permute-start(bf16[512,128]{1,0:T(8,128)(2,1)S(1)} %get-tuple-element.75), channel_id=1, source_target_pairs={{0,2},{1,3},{2,0},{3,1},{4,6},{5,7},{6,4},{7,5},{8,10},{9,11},{10,... | collective-permute-start | bytes 393224 | tf_op jit(solution)/shard_map/ppermute | solution.py:199
  50.5 10.1 %collective-permute-start.27 = (bf16[512,128]{1,0:T(8,128)(2,1)S(1)}, bf16[512,128]{1,0:T(8,128)(2,1)S(1)}, u32[]{:S(2)}, u32[]{:S(2)}) collective-permute-start(bf16[512,128]{1,0:T(8,128)(2,1)S(1)} %get-tuple-element.76), channel_id=1, source_target_pairs={{0,4},{1,5},{2,6},{3,7},{4,0},{5,1},{6,2},{7,3},{8,12},{9,13},{10,... | collective-permute-start | bytes 393224 | tf_op jit(solution)/shard_map/ppermute | solution.py:199
  50.5 10.2 %collective-permute-start.24 = (bf16[512,128]{1,0:T(8,128)(2,1)S(1)}, bf16[512,128]{1,0:T(8,128)(2,1)S(1)}, u32[]{:S(2)}, u32[]{:S(2)}) collective-permute-start(bf16[512,128]{1,0:T(8,128)(2,1)S(1)} %get-tuple-element.74.refs_0_), channel_id=1, source_target_pairs={{0,1},{1,0},{2,3},{3,2},{4,5},{5,4},{6,7},{7,6},{8,9},{9,8},{10,11... | collective-permute-start | bytes 393224 | tf_op jit(solution)/shard_map/ppermute | solution.py:228
  52.9 7.7 %collective-permute-start.29 = (bf16[512,128]{1,0:T(8,128)(2,1)S(1)}, bf16[512,128]{1,0:T(8,128)(2,1)S(1)}, u32[]{:S(2)}, u32[]{:S(2)}) collective-permute-start(bf16[512,128]{1,0:T(8,128)(2,1)S(1)} %collective-permute-done.23.refs_6_), channel_id=1, source_target_pairs={{0,1},{1,0},{2,3},{3,2},{4,5},{5,4},{6,7},{7,6},{8,9},{9,8},{10,11... | collective-permute-start | bytes 393224 | tf_op jit(solution)/shard_map/ppermute | solution.py:228
  55.0 5.6 %collective-permute-start.26 = (bf16[512,128]{1,0:T(8,128)(2,1)S(1)}, bf16[512,128]{1,0:T(8,128)(2,1)S(1)}, u32[]{:S(2)}, u32[]{:S(2)}) collective-permute-start(bf16[512,128]{1,0:T(8,128)(2,1)S(1)} %collective-permute-done.25.refs_2_), channel_id=1, source_target_pairs={{0,1},{1,0},{2,3},{3,2},{4,5},{5,4},{6,7},{7,6},{8,9},{9,8},{10,11... | collective-permute-start | bytes 393224 | tf_op jit(solution)/shard_map/ppermute | solution.py:228
  60.6 1.3 %collective-permute-start.28 = (bf16[512,128]{1,0:T(8,128)(2,1)S(1)}, bf16[512,128]{1,0:T(8,128)(2,1)S(1)}, u32[]{:S(2)}, u32[]{:S(2)}) collective-permute-start(bf16[512,128]{1,0:T(8,128)(2,1)S(1)} %collective-permute-done.27.refs_4_), channel_id=1, source_target_pairs={{0,1},{1,0},{2,3},{3,2},{4,5},{5,4},{6,7},{7,6},{8,9},{9,8},{10,11... | collective-permute-start | bytes 393224 | tf_op jit(solution)/shard_map/ppermute | solution.py:228
  62.5 4.3 %collective-permute-start.30 = (bf16[256,128]{1,0:T(8,128)(2,1)S(1)}, bf16[256,128]{1,0:T(8,128)(2,1)S(1)}, u32[]{:S(2)}, u32[]{:S(2)}) collective-permute-start(bf16[256,128]{1,0:T(8,128)(2,1)S(1)} %get-tuple-element.79), channel_id=1, source_target_pairs={{0,8},{8,0},{16,24},{24,16},{1,9},{9,1},{17,25},{25,17},{2,10},{10... | collective-permute-start | bytes 196616 | tf_op jit(solution)/shard_map/ppermute | solution.py:199
  63.5 4.3 %collective-permute-start.31 = (bf16[256,128]{1,0:T(8,128)(2,1)S(1)}, bf16[256,128]{1,0:T(8,128)(2,1)S(1)}, u32[]{:S(2)}, u32[]{:S(2)}) collective-permute-start(bf16[256,128]{1,0:T(8,128)(2,1)S(1)} %get-tuple-element.80), channel_id=1, source_target_pairs={{0,16},{8,24},{16,0},{24,8},{1,17},{9,25},{17,1},{25,9},{2,18},{10... | collective-permute-start | bytes 196616 | tf_op jit(solution)/shard_map/ppermute | solution.py:199
  64.8 5.2 %collective-permute-start.32 = (bf16[256,128]{1,0:T(8,128)(2,1)S(1)}, bf16[256,128]{1,0:T(8,128)(2,1)S(1)}, u32[]{:S(2)}, u32[]{:S(2)}) collective-permute-start(bf16[256,128]{1,0:T(8,128)(2,1)S(1)} %get-tuple-element.81), channel_id=1, source_target_pairs={{0,24},{8,16},{16,8},{24,0},{1,25},{9,17},{17,9},{25,1},{2,26},{10... | collective-permute-start | bytes 196616 | tf_op jit(solution)/shard_map/ppermute | solution.py:199
  (9 other events, 66.8 us)

commit v6 on v5

--- a/solution.py
+++ b/solution.py
@@ -358,8 +358,7 @@
         second_u, scaled = lax.optimization_barrier((second_u, scaled))
     full_u = assemble(late_u, first_u, sibling(swap_u), second_u, sibling(second_u))
 
-    half = chips // 2
-    groups = (range(half, chips), range(half))
+    groups = (range(chips - 1, chips), range(chips - 1))
     *far_grads, dhidden = pl.pallas_call(
         functools.partial(owner_kernel, groups[0], size),
         out_shape=[grad] * len(groups[0]) + [jax.ShapeDtypeStruct((samples, rank), BF16)],

time: 71.7 us -> 71.6 us (level)
  transfers between devices with their start and end apart: 33 -> 33, of which waited for: 17 -> 18; matrix products, arithmetic and copies ran while one was open for 2% -> 2% of each run, Pallas kernels for 12% -> 12%
where the time goes in v6:
time: 71.6 us; the launch traced here: 71.4 us
  starting transfers between devices  30.2 us (42%)
  waiting for transfers between devices  25.2 us (35%)
  Pallas kernels  12.9 us (18%)
  local copies, waits for them, and re-layouts  2.15 us (3%)
  between operations  0.89 us (1%)
    ppermute x24, starting transfers between devices, permute(): return lax.ppermute(value, ('node', 'table'), pairs)  17.7 us
    ppermute x9, waiting for transfers between devices, xor_permute(): return lax.ppermute(value, axis, [(i, i ^ k) for i in range(size)])  14.1 us
    ppermute x9, starting transfers between devices, xor_permute(): return lax.ppermute(value, axis, [(i, i ^ k) for i in range(size)])  12.5 us
    ppermute x24, waiting for transfers between devices, permute(): return lax.ppermute(value, ('node', 'table'), pairs)  11.2 us
    pallas_call x1, Pallas kernels, body(): pl.pallas_call(cross_kernel, out_shape=jax.ShapeDtypeStruct((samples, cro...  2.41 us
    pallas_call x1, Pallas kernels, body(): pl.pallas_call(functools.partial(owner_kernel, groups[0], size), out_shap...  2.06 us
    pallas_call x1, Pallas kernels, body(): pl.pallas_call(functools.partial(products_kernel, quota, size), out_shape...  2.04 us
    pallas_call x1, Pallas kernels, body(): pl.pallas_call(functools.partial(pool_kernel, tables, size), out_shape=[j...  1.98 us
  transfers between devices with their start and end apart: 33, of which 18 were waited for; matrix products, arithmetic and copies ran while one was open for 2% of the time, Pallas kernels for 12%

profile of v6, /device:TPU:0, one launch (start us, length us, event | category | flops | bytes accessed | tf_op | source)
XLA Modules:
  0.0 71.4 jit_solution(12038843404355336682)
XLA Ops:
  0.6 3.0 %collective-permute-start = (bf16[864,512]{1,0:T(8,128)(2,1)}, bf16[864,512]{1,0:T(8,128)(2,1)S(1)}, u32[]{:S(2)}, u32[]{:S(2)}) collective-permute-start(bf16[864,512]{1,0:T(8,128)(2,1)} %param.16), channel_id=1, source_target_pairs={{0,8},{1,17},{2,10},{3,19},{4,12},{5,21},{6,14},{7,23},{8,0},{9,25... | collective-permute-start | bytes 2654216 | tf_op jit(solution)/shard_map/ppermute | solution.py:228
  3.7 2.0 %products.1 = (bf16[272,128]{1,0:T(8,128)(2,1)}, bf16[272,128]{1,0:T(8,128)(2,1)}, bf16[272,128]{1,0:T(8,128)(2,1)}, bf16[272,128]{1,0:T(8,128)(2,1)}, bf16[272,128]{1,0:T(8,128)(2,1)}) custom-call(s32[8]{0:T(128)} %rows_ref.1, s32[8]{0:T(128)} %table_hbm.1, s32[8]{0:T(128)} %slot_hbm.1, bf16[512,128]{1,0:T(8,128)(2,1)} %emb_hbm.1, s32[8,128,128]{2,1,0:T(8,128)} %mult_ref.1), custom_call_target="tpu_custom_call" | custom-call | tf_op jit(solution)/shard_map/products/pallas_call | solution.py:280
  6.3 2.0 %collective-permute-start.1 = (bf16[272,128]{1,0:T(8,128)(2,1)}, bf16[272,128]{1,0:T(8,128)(2,1)S(1)}, u32[]{:S(2)}, u32[]{:S(2)}) collective-permute-start(bf16[272,128]{1,0:T(8,128)(2,1)} %get-tuple-element.43), channel_id=1, source_target_pairs={{0,16},{1,9},{2,18},{3,11},{4,20},{5,13},{6,22},{7,15},{8,24},{9,1... | collective-permute-start | bytes 208904 | tf_op jit(solution)/shard_map/ppermute | solution.py:228
  8.3 1.0 %collective-permute-start.3 = (bf16[272,128]{1,0:T(8,128)(2,1)S(1)}, bf16[272,128]{1,0:T(8,128)(2,1)S(1)}, u32[]{:S(2)}, u32[]{:S(2)}) collective-permute-start(bf16[272,128]{1,0:T(8,128)(2,1)S(1)} %collective-permute-done.2), channel_id=1, source_target_pairs={{0,16},{1,9},{2,18},{3,11},{4,20},{5,13},{6,22},{7,15},{8,24},{9,1... | collective-permute-start | bytes 208904 | tf_op jit(solution)/shard_map/ppermute | solution.py:228
  9.9 1.7 %collective-permute-done.1.refs_1_ = bf16[272,128]{1,0:T(8,128)(2,1)S(1)} collective-permute-done((bf16[272,128]{1,0:T(8,128)(2,1)}, bf16[272,128]{1,0:T(8,128)(2,1)S(1)}, u32[]{:S(2)}, u32[]{:S(2)}) %collective-permute-start.1) | collective-permute-done | bytes 69664 | tf_op jit(solution)/shard_map/ppermute | solution.py:228
  11.7 1.5 %collective-permute-start.5 = (bf16[272,128]{1,0:T(8,128)(2,1)}, bf16[272,128]{1,0:T(8,128)(2,1)S(1)}, u32[]{:S(2)}, u32[]{:S(2)}) collective-permute-start(bf16[272,128]{1,0:T(8,128)(2,1)} %get-tuple-element.45), channel_id=1, source_target_pairs={{0,0},{1,25},{2,2},{3,27},{4,4},{5,29},{6,6},{7,31},{8,8},{9,17},{... | collective-permute-start | bytes 208904 | tf_op jit(solution)/shard_map/ppermute | solution.py:228
  13.4 2.1 %collective-permute-start.4 = (bf16[272,128]{1,0:T(8,128)(2,1)S(1)}, bf16[272,128]{1,0:T(8,128)(2,1)S(1)}, u32[]{:S(2)}, u32[]{:S(2)}) collective-permute-start(bf16[272,128]{1,0:T(8,128)(2,1)S(1)} %collective-permute-done.3), channel_id=1, source_target_pairs={{0,1},{1,0},{2,3},{3,2},{4,5},{5,4},{6,7},{7,6},{8,9},{9,8},{10,11... | collective-permute-start | bytes 208904 | tf_op jit(solution)/shard_map/ppermute | solution.py:228
  16.8 0.9 %copy-done.2 = bf16[272,128]{1,0:T(8,128)(2,1)S(1)} copy-done((bf16[272,128]{1,0:T(8,128)(2,1)S(1)}, bf16[272,128]{1,0:T(8,128)(2,1)}, u32[]{:S(2)}) %copy-start.2) | copy-done | bytes 69656
  18.4 2.7 %collective-permute-start.12 = (bf16[544,128]{1,0:T(8,128)(2,1)S(1)}, bf16[544,128]{1,0:T(8,128)(2,1)S(1)}, u32[]{:S(2)}, u32[]{:S(2)}) collective-permute-start(bf16[544,128]{1,0:T(8,128)(2,1)S(1)} %get-tuple-element.52), channel_id=1, source_target_pairs={{0,4},{1,5},{2,6},{3,7},{4,0},{5,1},{6,2},{7,3},{8,12},{9,13},{10,... | collective-permute-start | bytes 417800 | tf_op jit(solution)/shard_map/ppermute | solution.py:199
  21.1 1.3 %collective-permute-start.13 = (bf16[544,128]{1,0:T(8,128)(2,1)S(1)}, bf16[544,128]{1,0:T(8,128)(2,1)S(1)}, u32[]{:S(2)}, u32[]{:S(2)}) collective-permute-start(bf16[544,128]{1,0:T(8,128)(2,1)S(1)} %get-tuple-element.53), channel_id=1, source_target_pairs={{0,6},{1,7},{2,4},{3,5},{4,2},{5,3},{6,0},{7,1},{8,14},{9,15},{10,... | collective-permute-start | bytes 417800 | tf_op jit(solution)/shard_map/ppermute | solution.py:199
  22.7 1.5 %collective-permute-start.9 = (bf16[432,512]{1,0:T(8,128)(2,1)S(1)}, bf16[432,512]{1,0:T(8,128)(2,1)S(1)}, u32[]{:S(2)}, u32[]{:S(2)}) collective-permute-start(bf16[432,512]{1,0:T(8,128)(2,1)S(1)} %constant_dynamic-slice_fusion.1), channel_id=1, source_target_pairs={{0,16},{1,9},{2,18},{3,11},{4,20},{5,13},{6,22},{7,15},{8,24},{9,1... | collective-permute-start | bytes 1327112 | tf_op jit(solution)/shard_map/ppermute | solution.py:228
  24.3 3.3 %collective-permute-done.10 = bf16[128,3456]{1,0:T(8,128)(2,1)S(1)} collective-permute-done((bf16[128,3456]{1,0:T(8,128)(2,1)}, bf16[128,3456]{1,0:T(8,128)(2,1)S(1)}, u32[]{:S(2)}, u32[]{:S(2)}) %collective-permute-start.10) | collective-permute-done | bytes 884768 | tf_op jit(solution)/shard_map/ppermute | solution.py:228
  28.0 2.7 %collective-permute-done.12.refs_4_ = bf16[544,128]{1,0:T(8,128)(2,1)S(1)} collective-permute-done((bf16[544,128]{1,0:T(8,128)(2,1)S(1)}, bf16[544,128]{1,0:T(8,128)(2,1)S(1)}, u32[]{:S(2)}, u32[]{:S(2)}) %collective-permute-start.12) | collective-permute-done | bytes 139296 | tf_op jit(solution)/shard_map/ppermute | solution.py:199
  30.6 2.3 %collective-permute-start.20 = (bf16[64,3456]{1,0:T(8,128)(2,1)S(1)}, bf16[64,3456]{1,0:T(8,128)(2,1)S(1)}, u32[]{:S(2)}, u32[]{:S(2)}) collective-permute-start(bf16[64,3456]{1,0:T(8,128)(2,1)S(1)} %constant_dynamic-slice_fusion), channel_id=1, source_target_pairs={{0,16},{1,9},{2,18},{3,11},{4,20},{5,13},{6,22},{7,15},{8,24},{9,1... | collective-permute-start | bytes 1327112 | tf_op jit(solution)/shard_map/ppermute | solution.py:228
  35.2 1.4 %collective-permute-done.14.refs_1_ = bf16[544,128]{1,0:T(8,128)(2,1)S(1)} collective-permute-done((bf16[544,128]{1,0:T(8,128)(2,1)S(1)}, bf16[544,128]{1,0:T(8,128)(2,1)S(1)}, u32[]{:S(2)}, u32[]{:S(2)}) %collective-permute-start.14) | collective-permute-done | bytes 139296 | tf_op jit(solution)/shard_map/ppermute | solution.py:228
  38.3 2.0 %pool.1 = (bf16[256,3456]{1,0:T(8,128)(2,1)S(1)}, bf16[256,3456]{1,0:T(8,128)(2,1)S(1)}, s32[16]{0:T(128)S(1)}, bf16[256,512]{1,0:T(8,128)(2,1)S(1)}) custom-call(bf16[544,128]{1,0:T(8,128)(2,1)S(1)} %get-tuple-element.54.refs_0_, bf16[544,128]{1,0:T(8,128)(2,1)S(1)} %collective-permute-done.14.refs_1_, ...), custom_call_target="tpu_custom_call" | custom-call | tf_op jit(solution)/shard_map/pool/pallas_call | solution.py:342
  40.7 1.4 %collective-permute-done.22 = bf16[64,3456]{1,0:T(8,128)(2,1)S(1)} collective-permute-done((bf16[64,3456]{1,0:T(8,128)(2,1)S(1)}, bf16[64,3456]{1,0:T(8,128)(2,1)S(1)}, u32[]{:S(2)}, u32[]{:S(2)}) %collective-permute-start.22) | collective-permute-done | bytes 442400 | tf_op jit(solution)/shard_map/ppermute | solution.py:228
  42.2 2.1 %owner.1 = (bf16[512,128]{1,0:T(8,128)(2,1)S(1)}, bf16[256,512]{1,0:T(8,128)(2,1)S(1)}) custom-call(s32[16]{0:T(128)S(1)} %get-tuple-element.61.slot_ref, bf16[256,512]{1,0:T(8,128)(2,1)S(1)} %get-tuple-element.62.hidden_ref, bf16[256,3456]{1,0:T(8,128)(2,1)S(1)} %get-tuple-element.64.scaled_ref, ...), custom_call_target="tpu_custom_call" | custom-call | tf_op jit(solution)/shard_map/owner/pallas_call | solution.py:362
  44.3 3.6 %collective-permute-start.23 = (bf16[512,128]{1,0:T(8,128)(2,1)S(1)}, bf16[512,128]{1,0:T(8,128)(2,1)S(1)}, u32[]{:S(2)}, u32[]{:S(2)}) collective-permute-start(bf16[512,128]{1,0:T(8,128)(2,1)S(1)} %get-tuple-element.69), channel_id=1, source_target_pairs={{0,6},{1,7},{2,4},{3,5},{4,2},{5,3},{6,0},{7,1},{8,14},{9,15},{10,... | collective-permute-start | bytes 393224 | tf_op jit(solution)/shard_map/ppermute | solution.py:199
  47.9 1.6 %blocks.1 = (bf16[512,128]{1,0:T(8,128)(2,1)S(1)}, bf16[512,128]{1,0:T(8,128)(2,1)S(1)}, bf16[512,128]{1,0:T(8,128)(2,1)S(1)}) custom-call(s32[16]{0:T(128)S(1)} %get-tuple-element.61.slot_ref, bf16[256,512]{1,0:T(8,128)(2,1)S(1)} %get-tuple-element.62.hidden_ref, bf16[256,512]{1,0:T(8,128)(2,1)S(1)} %get-tuple-element.73.dhidden_ref, ...), custom_call_target="tpu_custom_call" | custom-call | tf_op jit(solution)/shard_map/blocks/pallas_call | solution.py:370
  49.4 1.1 %collective-permute-start.25 = (bf16[512,128]{1,0:T(8,128)(2,1)S(1)}, bf16[512,128]{1,0:T(8,128)(2,1)S(1)}, u32[]{:S(2)}, u32[]{:S(2)}) collective-permute-start(bf16[512,128]{1,0:T(8,128)(2,1)S(1)} %get-tuple-element.75), channel_id=1, source_target_pairs={{0,2},{1,3},{2,0},{3,1},{4,6},{5,7},{6,4},{7,5},{8,10},{9,11},{10,... | collective-permute-start | bytes 393224 | tf_op jit(solution)/shard_map/ppermute | solution.py:199
  50.5 2.4 %cross.1 = bf16[256,3456]{1,0:T(8,128)(2,1)} custom-call(bf16[256,3456]{1,0:T(8,128)(2,1)S(1)} %get-tuple-element.70.first_ref, bf16[256,512]{1,0:T(8,128)(2,1)S(1)} %get-tuple-element.62.hidden_ref, bf16[512,3456]{1,0:T(8,128)(2,1)S(1)} %constant_dynamic-update-slice_fusion.u_ref, f32[1,3456]{1,0:T(1,128)S(1)} %reshape.7.bias_ref), custom_call_target="tpu_custom_call" | custom-call | flops 905969664 | bytes 7077888 | tf_op jit(solution)/shard_map/cross/pallas_call | solution.py:380
  52.9 2.1 %collective-permute-done.25.refs_2_ = bf16[512,128]{1,0:T(8,128)(2,1)S(1)} collective-permute-done((bf16[512,128]{1,0:T(8,128)(2,1)S(1)}, bf16[512,128]{1,0:T(8,128)(2,1)S(1)}, u32[]{:S(2)}, u32[]{:S(2)}) %collective-permute-start.25) | collective-permute-done | bytes 131104 | tf_op jit(solution)/shard_map/ppermute | solution.py:199
  55.0 5.3 %collective-permute-done.27.refs_4_ = bf16[512,128]{1,0:T(8,128)(2,1)S(1)} collective-permute-done((bf16[512,128]{1,0:T(8,128)(2,1)S(1)}, bf16[512,128]{1,0:T(8,128)(2,1)S(1)}, u32[]{:S(2)}, u32[]{:S(2)}) %collective-permute-start.27) | collective-permute-done | bytes 131104 | tf_op jit(solution)/shard_map/ppermute | solution.py:199
  60.8 0.8 %collective-permute-done.28.refs_5_ = bf16[512,128]{1,0:T(8,128)(2,1)S(1)} collective-permute-done((bf16[512,128]{1,0:T(8,128)(2,1)S(1)}, bf16[512,128]{1,0:T(8,128)(2,1)S(1)}, u32[]{:S(2)}, u32[]{:S(2)}) %collective-permute-start.28) | collective-permute-done | bytes 131104 | tf_op jit(solution)/shard_map/ppermute | solution.py:228
  62.4 1.0 %collective-permute-start.30 = (bf16[256,128]{1,0:T(8,128)(2,1)S(1)}, bf16[256,128]{1,0:T(8,128)(2,1)S(1)}, u32[]{:S(2)}, u32[]{:S(2)}) collective-permute-start(bf16[256,128]{1,0:T(8,128)(2,1)S(1)} %get-tuple-element.79), channel_id=1, source_target_pairs={{0,8},{8,0},{16,24},{24,16},{1,9},{9,1},{17,25},{25,17},{2,10},{10... | collective-permute-start | bytes 196616 | tf_op jit(solution)/shard_map/ppermute | solution.py:199
  63.4 1.3 %collective-permute-start.31 = (bf16[256,128]{1,0:T(8,128)(2,1)S(1)}, bf16[256,128]{1,0:T(8,128)(2,1)S(1)}, u32[]{:S(2)}, u32[]{:S(2)}) collective-permute-start(bf16[256,128]{1,0:T(8,128)(2,1)S(1)} %get-tuple-element.80), channel_id=1, source_target_pairs={{0,16},{8,24},{16,0},{24,8},{1,17},{9,25},{17,1},{25,9},{2,18},{10... | collective-permute-start | bytes 196616 | tf_op jit(solution)/shard_map/ppermute | solution.py:199
  64.6 1.3 %collective-permute-start.32 = (bf16[256,128]{1,0:T(8,128)(2,1)S(1)}, bf16[256,128]{1,0:T(8,128)(2,1)S(1)}, u32[]{:S(2)}, u32[]{:S(2)}) collective-permute-start(bf16[256,128]{1,0:T(8,128)(2,1)S(1)} %get-tuple-element.81), channel_id=1, source_target_pairs={{0,24},{8,16},{16,8},{24,0},{1,25},{9,17},{17,9},{25,1},{2,26},{10... | collective-permute-start | bytes 196616 | tf_op jit(solution)/shard_map/ppermute | solution.py:199
  66.0 0.8 %collective-permute-done.30.refs_1_ = bf16[256,128]{1,0:T(8,128)(2,1)S(1)} collective-permute-done((bf16[256,128]{1,0:T(8,128)(2,1)S(1)}, bf16[256,128]{1,0:T(8,128)(2,1)S(1)}, u32[]{:S(2)}, u32[]{:S(2)}) %collective-permute-start.30) | collective-permute-done | bytes 65568 | tf_op jit(solution)/shard_map/ppermute | solution.py:199
  66.8 0.9 %collective-permute-done.31.refs_2_ = bf16[256,128]{1,0:T(8,128)(2,1)S(1)} collective-permute-done((bf16[256,128]{1,0:T(8,128)(2,1)S(1)}, bf16[256,128]{1,0:T(8,128)(2,1)S(1)}, u32[]{:S(2)}, u32[]{:S(2)}) %collective-permute-start.31) | collective-permute-done | bytes 65568 | tf_op jit(solution)/shard_map/ppermute | solution.py:199
  67.7 2.1 %collective-permute-done.32.refs_3_ = bf16[256,128]{1,0:T(8,128)(2,1)S(1)} collective-permute-done((bf16[256,128]{1,0:T(8,128)(2,1)S(1)}, bf16[256,128]{1,0:T(8,128)(2,1)S(1)}, u32[]{:S(2)}, u32[]{:S(2)}) %collective-permute-start.32) | collective-permute-done | bytes 65568 | tf_op jit(solution)/shard_map/ppermute | solution.py:199
  69.8 1.5 %rows.1 = f32[512,128]{1,0:T(8,128)} custom-call(s32[8]{0:T(128)S(1)} %copy-done.4, s32[8,128,128]{2,1,0:T(8,128)S(1)} %copy-done.1, bf16[256,128]{1,0:T(8,128)(2,1)S(1)} %get-tuple-element.78.refs_0_, bf16[256,128]{1,0:T(8,128)(2,1)S(1)} %collective-permute-done.30.refs_1_, bf16[256,128]{1,0:T(8,128)(2,1)S(1)} %collective-permute-done.31.refs_2_, ...), custom_call_target="tpu_custom_call" | custom-call | tf_op jit(solution)/shard_map/rows/pallas_call | solution.py:413
  (73 shorter events, 10.0 us)
Async XLA Ops:
  0.6 21.8 %collective-permute-start = (bf16[864,512]{1,0:T(8,128)(2,1)}, bf16[864,512]{1,0:T(8,128)(2,1)S(1)}, u32[]{:S(2)}, u32[]{:S(2)}) collective-permute-start(bf16[864,512]{1,0:T(8,128)(2,1)} %param.16), channel_id=1, source_target_pairs={{0,8},{1,17},{2,10},{3,19},{4,12},{5,21},{6,14},{7,23},{8,0},{9,25... | collective-permute-start | bytes 2654216 | tf_op jit(solution)/shard_map/ppermute | solution.py:228
  3.6 23.9 %collective-permute-start.10 = (bf16[128,3456]{1,0:T(8,128)(2,1)}, bf16[128,3456]{1,0:T(8,128)(2,1)S(1)}, u32[]{:S(2)}, u32[]{:S(2)}) collective-permute-start(bf16[128,3456]{1,0:T(8,128)(2,1)} %param.17), channel_id=1, source_target_pairs={{0,8},{1,17},{2,10},{3,19},{4,12},{5,21},{6,14},{7,23},{8,0},{9,25... | collective-permute-start | bytes 2654216 | tf_op jit(solution)/shard_map/ppermute | solution.py:228
  5.8 2.6 %collective-permute-start.2 = (bf16[272,128]{1,0:T(8,128)(2,1)}, bf16[272,128]{1,0:T(8,128)(2,1)S(1)}, u32[]{:S(2)}, u32[]{:S(2)}) collective-permute-start(bf16[272,128]{1,0:T(8,128)(2,1)} %get-tuple-element.44), channel_id=1, source_target_pairs={{0,1},{1,0},{2,3},{3,2},{4,5},{5,4},{6,7},{7,6},{8,9},{9,8},{10,11... | collective-permute-start | bytes 208904 | tf_op jit(solution)/shard_map/ppermute | solution.py:228
  5.8 3.4 %collective-permute-start.6 = (bf16[272,128]{1,0:T(8,128)(2,1)}, bf16[272,128]{1,0:T(8,128)(2,1)S(1)}, u32[]{:S(2)}, u32[]{:S(2)}) collective-permute-start(bf16[272,128]{1,0:T(8,128)(2,1)} %get-tuple-element.46), channel_id=1, source_target_pairs={{0,1},{1,0},{2,3},{3,2},{4,5},{5,4},{6,7},{7,6},{8,9},{9,8},{10,11... | collective-permute-start | bytes 208904 | tf_op jit(solution)/shard_map/ppermute | solution.py:228
  6.3 5.3 %collective-permute-start.1 = (bf16[272,128]{1,0:T(8,128)(2,1)}, bf16[272,128]{1,0:T(8,128)(2,1)S(1)}, u32[]{:S(2)}, u32[]{:S(2)}) collective-permute-start(bf16[272,128]{1,0:T(8,128)(2,1)} %get-tuple-element.43), channel_id=1, source_target_pairs={{0,16},{1,9},{2,18},{3,11},{4,20},{5,13},{6,22},{7,15},{8,24},{9,1... | collective-permute-start | bytes 208904 | tf_op jit(solution)/shard_map/ppermute | solution.py:228
  8.3 5.1 %collective-permute-start.3 = (bf16[272,128]{1,0:T(8,128)(2,1)S(1)}, bf16[272,128]{1,0:T(8,128)(2,1)S(1)}, u32[]{:S(2)}, u32[]{:S(2)}) collective-permute-start(bf16[272,128]{1,0:T(8,128)(2,1)S(1)} %collective-permute-done.2), channel_id=1, source_target_pairs={{0,16},{1,9},{2,18},{3,11},{4,20},{5,13},{6,22},{7,15},{8,24},{9,1... | collective-permute-start | bytes 208904 | tf_op jit(solution)/shard_map/ppermute | solution.py:228
  9.3 6.2 %collective-permute-start.7 = (bf16[272,128]{1,0:T(8,128)(2,1)S(1)}, bf16[272,128]{1,0:T(8,128)(2,1)S(1)}, u32[]{:S(2)}, u32[]{:S(2)}) collective-permute-start(bf16[272,128]{1,0:T(8,128)(2,1)S(1)} %collective-permute-done.6), channel_id=1, source_target_pairs={{0,0},{1,25},{2,2},{3,27},{4,4},{5,29},{6,6},{7,31},{8,8},{9,17},{... | collective-permute-start | bytes 208904 | tf_op jit(solution)/shard_map/ppermute | solution.py:228
  11.7 4.2 %collective-permute-start.5 = (bf16[272,128]{1,0:T(8,128)(2,1)}, bf16[272,128]{1,0:T(8,128)(2,1)S(1)}, u32[]{:S(2)}, u32[]{:S(2)}) collective-permute-start(bf16[272,128]{1,0:T(8,128)(2,1)} %get-tuple-element.45), channel_id=1, source_target_pairs={{0,0},{1,25},{2,2},{3,27},{4,4},{5,29},{6,6},{7,31},{8,8},{9,17},{... | collective-permute-start | bytes 208904 | tf_op jit(solution)/shard_map/ppermute | solution.py:228
  13.4 3.0 %collective-permute-start.4 = (bf16[272,128]{1,0:T(8,128)(2,1)S(1)}, bf16[272,128]{1,0:T(8,128)(2,1)S(1)}, u32[]{:S(2)}, u32[]{:S(2)}) collective-permute-start(bf16[272,128]{1,0:T(8,128)(2,1)S(1)} %collective-permute-done.3), channel_id=1, source_target_pairs={{0,1},{1,0},{2,3},{3,2},{4,5},{5,4},{6,7},{7,6},{8,9},{9,8},{10,11... | collective-permute-start | bytes 208904 | tf_op jit(solution)/shard_map/ppermute | solution.py:228
  18.4 12.2 %collective-permute-start.12 = (bf16[544,128]{1,0:T(8,128)(2,1)S(1)}, bf16[544,128]{1,0:T(8,128)(2,1)S(1)}, u32[]{:S(2)}, u32[]{:S(2)}) collective-permute-start(bf16[544,128]{1,0:T(8,128)(2,1)S(1)} %get-tuple-element.52), channel_id=1, source_target_pairs={{0,4},{1,5},{2,6},{3,7},{4,0},{5,1},{6,2},{7,3},{8,12},{9,13},{10,... | collective-permute-start | bytes 417800 | tf_op jit(solution)/shard_map/ppermute | solution.py:199
  21.1 11.9 %collective-permute-start.13 = (bf16[544,128]{1,0:T(8,128)(2,1)S(1)}, bf16[544,128]{1,0:T(8,128)(2,1)S(1)}, u32[]{:S(2)}, u32[]{:S(2)}) collective-permute-start(bf16[544,128]{1,0:T(8,128)(2,1)S(1)} %get-tuple-element.53), channel_id=1, source_target_pairs={{0,6},{1,7},{2,4},{3,5},{4,2},{5,3},{6,0},{7,1},{8,14},{9,15},{10,... | collective-permute-start | bytes 417800 | tf_op jit(solution)/shard_map/ppermute | solution.py:199
  22.4 10.7 %collective-permute-start.11 = (bf16[544,128]{1,0:T(8,128)(2,1)S(1)}, bf16[544,128]{1,0:T(8,128)(2,1)S(1)}, u32[]{:S(2)}, u32[]{:S(2)}) collective-permute-start(bf16[544,128]{1,0:T(8,128)(2,1)S(1)} %get-tuple-element.51), channel_id=1, source_target_pairs={{0,2},{1,3},{2,0},{3,1},{4,6},{5,7},{6,4},{7,5},{8,10},{9,11},{10,... | collective-permute-start | bytes 417800 | tf_op jit(solution)/shard_map/ppermute | solution.py:199
  22.7 10.4 %collective-permute-start.9 = (bf16[432,512]{1,0:T(8,128)(2,1)S(1)}, bf16[432,512]{1,0:T(8,128)(2,1)S(1)}, u32[]{:S(2)}, u32[]{:S(2)}) collective-permute-start(bf16[432,512]{1,0:T(8,128)(2,1)S(1)} %constant_dynamic-slice_fusion.1), channel_id=1, source_target_pairs={{0,16},{1,9},{2,18},{3,11},{4,20},{5,13},{6,22},{7,15},{8,24},{9,1... | collective-permute-start | bytes 1327112 | tf_op jit(solution)/shard_map/ppermute | solution.py:228
  27.5 7.3 %collective-permute-start.18 = (bf16[864,512]{1,0:T(8,128)(2,1)S(1)}, bf16[864,512]{1,0:T(8,128)(2,1)S(1)}, u32[]{:S(2)}, u32[]{:S(2)}) collective-permute-start(bf16[864,512]{1,0:T(8,128)(2,1)S(1)} %collective-permute-done), channel_id=1, source_target_pairs={{0,1},{1,0},{2,3},{3,2},{4,5},{5,4},{6,7},{7,6},{8,9},{9,8},{10,11... | collective-permute-start | bytes 2654216 | tf_op jit(solution)/shard_map/ppermute | solution.py:228
  30.6 9.7 %collective-permute-start.20 = (bf16[64,3456]{1,0:T(8,128)(2,1)S(1)}, bf16[64,3456]{1,0:T(8,128)(2,1)S(1)}, u32[]{:S(2)}, u32[]{:S(2)}) collective-permute-start(bf16[64,3456]{1,0:T(8,128)(2,1)S(1)} %constant_dynamic-slice_fusion), channel_id=1, source_target_pairs={{0,16},{1,9},{2,18},{3,11},{4,20},{5,13},{6,22},{7,15},{8,24},{9,1... | collective-permute-start | bytes 1327112 | tf_op jit(solution)/shard_map/ppermute | solution.py:228
  33.1 3.8 %collective-permute-start.19 = (bf16[432,512]{1,0:T(8,128)(2,1)S(1)}, bf16[432,512]{1,0:T(8,128)(2,1)S(1)}, u32[]{:S(2)}, u32[]{:S(2)}) collective-permute-start(bf16[432,512]{1,0:T(8,128)(2,1)S(1)} %collective-permute-done.9), channel_id=1, source_target_pairs={{0,1},{1,0},{2,3},{3,2},{4,5},{5,4},{6,7},{7,6},{8,9},{9,8},{10,11... | collective-permute-start | bytes 1327112 | tf_op jit(solution)/shard_map/ppermute | solution.py:228
  33.7 6.9 %collective-permute-start.21 = (bf16[128,3456]{1,0:T(8,128)(2,1)S(1)}, bf16[128,3456]{1,0:T(8,128)(2,1)S(1)}, u32[]{:S(2)}, u32[]{:S(2)}) collective-permute-start(bf16[128,3456]{1,0:T(8,128)(2,1)S(1)} %collective-permute-done.10), channel_id=1, source_target_pairs={{0,1},{1,0},{2,3},{3,2},{4,5},{5,4},{6,7},{7,6},{8,9},{9,8},{10,11... | collective-permute-start | bytes 2654216 | tf_op jit(solution)/shard_map/ppermute | solution.py:228
  34.2 2.4 %collective-permute-start.14 = (bf16[544,128]{1,0:T(8,128)(2,1)S(1)}, bf16[544,128]{1,0:T(8,128)(2,1)S(1)}, u32[]{:S(2)}, u32[]{:S(2)}) collective-permute-start(bf16[544,128]{1,0:T(8,128)(2,1)S(1)} %get-tuple-element.54.refs_0_), channel_id=1, source_target_pairs={{0,1},{1,0},{2,3},{3,2},{4,5},{5,4},{6,7},{7,6},{8,9},{9,8},{10,11... | collective-permute-start | bytes 417800 | tf_op jit(solution)/shard_map/ppermute | solution.py:228
  34.8 2.3 %collective-permute-start.15 = (bf16[544,128]{1,0:T(8,128)(2,1)S(1)}, bf16[544,128]{1,0:T(8,128)(2,1)S(1)}, u32[]{:S(2)}, u32[]{:S(2)}) collective-permute-start(bf16[544,128]{1,0:T(8,128)(2,1)S(1)} %collective-permute-done.11.refs_2_), channel_id=1, source_target_pairs={{0,1},{1,0},{2,3},{3,2},{4,5},{5,4},{6,7},{7,6},{8,9},{9,8},{10,11... | collective-permute-start | bytes 417800 | tf_op jit(solution)/shard_map/ppermute | solution.py:228
  36.6 1.4 %collective-permute-start.16 = (bf16[544,128]{1,0:T(8,128)(2,1)S(1)}, bf16[544,128]{1,0:T(8,128)(2,1)S(1)}, u32[]{:S(2)}, u32[]{:S(2)}) collective-permute-start(bf16[544,128]{1,0:T(8,128)(2,1)S(1)} %collective-permute-done.12.refs_4_), channel_id=1, source_target_pairs={{0,1},{1,0},{2,3},{3,2},{4,5},{5,4},{6,7},{7,6},{8,9},{9,8},{10,11... | collective-permute-start | bytes 417800 | tf_op jit(solution)/shard_map/ppermute | solution.py:228
  36.9 1.4 %collective-permute-start.17 = (bf16[544,128]{1,0:T(8,128)(2,1)S(1)}, bf16[544,128]{1,0:T(8,128)(2,1)S(1)}, u32[]{:S(2)}, u32[]{:S(2)}) collective-permute-start(bf16[544,128]{1,0:T(8,128)(2,1)S(1)} %collective-permute-done.13.refs_6_), channel_id=1, source_target_pairs={{0,1},{1,0},{2,3},{3,2},{4,5},{5,4},{6,7},{7,6},{8,9},{9,8},{10,11... | collective-permute-start | bytes 417800 | tf_op jit(solution)/shard_map/ppermute | solution.py:228
  40.3 1.9 %collective-permute-start.22 = (bf16[64,3456]{1,0:T(8,128)(2,1)S(1)}, bf16[64,3456]{1,0:T(8,128)(2,1)S(1)}, u32[]{:S(2)}, u32[]{:S(2)}) collective-permute-start(bf16[64,3456]{1,0:T(8,128)(2,1)S(1)} %collective-permute-done.20), channel_id=1, source_target_pairs={{0,1},{1,0},{2,3},{3,2},{4,5},{5,4},{6,7},{7,6},{8,9},{9,8},{10,11... | collective-permute-start | bytes 1327112 | tf_op jit(solution)/shard_map/ppermute | solution.py:228
  44.3 8.7 %collective-permute-start.23 = (bf16[512,128]{1,0:T(8,128)(2,1)S(1)}, bf16[512,128]{1,0:T(8,128)(2,1)S(1)}, u32[]{:S(2)}, u32[]{:S(2)}) collective-permute-start(bf16[512,128]{1,0:T(8,128)(2,1)S(1)} %get-tuple-element.69), channel_id=1, source_target_pairs={{0,6},{1,7},{2,4},{3,5},{4,2},{5,3},{6,0},{7,1},{8,14},{9,15},{10,... | collective-permute-start | bytes 393224 | tf_op jit(solution)/shard_map/ppermute | solution.py:199
  49.4 5.5 %collective-permute-start.25 = (bf16[512,128]{1,0:T(8,128)(2,1)S(1)}, bf16[512,128]{1,0:T(8,128)(2,1)S(1)}, u32[]{:S(2)}, u32[]{:S(2)}) collective-permute-start(bf16[512,128]{1,0:T(8,128)(2,1)S(1)} %get-tuple-element.75), channel_id=1, source_target_pairs={{0,2},{1,3},{2,0},{3,1},{4,6},{5,7},{6,4},{7,5},{8,10},{9,11},{10,... | collective-permute-start | bytes 393224 | tf_op jit(solution)/shard_map/ppermute | solution.py:199
  50.5 9.8 %collective-permute-start.27 = (bf16[512,128]{1,0:T(8,128)(2,1)S(1)}, bf16[512,128]{1,0:T(8,128)(2,1)S(1)}, u32[]{:S(2)}, u32[]{:S(2)}) collective-permute-start(bf16[512,128]{1,0:T(8,128)(2,1)S(1)} %get-tuple-element.76), channel_id=1, source_target_pairs={{0,4},{1,5},{2,6},{3,7},{4,0},{5,1},{6,2},{7,3},{8,12},{9,13},{10,... | collective-permute-start | bytes 393224 | tf_op jit(solution)/shard_map/ppermute | solution.py:199
  50.5 10.3 %collective-permute-start.24 = (bf16[512,128]{1,0:T(8,128)(2,1)S(1)}, bf16[512,128]{1,0:T(8,128)(2,1)S(1)}, u32[]{:S(2)}, u32[]{:S(2)}) collective-permute-start(bf16[512,128]{1,0:T(8,128)(2,1)S(1)} %get-tuple-element.74.refs_0_), channel_id=1, source_target_pairs={{0,1},{1,0},{2,3},{3,2},{4,5},{5,4},{6,7},{7,6},{8,9},{9,8},{10,11... | collective-permute-start | bytes 393224 | tf_op jit(solution)/shard_map/ppermute | solution.py:228
  55.0 5.8 %collective-permute-start.26 = (bf16[512,128]{1,0:T(8,128)(2,1)S(1)}, bf16[512,128]{1,0:T(8,128)(2,1)S(1)}, u32[]{:S(2)}, u32[]{:S(2)}) collective-permute-start(bf16[512,128]{1,0:T(8,128)(2,1)S(1)} %collective-permute-done.25.refs_2_), channel_id=1, source_target_pairs={{0,1},{1,0},{2,3},{3,2},{4,5},{5,4},{6,7},{7,6},{8,9},{9,8},{10,11... | collective-permute-start | bytes 393224 | tf_op jit(solution)/shard_map/ppermute | solution.py:228
  60.3 1.3 %collective-permute-start.28 = (bf16[512,128]{1,0:T(8,128)(2,1)S(1)}, bf16[512,128]{1,0:T(8,128)(2,1)S(1)}, u32[]{:S(2)}, u32[]{:S(2)}) collective-permute-start(bf16[512,128]{1,0:T(8,128)(2,1)S(1)} %collective-permute-done.27.refs_4_), channel_id=1, source_target_pairs={{0,1},{1,0},{2,3},{3,2},{4,5},{5,4},{6,7},{7,6},{8,9},{9,8},{10,11... | collective-permute-start | bytes 393224 | tf_op jit(solution)/shard_map/ppermute | solution.py:228
  60.3 1.5 %collective-permute-start.29 = (bf16[512,128]{1,0:T(8,128)(2,1)S(1)}, bf16[512,128]{1,0:T(8,128)(2,1)S(1)}, u32[]{:S(2)}, u32[]{:S(2)}) collective-permute-start(bf16[512,128]{1,0:T(8,128)(2,1)S(1)} %collective-permute-done.23.refs_6_), channel_id=1, source_target_pairs={{0,1},{1,0},{2,3},{3,2},{4,5},{5,4},{6,7},{7,6},{8,9},{9,8},{10,11... | collective-permute-start | bytes 393224 | tf_op jit(solution)/shard_map/ppermute | solution.py:228
  62.4 4.4 %collective-permute-start.30 = (bf16[256,128]{1,0:T(8,128)(2,1)S(1)}, bf16[256,128]{1,0:T(8,128)(2,1)S(1)}, u32[]{:S(2)}, u32[]{:S(2)}) collective-permute-start(bf16[256,128]{1,0:T(8,128)(2,1)S(1)} %get-tuple-element.79), channel_id=1, source_target_pairs={{0,8},{8,0},{16,24},{24,16},{1,9},{9,1},{17,25},{25,17},{2,10},{10... | collective-permute-start | bytes 196616 | tf_op jit(solution)/shard_map/ppermute | solution.py:199
  63.4 4.3 %collective-permute-start.31 = (bf16[256,128]{1,0:T(8,128)(2,1)S(1)}, bf16[256,128]{1,0:T(8,128)(2,1)S(1)}, u32[]{:S(2)}, u32[]{:S(2)}) collective-permute-start(bf16[256,128]{1,0:T(8,128)(2,1)S(1)} %get-tuple-element.80), channel_id=1, source_target_pairs={{0,16},{8,24},{16,0},{24,8},{1,17},{9,25},{17,1},{25,9},{2,18},{10... | collective-permute-start | bytes 196616 | tf_op jit(solution)/shard_map/ppermute | solution.py:199
  64.6 5.2 %collective-permute-start.32 = (bf16[256,128]{1,0:T(8,128)(2,1)S(1)}, bf16[256,128]{1,0:T(8,128)(2,1)S(1)}, u32[]{:S(2)}, u32[]{:S(2)}) collective-permute-start(bf16[256,128]{1,0:T(8,128)(2,1)S(1)} %get-tuple-element.81), channel_id=1, source_target_pairs={{0,24},{8,16},{16,8},{24,0},{1,25},{9,17},{17,9},{25,1},{2,26},{10... | collective-permute-start | bytes 196616 | tf_op jit(solution)/shard_map/ppermute | solution.py:199
  (9 other events, 66.6 us)
